TPU v7x, 32 devices: a whole 2x2x4 slice. The times are simulated.
32 devices in a mesh: ctx: 16 (over z, y, core), ch: 2 (over x).
Axes of the slice: x: 2, y: 2, z: 4, core: 2. Of those that a mesh axis runs over, the one named last changes fastest.
Arguments:
- x_one: bfloat16 [2048, 4096], P('ctx', 'ch'), may hold values from -6 to 6
- x_two: bfloat16 [2048, 4096], P('ctx', 'ch'), may hold values from -6 to 6
- values: bfloat16 [2048, 4096], P('ctx', 'ch'), may hold values from -6 to 6
- grad_out: bfloat16 [2048, 4096], P('ctx', 'ch'), may hold values from -3 to 3
- filter_raw: bfloat16 [1024, 512], P('ctx', 'ch'), may hold values from -4 to 4
Outputs:
- grad_x_one: bfloat16 [2048, 4096], P('ctx', 'ch')
- grad_x_two: bfloat16 [2048, 4096], P('ctx', 'ch')
- grad_values: bfloat16 [2048, 4096], P('ctx', 'ch')
- grad_filter: float32 [1024, 512], P('ctx', 'ch')
All inputs are finite; a program needn't handle non-finite values.
Results may differ from a plain program's by a relative error of at most 0.0049.
Values may be sent and summed in bfloat16 or wider, within the bound.
No kernel may reach another device: no remote copies, remote signals or barrier semaphores. Data moves between devices by JAX's collectives and lax.ppermute only.
A program may use at most 192 MiB of HBM per device.

v0:
```python
import functools
import math

import jax
import jax.numpy as jnp
import ml_dtypes
import numpy as np
from jax import lax
from jax.experimental import pallas as pl
from jax.experimental.pallas import tpu as pltpu
from jax.sharding import PartitionSpec as P

GROUP = 4
f32 = jnp.float32
bf16 = jnp.bfloat16
VMEM_LIMIT = 24 * 1024 * 1024
BINS = 16


def dft_tables(block):
    size = 2 * block
    place = np.arange(block)
    rows = []
    for parity in (0, 1):
        freq = np.arange(parity, block, 2)
        angle = 2.0 * math.pi / (2 * size) * ((2 * freq[:, None] + 1) * place[None, :] % (2 * size))
        rows += [np.cos(angle), -np.sin(angle)]
    table = np.concatenate(rows, axis=0)
    high = table.astype(ml_dtypes.bfloat16)
    rest = (table - high.astype(np.float64)).astype(ml_dtypes.bfloat16)
    return high, rest, np.ascontiguousarray(high.T), np.ascontiguousarray(rest.T)


def call(kernel, outs, *args, scratch=(), flops=0, specs=None, out_specs=None, after=()):
    bytes_accessed = sum(a.size * a.dtype.itemsize for a in args)
    bytes_accessed += sum(math.prod(s) * jnp.dtype(t).itemsize for s, t in outs)
    whole = pl.BlockSpec(memory_space=pltpu.VMEM)
    n_args, n_after = len(args), len(after)

    def run(*refs):
        kernel(*refs[:n_args], *refs[n_args + n_after :])

    return pl.pallas_call(
        run,
        out_shape=[jax.ShapeDtypeStruct(s, t) for s, t in outs],
        in_specs=(specs or [whole] * n_args) + [pl.BlockSpec(memory_space=pl.ANY)] * n_after,
        out_specs=out_specs or [whole] * len(outs),
        scratch_shapes=list(scratch),
        compiler_params=pltpu.CompilerParams(vmem_limit_bytes=VMEM_LIMIT),
        cost_estimate=pl.CostEstimate(flops=0, bytes_accessed=0, transcendentals=0),
    )(*args, *after)


def gate_kernel(groups, chunks, *refs):
    hbm, outs, bufs, sems = refs[:4], refs[4 : 4 + GROUP], refs[4 + GROUP : 8 + GROUP], refs[8 + GROUP]
    tok, chans = bufs[0].shape
    part = groups // GROUP
    mine = lax.rem(lax.axis_index("ctx"), GROUP)
    step = tok // chunks
    copies = []
    for s in (0, 2):
        for i in range(chunks):
            rows = pl.ds(i * step, step)
            copies.append(
                [pltpu.make_async_copy(hbm[a].at[rows], bufs[a].at[rows], sems.at[a, i]) for a in (s, s + 1)]
            )
            for copy in copies[-1]:
                copy.start()
    for s in range(2):
        for i in range(chunks):
            for copy in copies[s * chunks + i]:
                copy.wait()
            rows, to = slice(i * step, (i + 1) * step), slice(s * tok + i * step, s * tok + (i + 1) * step)
            for d in range(GROUP):
                for r in range(chans // groups):
                    at = pl.ds(pl.multiple_of(r * groups + (mine ^ d) * part, part), part)
                    prod = bufs[2 * s][rows, at].astype(f32) * bufs[2 * s + 1][rows, at].astype(f32)
                    outs[d][to, r * part : (r + 1) * part] = prod.astype(bf16)


def assemble(pieces, p_out, g_out):
    rows = p_out.shape[0] // GROUP
    mine = lax.rem(lax.axis_index("ctx"), GROUP)
    for d in range(GROUP):
        at = pl.ds(pl.multiple_of((mine ^ d) * rows, rows), rows)
        p_out[at, :] = pieces[d][:rows, :]
        g_out[at, :] = pieces[d][rows:, :]


def assemble_kernel(*refs):
    assemble(refs[:GROUP], *refs[GROUP:])


def join_kernel(own, peer, out):
    part = own.shape[1]
    x = lax.axis_index("ch")
    for at, ref in ((x, own), (1 - x, peer)):
        out[:, pl.ds(pl.multiple_of(at * part, part), part)] = ref[...]


def assemble_split_kernel(*refs):
    pieces, raw, outs = refs[:GROUP], refs[GROUP : -GROUP - 2], refs[-GROUP:]
    assemble(pieces, *refs[-GROUP - 2 : -GROUP])
    part = outs[0].shape[1]
    sup, mine = lax.axis_index("ctx") // GROUP, lax.rem(lax.axis_index("ctx"), GROUP)
    for i, ref in enumerate(raw):
        rows = ref.shape[0]
        at = pl.ds(pl.multiple_of((sup ^ i) * rows, rows), rows)
        for d in range(GROUP):
            outs[d][at, :] = ref[:, pl.ds(pl.multiple_of((mine ^ d) * part, part), part)]


def pass_kernel(value, out):
    out[...] = value[...]


def filter_spectra_kernel(scale, fast, *refs):
    table_ref, rest_ref, out, taps_ref = refs[-4:]
    pieces = refs[:-4]
    n_slabs, slab, part = taps_ref.shape
    block = table_ref.shape[1]
    mine = lax.rem(lax.axis_index("ctx"), GROUP)
    for s in range(n_slabs):
        if fast:
            rows = slab // GROUP
            for d in range(GROUP):
                at = pl.ds(pl.multiple_of((mine ^ d) * rows, rows), rows)
                taps_ref[s, at, :] = pieces[d][s * rows : (s + 1) * rows, :]
        else:
            taps_ref[s] = pieces[0][s * slab : (s + 1) * slab, :]
    quarter = block // 2
    each = block // slab
    for k in range(n_slabs // each):
        spec = None
        for i in range(each):
            cols = slice(i * slab, (i + 1) * slab)
            for t in (table_ref, rest_ref):
                term = jnp.dot(t[:, cols], taps_ref[k * each + i], preferred_element_type=f32)
                spec = term if spec is None else spec + term
        spec = spec * scale
        for parity, sign in ((0, 1.0), (1, -1.0)):
            re = slice(parity * block, parity * block + quarter)
            im = slice(parity * block + quarter, (parity + 1) * block)
            if k == 0:
                out[0, re, :] = spec[re]
                out[0, im, :] = spec[im]
            else:
                out[k, re, :] += spec[re]
                out[k, im, :] += spec[im]
            out[k + 1, re, :] = -sign * spec[im]
            out[k + 1, im, :] = sign * spec[re]


def times(e_re, e_im, a_re, a_im, conj):
    if conj:
        return e_re * a_re + e_im * a_im, e_re * a_im - e_im * a_re
    return e_re * a_re - e_im * a_im, e_re * a_im + e_im * a_re


def bin_rows(block, visit):
    @pl.loop(0, 2)
    def _(parity):
        sign = 1.0 - 2.0 * parity.astype(f32)

        @pl.loop(0, block // 2 // BINS)
        def _(step):
            re = pl.multiple_of(parity * block + step * BINS, BINS)
            im = pl.multiple_of(parity * block + block // 2 + step * BINS, BINS)
            visit(sign, pl.ds(re, BINS), pl.ds(im, BINS))


def lag_kernel(fast, scale, *refs):
    blocks, (table, inverse, inverse_rest), refs = refs[:4], refs[4:7], refs[7:]
    spec, refs = refs[0], refs[1:]
    n_out = 2 if fast else 1
    lag_outs, (lag_prod, lag_low, lag_result) = refs[:n_out], refs[n_out:]
    block, wide = blocks[0].shape
    part = lag_result.shape[1] // 2
    for i, ref in enumerate(blocks):
        spec[i] = jnp.dot(table[...], ref[...], preferred_element_type=f32)

    def visit(sign, re, im):
        lags = [None] * 3
        for r in range(wide // part):
            cols = slice(r * part, (r + 1) * part)
            p0, p1, g0, g1 = ((spec[i, re, cols], spec[i, im, cols]) for i in range(4))
            for k, (p, g) in enumerate(((p0, g0), (p1, g0), (p1, g1))):
                t = times(*p, *g, True)
                lags[k] = t if lags[k] is None else (lags[k][0] + t[0], lags[k][1] + t[1])
        for k in range(2):
            cols = slice(k * part, (k + 1) * part)
            w_re = lags[k][0] + sign * lags[k + 1][1]
            w_im = lags[k][1] - sign * lags[k + 1][0]
            for rows, w in ((re, w_re), (im, w_im)):
                high = w.astype(bf16)
                lag_prod[rows, cols] = high
                lag_low[rows, cols] = (w - high.astype(f32)).astype(bf16)

    bin_rows(block, visit)
    total = jnp.dot(inverse[...], lag_prod[...], preferred_element_type=f32)
    total = total + jnp.dot(inverse[...], lag_low[...], preferred_element_type=f32)
    total = total + jnp.dot(inverse_rest[...], lag_prod[...], preferred_element_type=f32)
    lag_result[...] = total * (scale / block)
    if fast:
        x = lax.axis_index("ch")
        keep, send = lag_outs
        piece = keep.shape[0] // (lax.axis_size("ctx") // GROUP)
        for s in range(keep.shape[0] // piece):
            i, low = divmod(2 * piece * s, block)
            cols = slice(i * part, (i + 1) * part)
            to = slice(s * piece, (s + 1) * piece)
            keep[to, :] = lag_result[pl.ds(pl.multiple_of(low + x * piece, piece), piece), cols]
            send[to, :] = lag_result[pl.ds(pl.multiple_of(low + (1 - x) * piece, piece), piece), cols]
    else:
        for i in range(2):
            lag_outs[0][i * block : (i + 1) * block, :] = lag_result[:, i * part : (i + 1) * part]


def conv_kernel(conj, far, near, weights, table, inverse, *refs):
    outs, (spec, prod, result) = refs[:GROUP], refs[GROUP:]
    block, wide = far.shape
    part = weights.shape[2]
    first = 2 if conj else 0
    spec[...] = jnp.dot(table[...], far[...], preferred_element_type=f32)

    def visit(sign, re, im):
        e = [(weights[k, re, :], weights[k, im, :]) for k in range(3)]
        for r in range(wide // part):
            cols = slice(r * part, (r + 1) * part)
            total = times(*e[2], spec[re, cols], spec[im, cols], conj)
            for k in range(2):
                t = times(*e[k], near[first + k, re, cols], near[first + k, im, cols], conj)
                total = total[0] + t[0], total[1] + t[1]
            prod[re, cols] = total[0].astype(bf16)
            prod[im, cols] = total[1].astype(bf16)

    bin_rows(block, visit)
    result[...] = (jnp.dot(inverse[...], prod[...], preferred_element_type=f32) * (1.0 / block)).astype(bf16)
    rows = outs[0].shape[0]
    mine = lax.rem(lax.axis_index("ctx"), GROUP)
    for d in range(GROUP):
        outs[d][...] = result[pl.ds(pl.multiple_of((mine ^ d) * rows, rows), rows), :]


def lag_half_kernel(by, a, b, mine, theirs):
    rows = mine.shape[0]
    side = lax.rem(lax.axis_index("ctx") // (GROUP * by), 2)
    for out, at in ((mine, side), (theirs, 1 - side)):
        at = pl.ds(pl.multiple_of(at * rows, rows), rows)
        out[...] = a[at, :] + b[at, :]


def lag_sum_kernel(a, b, *outs):
    rows = outs[0].shape[0]
    low = lax.rem(lax.axis_index("ctx"), 2)
    for p in range(2):
        at = pl.ds(pl.multiple_of((low ^ p) * rows, rows), rows)
        outs[p][...] = a[at, :] + b[at, :]


def lag_place_kernel(a, b, out):
    part = a.shape[1]
    low = lax.rem(lax.axis_index("ctx"), 2)
    for p, ref in enumerate((a, b)):
        out[:, pl.ds(pl.multiple_of((low ^ p) * part, part), part)] = ref[...]


def finish_kernel(groups, chunks, n, *refs):
    pieces, gates, refs = refs[:GROUP], refs[GROUP : GROUP + n], refs[GROUP + n :]
    hbm, token, bufs, sems = refs[:n], refs[n], refs[n + 1 : 2 * n + 1], refs[2 * n + 1]
    tok, chans = gates[0].shape
    part = groups // GROUP
    mine = lax.rem(lax.axis_index("ctx"), GROUP)
    step = tok // chunks
    copies = []
    for i in range(chunks):
        rows = slice(i * step, (i + 1) * step)
        for d in range(GROUP):
            for r in range(chans // groups):
                cols = pl.ds(pl.multiple_of(r * groups + (mine ^ d) * part, part), part)
                piece = pieces[d][rows, r * part : (r + 1) * part].astype(f32)
                for a in range(n):
                    bufs[a][rows, cols] = (piece * gates[a][rows, cols].astype(f32)).astype(bf16)
        for a in range(n):
            at = pl.ds(i * step, step)
            copies.append(pltpu.make_async_copy(bufs[a].at[at], hbm[a].at[at], sems.at[a, i]))
            copies[-1].start()
    token[...] = jnp.zeros_like(token)
    for copy in copies:
        copy.wait()


def local(x_one, x_two, values, grad_out, filter_raw):
    tok, chans = x_one.shape
    tap_rows, own_filters = filter_raw.shape
    n, n_ch = lax.axis_size("ctx"), lax.axis_size("ch")
    taps, groups = tap_rows * n, own_filters * n_ch
    part = groups // GROUP
    repeat = chans // groups
    wide = repeat * part
    block = GROUP * tok
    span = taps // block
    assert span == 2 and taps % block == 0
    supers = n // GROUP
    scale = 1.0 / math.sqrt(taps)
    table, rest, inverse, inverse_rest = (jnp.asarray(t) for t in dft_tables(block))
    fast = n_ch == 2 and supers == 4 and taps // supers <= block

    def inside(value, d):
        return lax.ppermute(value, "ctx", [(i, i ^ d) for i in range(n)])

    def across(value, d):
        return lax.ppermute(value, "ctx", [(i, i ^ (d * GROUP)) for i in range(n)])

    def shift(value, by):
        by *= GROUP
        return lax.ppermute(value, "ctx", [(i, i + by) for i in range(n) if 0 <= i + by < n])

    def swap(value):
        return lax.ppermute(value, "ch", [(0, 1), (1, 0)])

    def trade(pieces):
        return [pieces[0]] + [inside(pieces[d], d) for d in range(1, GROUP)]

    chunks = 4
    in_hbm, in_vmem = pl.BlockSpec(memory_space=pltpu.HBM), pl.BlockSpec(memory_space=pltpu.VMEM)
    pieces_shape = [((tok, wide), bf16)] * GROUP
    block_shape = ((block, wide), bf16)

    gates = call(
        functools.partial(gate_kernel, groups, chunks),
        [((2 * tok, wide), bf16)] * GROUP,
        *(pltpu.with_memory_space_constraint(a, pltpu.HBM) for a in (x_one, values, grad_out, x_two)),
        scratch=[pltpu.VMEM((tok, chans), bf16)] * 4 + [pltpu.SemaphoreType.DMA((4, chunks))],
        specs=[in_hbm] * 4,
    )
    pieces = trade(gates)
    if fast:
        own_rows = call(join_kernel, [((tap_rows, groups), bf16)], filter_raw, swap(filter_raw), after=[pieces[1]])[0]
        raw = [own_rows] + [across(own_rows, d) for d in range(1, supers)]
        p_own, g_own, *filt = call(
            assemble_split_kernel,
            [block_shape, block_shape] + [((supers * tap_rows, part), bf16)] * GROUP,
            *pieces,
            *raw,
        )
        filt = trade(filt)
    else:
        p_own, g_own = call(assemble_kernel, [block_shape, block_shape], *pieces)
        whole = lax.all_gather(filter_raw, "ctx", axis=0, tiled=True)
        whole = lax.all_gather(whole, "ch", axis=1, tiled=True)
        start = lax.rem(lax.axis_index("ctx"), GROUP) * part
        filt = [lax.dynamic_slice(whole, (0, start), (taps, part))]
    slab = taps // supers if fast else block
    weights = call(
        functools.partial(filter_spectra_kernel, scale, fast),
        [((3, 2 * block, part), f32)],
        *filt,
        table,
        rest,
        scratch=[pltpu.VMEM((taps // slab, slab, part), bf16)],
    )[0]
    p_back, g_ahead = shift(p_own, 1), shift(g_own, -1)
    p_next = call(pass_kernel, [block_shape], p_back, after=[weights])[0]
    p_far, g_far = shift(p_next, 1), shift(g_ahead, -1)
    near, *lags = call(
        functools.partial(lag_kernel, fast, scale),
        [((4, 2 * block, wide), f32)] + ([((taps // 2, part), f32)] * 2 if fast else [((taps, part), f32)]),
        p_own,
        p_back,
        g_own,
        g_ahead,
        table,
        inverse,
        inverse_rest,
        scratch=[pltpu.VMEM((2 * block, 2 * part), bf16)] * 2
        + [pltpu.VMEM((block, 2 * part), f32)],
        after=[weights],
    )

    def convolve(conj, prior, far, *more):
        return call(
            functools.partial(conv_kernel, conj),
            pieces_shape,
            far,
            near,
            weights,
            table,
            inverse,
            scratch=[
                pltpu.VMEM((2 * block, wide), f32),
                pltpu.VMEM((2 * block, wide), bf16),
                pltpu.VMEM((block, wide), bf16),
            ],
            after=[prior, *more],
        )

    def finish(pieces, prior, *gates):
        n = len(gates)
        return call(
            functools.partial(finish_kernel, groups, chunks, n),
            [((tok, chans), bf16)] * n + [((8, 128), f32)],
            *pieces,
            *gates,
            scratch=[pltpu.VMEM((tok, chans), bf16)] * n + [pltpu.SemaphoreType.DMA((n, chunks))],
            out_specs=[in_hbm] * n + [in_vmem],
            after=[prior],
        )

    conv = convolve(False, lags[0], p_far)
    prior = conv[0]
    if fast:
        mine, theirs = lags
        mine, theirs = call(
            functools.partial(lag_half_kernel, 2),
            [((taps // 4, part), f32)] * 2,
            mine,
            swap(theirs),
            after=[prior],
        )
        prior = mine
    conv = trade(conv)
    back = convolve(True, prior, g_far, conv[1])
    prior = back[0]
    if fast:
        mine, theirs = call(
            functools.partial(lag_half_kernel, 1),
            [((taps // 8, part), f32)] * 2,
            mine,
            across(theirs, 2),
            after=[prior],
        )
        prior = mine
    grad_x_two, prior = finish(conv, prior, grad_out)
    if fast:
        sums = call(
            lag_sum_kernel, [((tap_rows, part), f32)] * 2, mine, across(theirs, 1), after=[prior]
        )
        prior = sums[0]
    grad_x_one, grad_values, prior = finish(trade(back), prior, values, x_one)
    if fast:

        def owner(value, p):
            pairs = []
            for i in range(n):
                j1, j0 = (i // 2) % 2, i % 2
                for x in range(2):
                    to = i // GROUP * GROUP + 2 * x + (p ^ j0)
                    pairs.append((i * 2 + x, to * 2 + j1))
            return lax.ppermute(value, ("ctx", "ch"), pairs)

        landed = [owner(s, p) for p, s in enumerate(sums)]
        grad_filter = call(lag_place_kernel, [((tap_rows, own_filters), f32)], *landed, after=[prior])[0]
    else:
        start = lax.rem(lax.axis_index("ctx"), GROUP) * part
        terms = lax.dynamic_update_slice(jnp.zeros((taps, groups), f32), lags[0], (0, start))
        by_taps = lax.psum_scatter(terms, "ctx", scatter_dimension=0, tiled=True)
        grad_filter = lax.psum_scatter(by_taps, "ch", scatter_dimension=1, tiled=True)
    return (grad_x_one, grad_x_two, grad_values, grad_filter)


def solution(mesh):
    placed = P("ctx", "ch")
    return jax.shard_map(
        local,
        mesh=mesh,
        in_specs=(placed,) * 5,
        out_specs=(placed,) * 4,
        check_vma=False,
    )
```

profile of v0, /device:TPU:3, one launch (start us, length us, event | category | flops | bytes accessed | tf_op | source)
XLA Modules:
  0.0 76.5 jit_solution(3436478896860728335)
XLA Ops:
  0.6 0.0 copy-start.1
  0.6 0.0 copy-start.2
  0.7 0.0 copy-start.6
  0.7 2.0 %shard_map.120 = (bf16[256,512]{1,0:T(8,128)(2,1)S(1)}, bf16[256,512]{1,0:T(8,128)(2,1)S(1)}, bf16[256,512]{1,0:T(8,128)(2,1)S(1)}, bf16[256,512]{1,0:T(8,128)(2,1)S(1)}) custom-call(bf16[128,2048]{1,0:T(8,128)(2,1)} %refs_5_.3, bf16[128,2048]{1,0:T(8,128)(2,1)} %refs_4_.7, bf16[128,2048]{1,0:T(8,128)(2,1)} %refs_4_.6, bf16[128,2048]{1,0:T(8,128)(2,1)} %refs_3_.3), custom_call_target="tpu_custom_call" | custom-call | tf_op jit(solution)/shard_map/pallas_call | solution.py:43
  2.6 0.7 collective-permute-start
  3.4 1.3 %collective-permute-start.1 = (bf16[256,512]{1,0:T(8,128)(2,1)S(1)}, bf16[256,512]{1,0:T(8,128)(2,1)S(1)}, u32[]{:S(2)}, u32[]{:S(2)}) collective-permute-start(bf16[256,512]{1,0:T(8,128)(2,1)S(1)} %get-tuple-element.38), channel_id=1, source_target_pairs={{0,4},{2,6},{4,0},{6,2},{8,12},{10,14},{12,8},{14,10},{16,20},{18,... | collective-permute-start | bytes 786440 | tf_op jit(solution)/shard_map/ppermute | solution.py:310
  4.6 0.5 collective-permute-start.2
  5.1 3.3 %collective-permute-done.3.refs_1_ = bf16[64,256]{1,0:T(8,128)(2,1)S(1)} collective-permute-done((bf16[64,256]{1,0:T(8,128)(2,1)}, bf16[64,256]{1,0:T(8,128)(2,1)S(1)}, u32[]{:S(2)}, u32[]{:S(2)}) %collective-permute-start.3) | collective-permute-done | bytes 32800 | tf_op jit(solution)/shard_map/ppermute | solution.py:320
  8.4 0.8 copy-done.8
  9.1 1.4 %collective-permute-start.4 = (bf16[64,512]{1,0:T(8,128)(2,1)S(1)}, bf16[64,512]{1,0:T(8,128)(2,1)S(1)}, u32[]{:S(2)}, u32[]{:S(2)}) collective-permute-start(bf16[64,512]{1,0:T(8,128)(2,1)S(1)} %shard_map.121.refs_4_), channel_id=1, source_target_pairs={{0,8},{2,10},{4,12},{6,14},{8,0},{10,2},{12,4},{14,6},{16,24},{18,... | collective-permute-start | bytes 196616 | tf_op jit(solution)/shard_map/ppermute | solution.py:313
  10.5 2.3 %collective-permute-start.5 = (bf16[64,512]{1,0:T(8,128)(2,1)S(1)}, bf16[64,512]{1,0:T(8,128)(2,1)S(1)}, u32[]{:S(2)}, u32[]{:S(2)}) collective-permute-start(bf16[64,512]{1,0:T(8,128)(2,1)S(1)} %shard_map.121.refs_4_), channel_id=1, source_target_pairs={{0,16},{2,18},{4,20},{6,22},{8,24},{10,26},{12,28},{14,30},{16,0},... | collective-permute-start | bytes 196616 | tf_op jit(solution)/shard_map/ppermute | solution.py:313
  12.8 4.5 %collective-permute-done.2.refs_3_ = bf16[256,512]{1,0:T(8,128)(2,1)S(1)} collective-permute-done((bf16[256,512]{1,0:T(8,128)(2,1)S(1)}, bf16[256,512]{1,0:T(8,128)(2,1)S(1)}, u32[]{:S(2)}, u32[]{:S(2)}) %collective-permute-start.2) | collective-permute-done | bytes 262176 | tf_op jit(solution)/shard_map/ppermute | solution.py:310
  17.3 0.4 collective-permute-done.6.refs_7_
  17.7 0.1 shard_map.122
  17.8 2.9 %collective-permute-start.9 = (bf16[512,512]{1,0:T(8,128)(2,1)S(1)}, bf16[512,512]{1,0:T(8,128)(2,1)S(1)}, u32[]{:S(2)}, u32[]{:S(2)}) collective-permute-start(bf16[512,512]{1,0:T(8,128)(2,1)S(1)} %get-tuple-element.41.refs_0_), channel_id=1, source_target_pairs={{0,8},{2,10},{4,12},{6,14},{8,16},{10,18},{12,20},{14,22},{16,24},... | collective-permute-start | bytes 1572872 | tf_op jit(solution)/shard_map/ppermute | solution.py:317
  20.7 1.3 %collective-permute-start.7 = (bf16[512,512]{1,0:T(8,128)(2,1)S(1)}, bf16[512,512]{1,0:T(8,128)(2,1)S(1)}, u32[]{:S(2)}, u32[]{:S(2)}) collective-permute-start(bf16[512,512]{1,0:T(8,128)(2,1)S(1)} %get-tuple-element.40.refs_2_), channel_id=1, source_target_pairs={{8,0},{10,2},{12,4},{14,6},{16,8},{18,10},{20,12},{22,14},{24,16},... | collective-permute-start | bytes 1572872 | tf_op jit(solution)/shard_map/ppermute | solution.py:317
  22.0 1.4 %collective-permute-start.10 = (bf16[256,128]{1,0:T(8,128)(2,1)S(1)}, bf16[256,128]{1,0:T(8,128)(2,1)S(1)}, u32[]{:S(2)}, u32[]{:S(2)}) collective-permute-start(bf16[256,128]{1,0:T(8,128)(2,1)S(1)} %get-tuple-element.43), channel_id=1, source_target_pairs={{0,2},{2,0},{4,6},{6,4},{8,10},{10,8},{12,14},{14,12},{16,18},{18,... | collective-permute-start | bytes 196616 | tf_op jit(solution)/shard_map/ppermute | solution.py:310
  23.4 1.3 %collective-permute-start.11 = (bf16[256,128]{1,0:T(8,128)(2,1)S(1)}, bf16[256,128]{1,0:T(8,128)(2,1)S(1)}, u32[]{:S(2)}, u32[]{:S(2)}) collective-permute-start(bf16[256,128]{1,0:T(8,128)(2,1)S(1)} %get-tuple-element.44), channel_id=1, source_target_pairs={{0,4},{2,6},{4,0},{6,2},{8,12},{10,14},{12,8},{14,10},{16,20},{18,... | collective-permute-start | bytes 196616 | tf_op jit(solution)/shard_map/ppermute | solution.py:310
  24.7 0.5 collective-permute-start.12
  25.1 2.0 %collective-permute-done.11.refs_2_ = bf16[256,128]{1,0:T(8,128)(2,1)S(1)} collective-permute-done((bf16[256,128]{1,0:T(8,128)(2,1)S(1)}, bf16[256,128]{1,0:T(8,128)(2,1)S(1)}, u32[]{:S(2)}, u32[]{:S(2)}) %collective-permute-start.11) | collective-permute-done | bytes 65568 | tf_op jit(solution)/shard_map/ppermute | solution.py:310
  27.1 1.9 %collective-permute-done.12.refs_3_ = bf16[256,128]{1,0:T(8,128)(2,1)S(1)} collective-permute-done((bf16[256,128]{1,0:T(8,128)(2,1)S(1)}, bf16[256,128]{1,0:T(8,128)(2,1)S(1)}, u32[]{:S(2)}, u32[]{:S(2)}) %collective-permute-start.12) | collective-permute-done | bytes 65568 | tf_op jit(solution)/shard_map/ppermute | solution.py:310
  29.0 1.2 %copy-done = bf16[1024,512]{1,0:T(8,128)(2,1)S(1)} copy-done((bf16[1024,512]{1,0:T(8,128)(2,1)S(1)}, bf16[1024,512]{1,0:T(8,128)(2,1)}, u32[]{:S(2)}) %copy-start) | copy-done | bytes 1048600
  30.2 1.2 %copy-done.7 = bf16[1024,512]{1,0:T(8,128)(2,1)S(1)} copy-done((bf16[1024,512]{1,0:T(8,128)(2,1)S(1)}, bf16[1024,512]{1,0:T(8,128)(2,1)}, u32[]{:S(2)}) %copy-start.7) | copy-done | bytes 1048600
  31.5 1.3 %shard_map.123.refs_7_.refs_1_.refs_2_ = f32[3,1024,128]{2,1,0:T(8,128)S(1)} custom-call(bf16[256,128]{1,0:T(8,128)(2,1)S(1)} %get-tuple-element.42.refs_0_, bf16[256,128]{1,0:T(8,128)(2,1)S(1)} %collective-permute-done.10.refs_1_, bf16[256,128]{1,0:T(8,128)(2,1)S(1)} %collective-permute-done.11.refs_2_, ...), custom_call_target="tpu_custom_call" | custom-call | tf_op jit(solution)/shard_map/pallas_call | solution.py:43
  32.8 4.5 %collective-permute-start.14 = (bf16[512,512]{1,0:T(8,128)(2,1)S(1)}, bf16[512,512]{1,0:T(8,128)(2,1)S(1)}, u32[]{:S(2)}, u32[]{:S(2)}) collective-permute-start(bf16[512,512]{1,0:T(8,128)(2,1)S(1)} %shard_map.125), channel_id=1, source_target_pairs={{0,8},{2,10},{4,12},{6,14},{8,16},{10,18},{12,20},{14,22},{16,24},... | collective-permute-start | bytes 1572872 | tf_op jit(solution)/shard_map/ppermute | solution.py:317
  37.3 1.3 %collective-permute-start.8 = (bf16[512,512]{1,0:T(8,128)(2,1)S(1)}, bf16[512,512]{1,0:T(8,128)(2,1)S(1)}, u32[]{:S(2)}, u32[]{:S(2)}) collective-permute-start(bf16[512,512]{1,0:T(8,128)(2,1)S(1)} %collective-permute-done.7.refs_3_), channel_id=1, source_target_pairs={{8,0},{10,2},{12,4},{14,6},{16,8},{18,10},{20,12},{22,14},{24,16},... | collective-permute-start | bytes 1572872 | tf_op jit(solution)/shard_map/ppermute | solution.py:317
  38.7 6.4 %shard_map.124 = (f32[4,1024,512]{2,1,0:T(8,128)S(1)}, f32[512,128]{1,0:T(8,128)S(1)}, f32[512,128]{1,0:T(8,128)S(1)}) custom-call(bf16[512,512]{1,0:T(8,128)(2,1)S(1)} %get-tuple-element.41.refs_0_, bf16[512,512]{1,0:T(8,128)(2,1)S(1)} %collective-permute-done.9.refs_1_.refs_0_, bf16[512,512]{1,0:T(8,128)(2,1)S(1)} %get-tuple-element.40.refs_2_, ...), custom_call_target="tpu_custom_call" | custom-call | tf_op jit(solution)/shard_map/pallas_call | solution.py:43
  45.1 0.3 collective-permute-start.13
  45.4 3.2 %collective-permute-done.14.refs_0_ = bf16[512,512]{1,0:T(8,128)(2,1)S(1)} collective-permute-done((bf16[512,512]{1,0:T(8,128)(2,1)S(1)}, bf16[512,512]{1,0:T(8,128)(2,1)S(1)}, u32[]{:S(2)}, u32[]{:S(2)}) %collective-permute-start.14) | collective-permute-done | bytes 524320 | tf_op jit(solution)/shard_map/ppermute | solution.py:317
  48.6 2.6 %shard_map.126 = (bf16[128,512]{1,0:T(8,128)(2,1)S(1)}, bf16[128,512]{1,0:T(8,128)(2,1)S(1)}, bf16[128,512]{1,0:T(8,128)(2,1)S(1)}, bf16[128,512]{1,0:T(8,128)(2,1)S(1)}) custom-call(bf16[512,512]{1,0:T(8,128)(2,1)S(1)} %collective-permute-done.14.refs_0_, f32[4,1024,512]{2,1,0:T(8,128)S(1)} %get-tuple-element.46.refs_1_, ...), custom_call_target="tpu_custom_call" | custom-call | tf_op jit(solution)/shard_map/pallas_call | solution.py:43
  51.2 0.9 %collective-permute-start.15 = (bf16[128,512]{1,0:T(8,128)(2,1)S(1)}, bf16[128,512]{1,0:T(8,128)(2,1)S(1)}, u32[]{:S(2)}, u32[]{:S(2)}) collective-permute-start(bf16[128,512]{1,0:T(8,128)(2,1)S(1)} %get-tuple-element.51), channel_id=1, source_target_pairs={{0,2},{2,0},{4,6},{6,4},{8,10},{10,8},{12,14},{14,12},{16,18},{18,... | collective-permute-start | bytes 393224 | tf_op jit(solution)/shard_map/ppermute | solution.py:310
  52.1 0.6 collective-permute-done.13.refs_1_
  52.7 3.2 %collective-permute-start.19 = (f32[256,128]{1,0:T(8,128)S(1)}, f32[256,128]{1,0:T(8,128)S(1)}, u32[]{:S(2)}, u32[]{:S(2)}) collective-permute-start(f32[256,128]{1,0:T(8,128)S(1)} %get-tuple-element.56), channel_id=1, source_target_pairs={{0,16},{2,18},{4,20},{6,22},{8,24},{10,26},{12,28},{14,30},{16,0},... | collective-permute-start | bytes 393224 | tf_op jit(solution)/shard_map/ppermute | solution.py:313
  56.0 1.3 %collective-permute-start.21 = (bf16[128,512]{1,0:T(8,128)(2,1)S(1)}, bf16[128,512]{1,0:T(8,128)(2,1)S(1)}, u32[]{:S(2)}, u32[]{:S(2)}) collective-permute-start(bf16[128,512]{1,0:T(8,128)(2,1)S(1)} %get-tuple-element.59), channel_id=1, source_target_pairs={{0,4},{2,6},{4,0},{6,2},{8,12},{10,14},{12,8},{14,10},{16,20},{18,... | collective-permute-start | bytes 393224 | tf_op jit(solution)/shard_map/ppermute | solution.py:310
  57.3 2.1 %collective-permute-start.22 = (bf16[128,512]{1,0:T(8,128)(2,1)S(1)}, bf16[128,512]{1,0:T(8,128)(2,1)S(1)}, u32[]{:S(2)}, u32[]{:S(2)}) collective-permute-start(bf16[128,512]{1,0:T(8,128)(2,1)S(1)} %get-tuple-element.60), channel_id=1, source_target_pairs={{0,6},{2,4},{4,2},{6,0},{8,14},{10,12},{12,10},{14,8},{16,22},{18,... | collective-permute-start | bytes 393224 | tf_op jit(solution)/shard_map/ppermute | solution.py:310
  59.4 2.6 %shard_map.128 = (bf16[128,512]{1,0:T(8,128)(2,1)S(1)}, bf16[128,512]{1,0:T(8,128)(2,1)S(1)}, bf16[128,512]{1,0:T(8,128)(2,1)S(1)}, bf16[128,512]{1,0:T(8,128)(2,1)S(1)}) custom-call(bf16[512,512]{1,0:T(8,128)(2,1)S(1)} %collective-permute-done.8.refs_0_, f32[4,1024,512]{2,1,0:T(8,128)S(1)} %get-tuple-element.46.refs_1_, ...), custom_call_target="tpu_custom_call" | custom-call | tf_op jit(solution)/shard_map/pallas_call | solution.py:43
  62.0 0.1 collective-permute-start.16
  62.0 1.3 %collective-permute-start.17 = (bf16[128,512]{1,0:T(8,128)(2,1)S(1)}, bf16[128,512]{1,0:T(8,128)(2,1)S(1)}, u32[]{:S(2)}, u32[]{:S(2)}) collective-permute-start(bf16[128,512]{1,0:T(8,128)(2,1)S(1)} %get-tuple-element.54), channel_id=1, source_target_pairs={{0,4},{2,6},{4,0},{6,2},{8,12},{10,14},{12,8},{14,10},{16,20},{18,... | collective-permute-start | bytes 393224 | tf_op jit(solution)/shard_map/ppermute | solution.py:310
  63.3 1.1 %collective-permute-start.18 = (bf16[128,512]{1,0:T(8,128)(2,1)S(1)}, bf16[128,512]{1,0:T(8,128)(2,1)S(1)}, u32[]{:S(2)}, u32[]{:S(2)}) collective-permute-start(bf16[128,512]{1,0:T(8,128)(2,1)S(1)} %get-tuple-element.55), channel_id=1, source_target_pairs={{0,6},{2,4},{4,2},{6,0},{8,14},{10,12},{12,10},{14,8},{16,22},{18,... | collective-permute-start | bytes 393224 | tf_op jit(solution)/shard_map/ppermute | solution.py:310
  64.5 0.4 collective-permute-start.20
  64.8 0.2 collective-permute-done.22.refs_3_
  65.1 1.0 %shard_map.130 = (bf16[128,2048]{1,0:T(8,128)(2,1)}, f32[8,128]{1,0:T(8,128)S(1)}) custom-call(bf16[128,512]{1,0:T(8,128)(2,1)S(1)} %get-tuple-element.49.refs_2_.refs_0_, bf16[128,512]{1,0:T(8,128)(2,1)S(1)} %collective-permute-done.15.refs_6_.refs_1_, bf16[128,512]{1,0:T(8,128)(2,1)S(1)} %collective-permute-done.21.refs_2_, ...), custom_call_target="tpu_custom_call" | custom-call | tf_op jit(solution)/shard_map/pallas_call | solution.py:43
  66.0 2.5 %collective-permute-done.20.refs_1_ = f32[128,128]{1,0:T(8,128)S(1)} collective-permute-done((f32[128,128]{1,0:T(8,128)S(1)}, f32[128,128]{1,0:T(8,128)S(1)}, u32[]{:S(2)}, u32[]{:S(2)}) %collective-permute-start.20) | collective-permute-done | bytes 65568 | tf_op jit(solution)/shard_map/ppermute | solution.py:313
  68.6 2.6 %collective-permute-start.23 = (f32[64,128]{1,0:T(8,128)S(1)}, f32[64,128]{1,0:T(8,128)S(1)}, u32[]{:S(2)}, u32[]{:S(2)}) collective-permute-start(f32[64,128]{1,0:T(8,128)S(1)} %get-tuple-element.62.refs_6_), channel_id=1, source_target_pairs={{0,0},{1,4},{2,2},{3,6},{4,1},{5,5},{6,3},{7,7},{8,8},{9,12},{10,1... | collective-permute-start | bytes 98312 | tf_op jit(solution)/shard_map/ppermute | solution.py:450
  71.2 2.3 %collective-permute-start.24 = (f32[64,128]{1,0:T(8,128)S(1)}, f32[64,128]{1,0:T(8,128)S(1)}, u32[]{:S(2)}, u32[]{:S(2)}) collective-permute-start(f32[64,128]{1,0:T(8,128)S(1)} %get-tuple-element.66), channel_id=1, source_target_pairs={{0,2},{1,6},{2,0},{3,4},{4,3},{5,7},{6,1},{7,5},{8,10},{9,14},{10,... | collective-permute-start | bytes 98312 | tf_op jit(solution)/shard_map/ppermute | solution.py:450
  73.6 1.3 %shard_map.132 = (bf16[128,2048]{1,0:T(8,128)(2,1)}, bf16[128,2048]{1,0:T(8,128)(2,1)}, f32[8,128]{1,0:T(8,128)S(1)}) custom-call(bf16[128,512]{1,0:T(8,128)(2,1)S(1)} %get-tuple-element.52.refs_2_.refs_0_, bf16[128,512]{1,0:T(8,128)(2,1)S(1)} %collective-permute-done.16.refs_1_, bf16[128,512]{1,0:T(8,128)(2,1)S(1)} %collective-permute-done.17.refs_2_, ...), custom_call_target="tpu_custom_call" | custom-call | tf_op jit(solution)/shard_map/pallas_call | solution.py:43
  74.9 1.0 %collective-permute-done.24.refs_1_ = f32[64,128]{1,0:T(8,128)S(1)} collective-permute-done((f32[64,128]{1,0:T(8,128)S(1)}, f32[64,128]{1,0:T(8,128)S(1)}, u32[]{:S(2)}, u32[]{:S(2)}) %collective-permute-start.24) | collective-permute-done | bytes 32800 | tf_op jit(solution)/shard_map/ppermute | solution.py:450
  75.9 0.6 shard_map.133
  (34 shorter events, 0.2 us)
Async XLA Ops:
  0.6 38.0 %copy-start.1 = (bf16[1024,512]{1,0:T(8,128)(2,1)S(1)}, bf16[1024,512]{1,0:T(8,128)(2,1)}, u32[]{:S(2)}) copy-start(bf16[1024,512]{1,0:T(8,128)(2,1)} %constant.8.clone.refs_4_.refs_3_) | copy-start | bytes 3145732
  0.6 38.0 %copy-start.2 = (bf16[512,1024]{1,0:T(8,128)(2,1)S(1)}, bf16[512,1024]{1,0:T(8,128)(2,1)}, u32[]{:S(2)}) copy-start(bf16[512,1024]{1,0:T(8,128)(2,1)} %constant.10.clone.refs_5_.refs_4_) | copy-start | bytes 3145732
  0.7 38.0 %copy-start.6 = (bf16[512,1024]{1,0:T(8,128)(2,1)S(1)}, bf16[512,1024]{1,0:T(8,128)(2,1)}, u32[]{:S(2)}) copy-start(bf16[512,1024]{1,0:T(8,128)(2,1)} %constant.11.clone.refs_6_) | copy-start | bytes 3145732
  2.6 5.7 %collective-permute-start = (bf16[256,512]{1,0:T(8,128)(2,1)S(1)}, bf16[256,512]{1,0:T(8,128)(2,1)S(1)}, u32[]{:S(2)}, u32[]{:S(2)}) collective-permute-start(bf16[256,512]{1,0:T(8,128)(2,1)S(1)} %get-tuple-element.37), channel_id=1, source_target_pairs={{0,2},{2,0},{4,6},{6,4},{8,10},{10,8},{12,14},{14,12},{16,18},{18,... | collective-permute-start | bytes 786440 | tf_op jit(solution)/shard_map/ppermute | solution.py:310
  3.4 9.4 %collective-permute-start.1 = (bf16[256,512]{1,0:T(8,128)(2,1)S(1)}, bf16[256,512]{1,0:T(8,128)(2,1)S(1)}, u32[]{:S(2)}, u32[]{:S(2)}) collective-permute-start(bf16[256,512]{1,0:T(8,128)(2,1)S(1)} %get-tuple-element.38), channel_id=1, source_target_pairs={{0,4},{2,6},{4,0},{6,2},{8,12},{10,14},{12,8},{14,10},{16,20},{18,... | collective-permute-start | bytes 786440 | tf_op jit(solution)/shard_map/ppermute | solution.py:310
  4.6 12.7 %collective-permute-start.2 = (bf16[256,512]{1,0:T(8,128)(2,1)S(1)}, bf16[256,512]{1,0:T(8,128)(2,1)S(1)}, u32[]{:S(2)}, u32[]{:S(2)}) collective-permute-start(bf16[256,512]{1,0:T(8,128)(2,1)S(1)} %get-tuple-element.39), channel_id=1, source_target_pairs={{0,6},{2,4},{4,2},{6,0},{8,14},{10,12},{12,10},{14,8},{16,22},{18,... | collective-permute-start | bytes 786440 | tf_op jit(solution)/shard_map/ppermute | solution.py:310
  5.1 3.3 %collective-permute-start.3 = (bf16[64,256]{1,0:T(8,128)(2,1)}, bf16[64,256]{1,0:T(8,128)(2,1)S(1)}, u32[]{:S(2)}, u32[]{:S(2)}) collective-permute-start(bf16[64,256]{1,0:T(8,128)(2,1)} %refs_0_.3), channel_id=1, source_target_pairs={{0,1},{1,0},{2,3},{3,2},{4,5},{5,4},{6,7},{7,6},{8,9},{9,8},{10,11... | collective-permute-start | bytes 98312 | tf_op jit(solution)/shard_map/ppermute | solution.py:320
  8.4 0.8 copy-start.8
  9.1 8.2 %collective-permute-start.4 = (bf16[64,512]{1,0:T(8,128)(2,1)S(1)}, bf16[64,512]{1,0:T(8,128)(2,1)S(1)}, u32[]{:S(2)}, u32[]{:S(2)}) collective-permute-start(bf16[64,512]{1,0:T(8,128)(2,1)S(1)} %shard_map.121.refs_4_), channel_id=1, source_target_pairs={{0,8},{2,10},{4,12},{6,14},{8,0},{10,2},{12,4},{14,6},{16,24},{18,... | collective-permute-start | bytes 196616 | tf_op jit(solution)/shard_map/ppermute | solution.py:313
  10.5 6.8 %collective-permute-start.5 = (bf16[64,512]{1,0:T(8,128)(2,1)S(1)}, bf16[64,512]{1,0:T(8,128)(2,1)S(1)}, u32[]{:S(2)}, u32[]{:S(2)}) collective-permute-start(bf16[64,512]{1,0:T(8,128)(2,1)S(1)} %shard_map.121.refs_4_), channel_id=1, source_target_pairs={{0,16},{2,18},{4,20},{6,22},{8,24},{10,26},{12,28},{14,30},{16,0},... | collective-permute-start | bytes 196616 | tf_op jit(solution)/shard_map/ppermute | solution.py:313
  12.8 4.9 %collective-permute-start.6 = (bf16[64,512]{1,0:T(8,128)(2,1)S(1)}, bf16[64,512]{1,0:T(8,128)(2,1)S(1)}, u32[]{:S(2)}, u32[]{:S(2)}) collective-permute-start(bf16[64,512]{1,0:T(8,128)(2,1)S(1)} %shard_map.121.refs_4_), channel_id=1, source_target_pairs={{0,24},{2,26},{4,28},{6,30},{8,16},{10,18},{12,20},{14,22},{16,8},... | collective-permute-start | bytes 196616 | tf_op jit(solution)/shard_map/ppermute | solution.py:313
  17.8 14.9 %collective-permute-start.9 = (bf16[512,512]{1,0:T(8,128)(2,1)S(1)}, bf16[512,512]{1,0:T(8,128)(2,1)S(1)}, u32[]{:S(2)}, u32[]{:S(2)}) collective-permute-start(bf16[512,512]{1,0:T(8,128)(2,1)S(1)} %get-tuple-element.41.refs_0_), channel_id=1, source_target_pairs={{0,8},{2,10},{4,12},{6,14},{8,16},{10,18},{12,20},{14,22},{16,24},... | collective-permute-start | bytes 1572872 | tf_op jit(solution)/shard_map/ppermute | solution.py:317
  20.7 16.6 %collective-permute-start.7 = (bf16[512,512]{1,0:T(8,128)(2,1)S(1)}, bf16[512,512]{1,0:T(8,128)(2,1)S(1)}, u32[]{:S(2)}, u32[]{:S(2)}) collective-permute-start(bf16[512,512]{1,0:T(8,128)(2,1)S(1)} %get-tuple-element.40.refs_2_), channel_id=1, source_target_pairs={{8,0},{10,2},{12,4},{14,6},{16,8},{18,10},{20,12},{22,14},{24,16},... | collective-permute-start | bytes 1572872 | tf_op jit(solution)/shard_map/ppermute | solution.py:317
  22.0 3.1 %collective-permute-start.10 = (bf16[256,128]{1,0:T(8,128)(2,1)S(1)}, bf16[256,128]{1,0:T(8,128)(2,1)S(1)}, u32[]{:S(2)}, u32[]{:S(2)}) collective-permute-start(bf16[256,128]{1,0:T(8,128)(2,1)S(1)} %get-tuple-element.43), channel_id=1, source_target_pairs={{0,2},{2,0},{4,6},{6,4},{8,10},{10,8},{12,14},{14,12},{16,18},{18,... | collective-permute-start | bytes 196616 | tf_op jit(solution)/shard_map/ppermute | solution.py:310
  23.4 3.7 %collective-permute-start.11 = (bf16[256,128]{1,0:T(8,128)(2,1)S(1)}, bf16[256,128]{1,0:T(8,128)(2,1)S(1)}, u32[]{:S(2)}, u32[]{:S(2)}) collective-permute-start(bf16[256,128]{1,0:T(8,128)(2,1)S(1)} %get-tuple-element.44), channel_id=1, source_target_pairs={{0,4},{2,6},{4,0},{6,2},{8,12},{10,14},{12,8},{14,10},{16,20},{18,... | collective-permute-start | bytes 196616 | tf_op jit(solution)/shard_map/ppermute | solution.py:310
  24.7 4.3 %collective-permute-start.12 = (bf16[256,128]{1,0:T(8,128)(2,1)S(1)}, bf16[256,128]{1,0:T(8,128)(2,1)S(1)}, u32[]{:S(2)}, u32[]{:S(2)}) collective-permute-start(bf16[256,128]{1,0:T(8,128)(2,1)S(1)} %get-tuple-element.45), channel_id=1, source_target_pairs={{0,6},{2,4},{4,2},{6,0},{8,14},{10,12},{12,10},{14,8},{16,22},{18,... | collective-permute-start | bytes 196616 | tf_op jit(solution)/shard_map/ppermute | solution.py:310
  29.0 1.2 %copy-start = (bf16[1024,512]{1,0:T(8,128)(2,1)S(1)}, bf16[1024,512]{1,0:T(8,128)(2,1)}, u32[]{:S(2)}) copy-start(bf16[1024,512]{1,0:T(8,128)(2,1)} %constant.8.clone.refs_4_.refs_3_) | copy-start | bytes 3145732
  30.2 1.2 %copy-start.7 = (bf16[1024,512]{1,0:T(8,128)(2,1)S(1)}, bf16[1024,512]{1,0:T(8,128)(2,1)}, u32[]{:S(2)}) copy-start(bf16[1024,512]{1,0:T(8,128)(2,1)} %constant.9.clone.refs_5_) | copy-start | bytes 3145732
  32.8 15.8 %collective-permute-start.14 = (bf16[512,512]{1,0:T(8,128)(2,1)S(1)}, bf16[512,512]{1,0:T(8,128)(2,1)S(1)}, u32[]{:S(2)}, u32[]{:S(2)}) collective-permute-start(bf16[512,512]{1,0:T(8,128)(2,1)S(1)} %shard_map.125), channel_id=1, source_target_pairs={{0,8},{2,10},{4,12},{6,14},{8,16},{10,18},{12,20},{14,22},{16,24},... | collective-permute-start | bytes 1572872 | tf_op jit(solution)/shard_map/ppermute | solution.py:317
  37.3 22.0 %collective-permute-start.8 = (bf16[512,512]{1,0:T(8,128)(2,1)S(1)}, bf16[512,512]{1,0:T(8,128)(2,1)S(1)}, u32[]{:S(2)}, u32[]{:S(2)}) collective-permute-start(bf16[512,512]{1,0:T(8,128)(2,1)S(1)} %collective-permute-done.7.refs_3_), channel_id=1, source_target_pairs={{8,0},{10,2},{12,4},{14,6},{16,8},{18,10},{20,12},{22,14},{24,16},... | collective-permute-start | bytes 1572872 | tf_op jit(solution)/shard_map/ppermute | solution.py:317
  45.1 7.6 %collective-permute-start.13 = (f32[512,128]{1,0:T(8,128)S(1)}, f32[512,128]{1,0:T(8,128)S(1)}, u32[]{:S(2)}, u32[]{:S(2)}) collective-permute-start(f32[512,128]{1,0:T(8,128)S(1)} %get-tuple-element.48), channel_id=1, source_target_pairs={{0,1},{1,0},{2,3},{3,2},{4,5},{5,4},{6,7},{7,6},{8,9},{9,8},{10,11... | collective-permute-start | bytes 786440 | tf_op jit(solution)/shard_map/ppermute | solution.py:320
  51.2 13.9 %copy-start.5 = (bf16[128,2048]{1,0:T(8,128)(2,1)S(1)}, bf16[128,2048]{1,0:T(8,128)(2,1)}, u32[]{:S(2)}) copy-start(bf16[128,2048]{1,0:T(8,128)(2,1)} %refs_4_.6) | copy-start | bytes 1572868
  51.2 22.4 %copy-start.3 = (bf16[128,2048]{1,0:T(8,128)(2,1)S(1)}, bf16[128,2048]{1,0:T(8,128)(2,1)}, u32[]{:S(2)}) copy-start(bf16[128,2048]{1,0:T(8,128)(2,1)} %refs_5_.3) | copy-start | bytes 1572868
  51.2 22.4 %copy-start.4 = (bf16[128,2048]{1,0:T(8,128)(2,1)S(1)}, bf16[128,2048]{1,0:T(8,128)(2,1)}, u32[]{:S(2)}) copy-start(bf16[128,2048]{1,0:T(8,128)(2,1)} %refs_4_.7) | copy-start | bytes 1572868
  51.2 8.2 %collective-permute-start.15 = (bf16[128,512]{1,0:T(8,128)(2,1)S(1)}, bf16[128,512]{1,0:T(8,128)(2,1)S(1)}, u32[]{:S(2)}, u32[]{:S(2)}) collective-permute-start(bf16[128,512]{1,0:T(8,128)(2,1)S(1)} %get-tuple-element.51), channel_id=1, source_target_pairs={{0,2},{2,0},{4,6},{6,4},{8,10},{10,8},{12,14},{14,12},{16,18},{18,... | collective-permute-start | bytes 393224 | tf_op jit(solution)/shard_map/ppermute | solution.py:310
  52.7 10.6 %collective-permute-start.19 = (f32[256,128]{1,0:T(8,128)S(1)}, f32[256,128]{1,0:T(8,128)S(1)}, u32[]{:S(2)}, u32[]{:S(2)}) collective-permute-start(f32[256,128]{1,0:T(8,128)S(1)} %get-tuple-element.56), channel_id=1, source_target_pairs={{0,16},{2,18},{4,20},{6,22},{8,24},{10,26},{12,28},{14,30},{16,0},... | collective-permute-start | bytes 393224 | tf_op jit(solution)/shard_map/ppermute | solution.py:313
  56.0 8.5 %collective-permute-start.21 = (bf16[128,512]{1,0:T(8,128)(2,1)S(1)}, bf16[128,512]{1,0:T(8,128)(2,1)S(1)}, u32[]{:S(2)}, u32[]{:S(2)}) collective-permute-start(bf16[128,512]{1,0:T(8,128)(2,1)S(1)} %get-tuple-element.59), channel_id=1, source_target_pairs={{0,4},{2,6},{4,0},{6,2},{8,12},{10,14},{12,8},{14,10},{16,20},{18,... | collective-permute-start | bytes 393224 | tf_op jit(solution)/shard_map/ppermute | solution.py:310
  57.3 7.8 %collective-permute-start.22 = (bf16[128,512]{1,0:T(8,128)(2,1)S(1)}, bf16[128,512]{1,0:T(8,128)(2,1)S(1)}, u32[]{:S(2)}, u32[]{:S(2)}) collective-permute-start(bf16[128,512]{1,0:T(8,128)(2,1)S(1)} %get-tuple-element.60), channel_id=1, source_target_pairs={{0,6},{2,4},{4,2},{6,0},{8,14},{10,12},{12,10},{14,8},{16,22},{18,... | collective-permute-start | bytes 393224 | tf_op jit(solution)/shard_map/ppermute | solution.py:310
  62.0 11.6 %collective-permute-start.16 = (bf16[128,512]{1,0:T(8,128)(2,1)S(1)}, bf16[128,512]{1,0:T(8,128)(2,1)S(1)}, u32[]{:S(2)}, u32[]{:S(2)}) collective-permute-start(bf16[128,512]{1,0:T(8,128)(2,1)S(1)} %get-tuple-element.53), channel_id=1, source_target_pairs={{0,2},{2,0},{4,6},{6,4},{8,10},{10,8},{12,14},{14,12},{16,18},{18,... | collective-permute-start | bytes 393224 | tf_op jit(solution)/shard_map/ppermute | solution.py:310
  62.0 11.5 %collective-permute-start.17 = (bf16[128,512]{1,0:T(8,128)(2,1)S(1)}, bf16[128,512]{1,0:T(8,128)(2,1)S(1)}, u32[]{:S(2)}, u32[]{:S(2)}) collective-permute-start(bf16[128,512]{1,0:T(8,128)(2,1)S(1)} %get-tuple-element.54), channel_id=1, source_target_pairs={{0,4},{2,6},{4,0},{6,2},{8,12},{10,14},{12,8},{14,10},{16,20},{18,... | collective-permute-start | bytes 393224 | tf_op jit(solution)/shard_map/ppermute | solution.py:310
  63.3 10.3 %collective-permute-start.18 = (bf16[128,512]{1,0:T(8,128)(2,1)S(1)}, bf16[128,512]{1,0:T(8,128)(2,1)S(1)}, u32[]{:S(2)}, u32[]{:S(2)}) collective-permute-start(bf16[128,512]{1,0:T(8,128)(2,1)S(1)} %get-tuple-element.55), channel_id=1, source_target_pairs={{0,6},{2,4},{4,2},{6,0},{8,14},{10,12},{12,10},{14,8},{16,22},{18,... | collective-permute-start | bytes 393224 | tf_op jit(solution)/shard_map/ppermute | solution.py:310
  64.5 4.1 %collective-permute-start.20 = (f32[128,128]{1,0:T(8,128)S(1)}, f32[128,128]{1,0:T(8,128)S(1)}, u32[]{:S(2)}, u32[]{:S(2)}) collective-permute-start(f32[128,128]{1,0:T(8,128)S(1)} %get-tuple-element.58), channel_id=1, source_target_pairs={{0,8},{2,10},{4,12},{6,14},{8,0},{10,2},{12,4},{14,6},{16,24},{18,... | collective-permute-start | bytes 196616 | tf_op jit(solution)/shard_map/ppermute | solution.py:313
  68.6 6.3 %collective-permute-start.23 = (f32[64,128]{1,0:T(8,128)S(1)}, f32[64,128]{1,0:T(8,128)S(1)}, u32[]{:S(2)}, u32[]{:S(2)}) collective-permute-start(f32[64,128]{1,0:T(8,128)S(1)} %get-tuple-element.62.refs_6_), channel_id=1, source_target_pairs={{0,0},{1,4},{2,2},{3,6},{4,1},{5,5},{6,3},{7,7},{8,8},{9,12},{10,1... | collective-permute-start | bytes 98312 | tf_op jit(solution)/shard_map/ppermute | solution.py:450
  71.2 4.7 %collective-permute-start.24 = (f32[64,128]{1,0:T(8,128)S(1)}, f32[64,128]{1,0:T(8,128)S(1)}, u32[]{:S(2)}, u32[]{:S(2)}) collective-permute-start(f32[64,128]{1,0:T(8,128)S(1)} %get-tuple-element.66), channel_id=1, source_target_pairs={{0,2},{1,6},{2,0},{3,4},{4,3},{5,7},{6,1},{7,5},{8,10},{9,14},{10,... | collective-permute-start | bytes 98312 | tf_op jit(solution)/shard_map/ppermute | solution.py:450
where the time goes:
time: 77.6 us; the launch traced here: 76.5 us
  starting transfers between devices  34.8 us (45%)
  waiting for transfers between devices  19.6 us (25%)
  Pallas kernels  17.9 us (23%)
  local copies, waits for them, and re-layouts  3.25 us (4%)
  between operations  0.9 us (1%)
    pallas_call x14, Pallas kernels, call(): pl.pallas_call(run, out_shape=[jax.ShapeDtypeStruct(s, t) for s, t in out...  17.9 us
    ppermute x12, starting transfers between devices, inside(): return lax.ppermute(value, 'ctx', [(i, i ^ d) for i in range(n)])  12.3 us
    ppermute x4, starting transfers between devices, shift(): lax.ppermute(value, 'ctx', [(i, i + by) for i in range(n) if 0 <= i + by...  9.99 us
    ppermute x12, waiting for transfers between devices, inside(): return lax.ppermute(value, 'ctx', [(i, i ^ d) for i in range(n)])  8.66 us
    ppermute x5, starting transfers between devices, across(): return lax.ppermute(value, 'ctx', [(i, i ^ d * GROUP) for i in range(n)])  7.28 us
    ppermute x2, starting transfers between devices, owner(): return lax.ppermute(value, ('ctx', 'ch'), pairs)  4.95 us
    ppermute x2, waiting for transfers between devices, swap(): return lax.ppermute(value, 'ch', [(0, 1), (1, 0)])  3.86 us
    unnamed x18, local copies, waits for them, and re-layouts  3.25 us
  transfers between devices with their start and end apart: 25, of which 10 were waited for; matrix products, arithmetic and copies ran while one was open for 0% of the time, Pallas kernels for 20%

commit v1 on v0

--- a/solution.py
+++ b/solution.py
@@ -31,7 +31,7 @@
     return high, rest, np.ascontiguousarray(high.T), np.ascontiguousarray(rest.T)
 
 
-def call(kernel, outs, *args, scratch=(), flops=0, specs=None, out_specs=None, after=()):
+def call(kernel, outs, *args, scratch=(), flops=0, specs=None, out_specs=None, after=(), aliases=None):
     bytes_accessed = sum(a.size * a.dtype.itemsize for a in args)
     bytes_accessed += sum(math.prod(s) * jnp.dtype(t).itemsize for s, t in outs)
     whole = pl.BlockSpec(memory_space=pltpu.VMEM)
@@ -46,6 +46,7 @@
         in_specs=(specs or [whole] * n_args) + [pl.BlockSpec(memory_space=pl.ANY)] * n_after,
         out_specs=out_specs or [whole] * len(outs),
         scratch_shapes=list(scratch),
+        input_output_aliases=aliases or {},
         compiler_params=pltpu.CompilerParams(vmem_limit_bytes=VMEM_LIMIT),
         cost_estimate=pl.CostEstimate(flops=0, bytes_accessed=0, transcendentals=0),
     )(*args, *after)
@@ -78,36 +79,38 @@
                     outs[d][to, r * part : (r + 1) * part] = prod.astype(bf16)
 
 
-def assemble(pieces, p_out, g_out):
-    rows = p_out.shape[0] // GROUP
+def even_super():
+    return lax.rem(lax.axis_index("ctx") // GROUP, 2) == 0
+
+
+def assemble(pieces, lower, upper):
+    rows = lower.shape[0] // GROUP
     mine = lax.rem(lax.axis_index("ctx"), GROUP)
-    for d in range(GROUP):
-        at = pl.ds(pl.multiple_of((mine ^ d) * rows, rows), rows)
-        p_out[at, :] = pieces[d][:rows, :]
-        g_out[at, :] = pieces[d][rows:, :]
+
+    def place(p_out, g_out):
+        for d in range(GROUP):
+            at = pl.ds(pl.multiple_of((mine ^ d) * rows, rows), rows)
+            p_out[at, :] = pieces[d][:rows, :]
+            g_out[at, :] = pieces[d][rows:, :]
+
+    even = even_super()
+    pl.when(even)(lambda: place(lower, upper))
+    pl.when(jnp.logical_not(even))(lambda: place(upper, lower))
 
 
 def assemble_kernel(*refs):
     assemble(refs[:GROUP], *refs[GROUP:])
 
 
-def join_kernel(own, peer, out):
-    part = own.shape[1]
-    x = lax.axis_index("ch")
-    for at, ref in ((x, own), (1 - x, peer)):
-        out[:, pl.ds(pl.multiple_of(at * part, part), part)] = ref[...]
-
-
 def assemble_split_kernel(*refs):
-    pieces, raw, outs = refs[:GROUP], refs[GROUP : -GROUP - 2], refs[-GROUP:]
-    assemble(pieces, *refs[-GROUP - 2 : -GROUP])
-    part = outs[0].shape[1]
-    sup, mine = lax.axis_index("ctx") // GROUP, lax.rem(lax.axis_index("ctx"), GROUP)
-    for i, ref in enumerate(raw):
-        rows = ref.shape[0]
-        at = pl.ds(pl.multiple_of((sup ^ i) * rows, rows), rows)
-        for d in range(GROUP):
-            outs[d][at, :] = ref[:, pl.ds(pl.multiple_of((mine ^ d) * part, part), part)]
+    pieces, raw, (lower, upper, *outs) = refs[:GROUP], refs[GROUP:-4], refs[-4:]
+    assemble(pieces, lower, upper)
+    sup, low = lax.axis_index("ctx") // GROUP, lax.rem(lax.axis_index("ctx"), 2)
+    rows, part = raw[0].shape[0], outs[0].shape[1]
+    for d, ref in enumerate(raw):
+        at = pl.ds(pl.multiple_of((sup ^ d) * rows, rows), rows)
+        for p in range(2):
+            outs[p][at, :] = ref[:, pl.ds(pl.multiple_of((low ^ p) * part, part), part)]
 
 
 def pass_kernel(value, out):
@@ -124,7 +127,9 @@
         if fast:
             rows = slab // GROUP
             for d in range(GROUP):
-                at = pl.ds(pl.multiple_of((mine ^ d) * rows, rows), rows)
+                p, q = divmod(d, 2)
+                member = (q ^ lax.axis_index("ch")) * 2 + (p ^ lax.rem(mine, 2))
+                at = pl.ds(pl.multiple_of(member * rows, rows), rows)
                 taps_ref[s, at, :] = pieces[d][s * rows : (s + 1) * rows, :]
         else:
             taps_ref[s] = pieces[0][s * slab : (s + 1) * slab, :]
@@ -151,10 +156,12 @@
             out[k + 1, im, :] = sign * spec[re]
 
 
-def times(e_re, e_im, a_re, a_im, conj):
-    if conj:
-        return e_re * a_re + e_im * a_im, e_re * a_im - e_im * a_re
+def times(e_re, e_im, a_re, a_im):
     return e_re * a_re - e_im * a_im, e_re * a_im + e_im * a_re
+
+
+def conj_times(e_re, e_im, a_re, a_im):
+    return e_re * a_re + e_im * a_im, e_re * a_im - e_im * a_re
 
 
 def bin_rows(block, visit):
@@ -169,23 +176,42 @@
             visit(sign, pl.ds(re, BINS), pl.ds(im, BINS))
 
 
-def lag_kernel(fast, scale, *refs):
-    blocks, (table, inverse, inverse_rest), refs = refs[:4], refs[4:7], refs[7:]
-    spec, refs = refs[0], refs[1:]
+def own_kernel(lower, upper, table, spec, lag):
+    block, wide = lower.shape
+    part = lag.shape[1]
+    spec[0] = jnp.dot(table[...], lower[...], preferred_element_type=f32)
+    spec[1] = jnp.dot(table[...], upper[...], preferred_element_type=f32)
+    sign = jnp.where(even_super(), 1.0, -1.0).astype(f32)
+
+    def visit(_, re, im):
+        total = None
+        for r in range(wide // part):
+            cols = slice(r * part, (r + 1) * part)
+            t = conj_times(spec[0, re, cols], spec[0, im, cols], spec[1, re, cols], spec[1, im, cols])
+            total = t if total is None else (total[0] + t[0], total[1] + t[1])
+        lag[re, :], lag[im, :] = total[0], total[1] * sign
+
+    bin_rows(block, visit)
+
+
+def lag_kernel(fast, scale, one, two, own, own_lag, table, inverse, inverse_rest, spec, *refs):
     n_out = 2 if fast else 1
     lag_outs, (lag_prod, lag_low, lag_result) = refs[:n_out], refs[n_out:]
-    block, wide = blocks[0].shape
-    part = lag_result.shape[1] // 2
-    for i, ref in enumerate(blocks):
-        spec[i] = jnp.dot(table[...], ref[...], preferred_element_type=f32)
+    block, wide = one.shape
+    part = own_lag.shape[1]
+    spec[0] = jnp.dot(table[...], one[...], preferred_element_type=f32)
+    spec[1] = jnp.dot(table[...], two[...], preferred_element_type=f32)
+    at = jnp.where(even_super(), 1, 0)
 
     def visit(sign, re, im):
-        lags = [None] * 3
+        lags = [(own_lag[re, :], own_lag[im, :]), None, None]
         for r in range(wide // part):
             cols = slice(r * part, (r + 1) * part)
-            p0, p1, g0, g1 = ((spec[i, re, cols], spec[i, im, cols]) for i in range(4))
-            for k, (p, g) in enumerate(((p0, g0), (p1, g0), (p1, g1))):
-                t = times(*p, *g, True)
+            p1 = spec[at, re, cols], spec[at, im, cols]
+            g1 = spec[1 - at, re, cols], spec[1 - at, im, cols]
+            g0 = own[at, re, cols], own[at, im, cols]
+            for k, (p, g) in ((1, (p1, g0)), (2, (p1, g1))):
+                t = conj_times(*p, *g)
                 lags[k] = t if lags[k] is None else (lags[k][0] + t[0], lags[k][1] + t[1])
         for k in range(2):
             cols = slice(k * part, (k + 1) * part)
@@ -210,26 +236,28 @@
             cols = slice(i * part, (i + 1) * part)
             to = slice(s * piece, (s + 1) * piece)
             keep[to, :] = lag_result[pl.ds(pl.multiple_of(low + x * piece, piece), piece), cols]
-            send[to, :] = lag_result[pl.ds(pl.multiple_of(low + (1 - x) * piece, piece), piece), cols]
+            there = pl.ds(pl.multiple_of(low + (1 - x) * piece, piece), piece)
+            send[to, :] = lag_result[there, cols].astype(bf16)
     else:
         for i in range(2):
             lag_outs[0][i * block : (i + 1) * block, :] = lag_result[:, i * part : (i + 1) * part]
 
 
-def conv_kernel(conj, far, near, weights, table, inverse, *refs):
+def conv_kernel(which, far, near, own, weights, table, inverse, *refs):
     outs, (spec, prod, result) = refs[:GROUP], refs[GROUP:]
     block, wide = far.shape
     part = weights.shape[2]
-    first = 2 if conj else 0
+    conj = jnp.where(even_super(), 1 - which, which)
+    side = (1 - 2 * conj).astype(f32)
     spec[...] = jnp.dot(table[...], far[...], preferred_element_type=f32)
 
-    def visit(sign, re, im):
-        e = [(weights[k, re, :], weights[k, im, :]) for k in range(3)]
+    def visit(_, re, im):
+        e = [(weights[k, re, :], weights[k, im, :] * side) for k in range(3)]
         for r in range(wide // part):
             cols = slice(r * part, (r + 1) * part)
-            total = times(*e[2], spec[re, cols], spec[im, cols], conj)
-            for k in range(2):
-                t = times(*e[k], near[first + k, re, cols], near[first + k, im, cols], conj)
+            total = times(*e[2], spec[re, cols], spec[im, cols])
+            for k, ref, i in ((0, own, 1 - which), (1, near, which)):
+                t = times(*e[k], ref[i, re, cols], ref[i, im, cols])
                 total = total[0] + t[0], total[1] + t[1]
             prod[re, cols] = total[0].astype(bf16)
             prod[im, cols] = total[1].astype(bf16)
@@ -247,7 +275,7 @@
     side = lax.rem(lax.axis_index("ctx") // (GROUP * by), 2)
     for out, at in ((mine, side), (theirs, 1 - side)):
         at = pl.ds(pl.multiple_of(at * rows, rows), rows)
-        out[...] = a[at, :] + b[at, :]
+        out[...] = (a[at, :] + b[at, :].astype(f32)).astype(out.dtype)
 
 
 def lag_sum_kernel(a, b, *outs):
@@ -255,7 +283,7 @@
     low = lax.rem(lax.axis_index("ctx"), 2)
     for p in range(2):
         at = pl.ds(pl.multiple_of((low ^ p) * rows, rows), rows)
-        outs[p][...] = a[at, :] + b[at, :]
+        outs[p][...] = a[at, :] + b[at, :].astype(f32)
 
 
 def lag_place_kernel(a, b, out):
@@ -265,29 +293,35 @@
         out[:, pl.ds(pl.multiple_of((low ^ p) * part, part), part)] = ref[...]
 
 
-def finish_kernel(groups, chunks, n, *refs):
-    pieces, gates, refs = refs[:GROUP], refs[GROUP : GROUP + n], refs[GROUP + n :]
-    hbm, token, bufs, sems = refs[:n], refs[n], refs[n + 1 : 2 * n + 1], refs[2 * n + 1]
-    tok, chans = gates[0].shape
+def finish_kernel(groups, chunks, which, *refs):
+    pieces, (grad_out, values, x_one), refs = refs[:GROUP], refs[GROUP : GROUP + 3], refs[-8:]
+    hbm, token, bufs, sems = refs[:3], refs[3], refs[4:7], refs[7]
+    tok, chans = values.shape
     part = groups // GROUP
     mine = lax.rem(lax.axis_index("ctx"), GROUP)
     step = tok // chunks
-    copies = []
-    for i in range(chunks):
-        rows = slice(i * step, (i + 1) * step)
-        for d in range(GROUP):
-            for r in range(chans // groups):
-                cols = pl.ds(pl.multiple_of(r * groups + (mine ^ d) * part, part), part)
-                piece = pieces[d][rows, r * part : (r + 1) * part].astype(f32)
-                for a in range(n):
-                    bufs[a][rows, cols] = (piece * gates[a][rows, cols].astype(f32)).astype(bf16)
-        for a in range(n):
+    token[...] = jnp.zeros_like(token)
+
+    def write(outs):
+        copies = []
+        for i in range(chunks):
+            rows = slice(i * step, (i + 1) * step)
+            for d in range(GROUP):
+                for r in range(chans // groups):
+                    cols = pl.ds(pl.multiple_of(r * groups + (mine ^ d) * part, part), part)
+                    piece = pieces[d][rows, r * part : (r + 1) * part].astype(f32)
+                    for a, gate in outs:
+                        bufs[a][rows, cols] = (piece * gate[rows, cols].astype(f32)).astype(bf16)
             at = pl.ds(i * step, step)
-            copies.append(pltpu.make_async_copy(bufs[a].at[at], hbm[a].at[at], sems.at[a, i]))
-            copies[-1].start()
-    token[...] = jnp.zeros_like(token)
-    for copy in copies:
-        copy.wait()
+            for a, _ in outs:
+                copies.append(pltpu.make_async_copy(bufs[a].at[at], hbm[a].at[at], sems.at[a, i]))
+                copies[-1].start()
+        for copy in copies:
+            copy.wait()
+
+    is_grad = jnp.where(even_super(), 0, 1) == which
+    pl.when(is_grad)(lambda: write([(0, values), (2, x_one)]))
+    pl.when(jnp.logical_not(is_grad))(lambda: write([(1, grad_out)]))
 
 
 def local(x_one, x_two, values, grad_out, filter_raw):
@@ -312,9 +346,9 @@
     def across(value, d):
         return lax.ppermute(value, "ctx", [(i, i ^ (d * GROUP)) for i in range(n)])
 
-    def shift(value, by):
-        by *= GROUP
-        return lax.ppermute(value, "ctx", [(i, i + by) for i in range(n) if 0 <= i + by < n])
+    def beside(value, odd):
+        sides = [(i, ((i // GROUP - odd) ^ 1) + odd) for i in range(n) if i // GROUP >= odd]
+        return lax.ppermute(value, "ctx", [(i, s * GROUP + i % GROUP) for i, s in sides if s < supers])
 
     def swap(value):
         return lax.ppermute(value, "ch", [(0, 1), (1, 0)])
@@ -336,21 +370,34 @@
     )
     pieces = trade(gates)
     if fast:
-        own_rows = call(join_kernel, [((tap_rows, groups), bf16)], filter_raw, swap(filter_raw), after=[pieces[1]])[0]
+        own_rows = call(pass_kernel, [(filter_raw.shape, bf16)], filter_raw, after=[pieces[1]])[0]
         raw = [own_rows] + [across(own_rows, d) for d in range(1, supers)]
-        p_own, g_own, *filt = call(
+        lower, upper, *cut = call(
             assemble_split_kernel,
-            [block_shape, block_shape] + [((supers * tap_rows, part), bf16)] * GROUP,
+            [block_shape, block_shape] + [((supers * tap_rows, part), bf16)] * 2,
             *pieces,
             *raw,
         )
-        filt = trade(filt)
+
+        def to_users(value, p, q):
+            pairs = []
+            for i in range(n):
+                j1, j0 = (i // 2) % 2, i % 2
+                for x in range(2):
+                    to = i // GROUP * GROUP + 2 * x + (p ^ j0)
+                    pairs.append((i * 2 + x, to * 2 + (q ^ j1)))
+            return lax.ppermute(value, ("ctx", "ch"), pairs)
+
+        filt = [to_users(cut[p], p, q) for p in range(2) for q in range(2)]
     else:
-        p_own, g_own = call(assemble_kernel, [block_shape, block_shape], *pieces)
+        lower, upper = call(assemble_kernel, [block_shape, block_shape], *pieces)
         whole = lax.all_gather(filter_raw, "ctx", axis=0, tiled=True)
         whole = lax.all_gather(whole, "ch", axis=1, tiled=True)
         start = lax.rem(lax.axis_index("ctx"), GROUP) * part
         filt = [lax.dynamic_slice(whole, (0, start), (taps, part))]
+    own, own_lag = call(
+        own_kernel, [((2, 2 * block, wide), f32), ((2 * block, part), f32)], lower, upper, table
+    )
     slab = taps // supers if fast else block
     weights = call(
         functools.partial(filter_spectra_kernel, scale, fast),
@@ -359,31 +406,32 @@
         table,
         rest,
         scratch=[pltpu.VMEM((taps // slab, slab, part), bf16)],
+        after=[own_lag],
     )[0]
-    p_back, g_ahead = shift(p_own, 1), shift(g_own, -1)
-    p_next = call(pass_kernel, [block_shape], p_back, after=[weights])[0]
-    p_far, g_far = shift(p_next, 1), shift(g_ahead, -1)
+    one, two = beside(lower, 0), beside(upper, 1)
+    passed = call(pass_kernel, [block_shape], two, after=[weights])[0]
+    far_one, far_two = beside(passed, 0), beside(one, 1)
     near, *lags = call(
         functools.partial(lag_kernel, fast, scale),
-        [((4, 2 * block, wide), f32)] + ([((taps // 2, part), f32)] * 2 if fast else [((taps, part), f32)]),
-        p_own,
-        p_back,
-        g_own,
-        g_ahead,
+        [((2, 2 * block, wide), f32)] + ([((taps // 2, part), t) for t in (f32, bf16)] if fast else [((taps, part), f32)]),
+        one,
+        two,
+        own,
+        own_lag,
         table,
         inverse,
         inverse_rest,
-        scratch=[pltpu.VMEM((2 * block, 2 * part), bf16)] * 2
-        + [pltpu.VMEM((block, 2 * part), f32)],
+        scratch=[pltpu.VMEM((2 * block, 2 * part), bf16)] * 2 + [pltpu.VMEM((block, 2 * part), f32)],
         after=[weights],
     )
 
-    def convolve(conj, prior, far, *more):
+    def convolve(which, prior, far, *more):
         return call(
-            functools.partial(conv_kernel, conj),
+            functools.partial(conv_kernel, which),
             pieces_shape,
             far,
             near,
+            own,
             weights,
             table,
             inverse,
@@ -395,49 +443,53 @@
             after=[prior, *more],
         )
 
-    def finish(pieces, prior, *gates):
-        n = len(gates)
+    def finish(pieces, prior, which, *others):
         return call(
-            functools.partial(finish_kernel, groups, chunks, n),
-            [((tok, chans), bf16)] * n + [((8, 128), f32)],
+            functools.partial(finish_kernel, groups, chunks, which),
+            [((tok, chans), bf16)] * 3 + [((8, 128), f32)],
             *pieces,
-            *gates,
-            scratch=[pltpu.VMEM((tok, chans), bf16)] * n + [pltpu.SemaphoreType.DMA((n, chunks))],
-            out_specs=[in_hbm] * n + [in_vmem],
+            grad_out,
+            values,
+            x_one,
+            *others,
+            scratch=[pltpu.VMEM((tok, chans), bf16)] * 3 + [pltpu.SemaphoreType.DMA((3, chunks))],
+            specs=[in_vmem] * (GROUP + 3) + [in_hbm] * len(others),
+            out_specs=[in_hbm] * 3 + [in_vmem],
+            aliases={GROUP + 3 + i: i for i in range(len(others))},
             after=[prior],
         )
 
-    conv = convolve(False, lags[0], p_far)
+    conv = convolve(0, lags[0], far_one)
     prior = conv[0]
     if fast:
         mine, theirs = lags
         mine, theirs = call(
             functools.partial(lag_half_kernel, 2),
-            [((taps // 4, part), f32)] * 2,
+            [((taps // 4, part), t) for t in (f32, bf16)],
             mine,
             swap(theirs),
             after=[prior],
         )
         prior = mine
     conv = trade(conv)
-    back = convolve(True, prior, g_far, conv[1])
+    back = convolve(1, prior, far_two, conv[1])
     prior = back[0]
     if fast:
         mine, theirs = call(
             functools.partial(lag_half_kernel, 1),
-            [((taps // 8, part), f32)] * 2,
+            [((taps // 8, part), t) for t in (f32, bf16)],
             mine,
             across(theirs, 2),
             after=[prior],
         )
         prior = mine
-    grad_x_two, prior = finish(conv, prior, grad_out)
+    *grads, prior = finish(conv, prior, 0)
     if fast:
         sums = call(
             lag_sum_kernel, [((tap_rows, part), f32)] * 2, mine, across(theirs, 1), after=[prior]
         )
         prior = sums[0]
-    grad_x_one, grad_values, prior = finish(trade(back), prior, values, x_one)
+    *grads, prior = finish(trade(back), prior, 1, *grads)
     if fast:
 
         def owner(value, p):
@@ -456,7 +508,7 @@
         terms = lax.dynamic_update_slice(jnp.zeros((taps, groups), f32), lags[0], (0, start))
         by_taps = lax.psum_scatter(terms, "ctx", scatter_dimension=0, tiled=True)
         grad_filter = lax.psum_scatter(by_taps, "ch", scatter_dimension=1, tiled=True)
-    return (grad_x_one, grad_x_two, grad_values, grad_filter)
+    return (*grads, grad_filter)
 
 
 def solution(mesh):

time: 77.6 us -> 70.9 us (0.914)
  waiting for transfers between devices: 19.6 us -> 17.1 us
  local copies, waits for them, and re-layouts: 3.25 us -> 0.8 us
  starting transfers between devices: 34.8 us -> 33.4 us
    ppermute x2 -> x1, waiting for transfers between devices: 3.86 us -> 0.01 us  [swap(): return lax.ppermute(value, 'ch', [(0, 1), (1, 0)])]
    ppermute x5, waiting for transfers between devices: 2.93 us -> 0.01 us  [across(): return lax.ppermute(value, 'ctx', [(i, i ^ d * GROUP) for i in range(n)])]
    ppermute x4 -> x8, waiting for transfers between devices: 3.23 us -> 5.79 us  [the longest x4 3.89 us: beside(): lax.ppermute(value, 'ctx', [(i, s * GROUP + i % GROUP) for i, s in sides...]
    ppermute x12 -> x9, starting transfers between devices: 12.3 us -> 9.79 us  [inside(): return lax.ppermute(value, 'ctx', [(i, i ^ d) for i in range(n)])]
    unnamed x18 -> x16, local copies, waits for them, and re-layouts: 3.25 us -> 0.8 us
    ppermute x4 -> x8, starting transfers between devices: 9.99 us -> 12.2 us  [the longest x4 6.61 us: beside(): lax.ppermute(value, 'ctx', [(i, s * GROUP + i % GROUP) for i, s in sides...]
    ppermute x5, starting transfers between devices: 7.28 us -> 6.05 us  [across(): return lax.ppermute(value, 'ctx', [(i, i ^ d * GROUP) for i in range(n)])]
    ppermute x2, waiting for transfers between devices: 0.96 us -> 1.83 us  [owner(): return lax.ppermute(value, ('ctx', 'ch'), pairs)]
  transfers between devices with their start and end apart: 25 -> 25, of which waited for: 10 -> 7; matrix products, arithmetic and copies ran while one was open for 0% -> 0% of each run, Pallas kernels for 20% -> 22%
where the time goes in v1:
time: 70.9 us; the launch traced here: 70.6 us
  starting transfers between devices  33.4 us (47%)
  Pallas kernels  18.4 us (26%)
  waiting for transfers between devices  17.1 us (24%)
  between operations  0.9 us (1%)
  local copies, waits for them, and re-layouts  0.8 us (1%)
    pallas_call x15, Pallas kernels, call(): pl.pallas_call(run, out_shape=[jax.ShapeDtypeStruct(s, t) for s, t in out...  18.4 us
    ppermute x9, starting transfers between devices, inside(): return lax.ppermute(value, 'ctx', [(i, i ^ d) for i in range(n)])  9.79 us
    ppermute x9, waiting for transfers between devices, inside(): return lax.ppermute(value, 'ctx', [(i, i ^ d) for i in range(n)])  9.49 us
    ppermute x4, starting transfers between devices, beside(): lax.ppermute(value, 'ctx', [(i, s * GROUP + i % GROUP) for i, s in sides...  6.61 us
    ppermute x5, starting transfers between devices, across(): return lax.ppermute(value, 'ctx', [(i, i ^ d * GROUP) for i in range(n)])  6.05 us
    ppermute x4, starting transfers between devices, to_users(): return lax.ppermute(value, ('ctx', 'ch'), pairs)  5.56 us
    ppermute x2, starting transfers between devices, owner(): return lax.ppermute(value, ('ctx', 'ch'), pairs)  5.04 us
    ppermute x4, waiting for transfers between devices, beside(): lax.ppermute(value, 'ctx', [(i, s * GROUP + i % GROUP) for i, s in sides...  3.89 us
  transfers between devices with their start and end apart: 25, of which 7 were waited for; matrix products, arithmetic and copies ran while one was open for 0% of the time, Pallas kernels for 22%

profile of v1, /device:TPU:3, one launch (start us, length us, event | category | flops | bytes accessed | tf_op | source)
XLA Modules:
  0.0 70.6 jit_solution(4499755112580279817)
XLA Ops:
  0.6 0.0 copy-start
  0.6 0.0 copy-start.6
  0.7 1.9 %shard_map.120 = (bf16[256,512]{1,0:T(8,128)(2,1)S(1)}, bf16[256,512]{1,0:T(8,128)(2,1)S(1)}, bf16[256,512]{1,0:T(8,128)(2,1)S(1)}, bf16[256,512]{1,0:T(8,128)(2,1)S(1)}) custom-call(bf16[128,2048]{1,0:T(8,128)(2,1)} %refs_6_.4, bf16[128,2048]{1,0:T(8,128)(2,1)} %refs_5_.7, bf16[128,2048]{1,0:T(8,128)(2,1)} %refs_4_.7, bf16[128,2048]{1,0:T(8,128)(2,1)} %refs_3_.1), custom_call_target="tpu_custom_call" | custom-call | tf_op jit(solution)/shard_map/pallas_call | solution.py:43
  2.6 0.7 %collective-permute-start = (bf16[256,512]{1,0:T(8,128)(2,1)S(1)}, bf16[256,512]{1,0:T(8,128)(2,1)S(1)}, u32[]{:S(2)}, u32[]{:S(2)}) collective-permute-start(bf16[256,512]{1,0:T(8,128)(2,1)S(1)} %get-tuple-element.40), channel_id=1, source_target_pairs={{0,2},{2,0},{4,6},{6,4},{8,10},{10,8},{12,14},{14,12},{16,18},{18,... | collective-permute-start | bytes 786440 | tf_op jit(solution)/shard_map/ppermute | solution.py:344
  3.4 1.3 %collective-permute-start.1 = (bf16[256,512]{1,0:T(8,128)(2,1)S(1)}, bf16[256,512]{1,0:T(8,128)(2,1)S(1)}, u32[]{:S(2)}, u32[]{:S(2)}) collective-permute-start(bf16[256,512]{1,0:T(8,128)(2,1)S(1)} %get-tuple-element.41), channel_id=1, source_target_pairs={{0,4},{2,6},{4,0},{6,2},{8,12},{10,14},{12,8},{14,10},{16,20},{18,... | collective-permute-start | bytes 786440 | tf_op jit(solution)/shard_map/ppermute | solution.py:344
  4.6 0.5 collective-permute-start.2
  5.1 0.0 collective-permute-done.refs_1_
  5.1 0.8 %copy-done.7 = bf16[64,256]{1,0:T(8,128)(2,1)S(1)} copy-done((bf16[64,256]{1,0:T(8,128)(2,1)S(1)}, bf16[64,256]{1,0:T(8,128)(2,1)}, u32[]{:S(2)}) %copy-start.7) | copy-done | bytes 32792
  5.8 1.3 %collective-permute-start.3 = (bf16[64,256]{1,0:T(8,128)(2,1)S(1)}, bf16[64,256]{1,0:T(8,128)(2,1)S(1)}, u32[]{:S(2)}, u32[]{:S(2)}) collective-permute-start(bf16[64,256]{1,0:T(8,128)(2,1)S(1)} %shard_map.121.refs_4_), channel_id=1, source_target_pairs={{0,8},{2,10},{4,12},{6,14},{8,0},{10,2},{12,4},{14,6},{16,24},{18,... | collective-permute-start | bytes 98312 | tf_op jit(solution)/shard_map/ppermute | solution.py:347
  7.1 2.3 %collective-permute-start.4 = (bf16[64,256]{1,0:T(8,128)(2,1)S(1)}, bf16[64,256]{1,0:T(8,128)(2,1)S(1)}, u32[]{:S(2)}, u32[]{:S(2)}) collective-permute-start(bf16[64,256]{1,0:T(8,128)(2,1)S(1)} %shard_map.121.refs_4_), channel_id=1, source_target_pairs={{0,16},{2,18},{4,20},{6,22},{8,24},{10,26},{12,28},{14,30},{16,0},... | collective-permute-start | bytes 98312 | tf_op jit(solution)/shard_map/ppermute | solution.py:347
  9.4 1.8 %collective-permute-done.1.refs_2_ = bf16[256,512]{1,0:T(8,128)(2,1)S(1)} collective-permute-done((bf16[256,512]{1,0:T(8,128)(2,1)S(1)}, bf16[256,512]{1,0:T(8,128)(2,1)S(1)}, u32[]{:S(2)}, u32[]{:S(2)}) %collective-permute-start.1) | collective-permute-done | bytes 262176 | tf_op jit(solution)/shard_map/ppermute | solution.py:344
  11.2 5.8 %collective-permute-done.2.refs_3_ = bf16[256,512]{1,0:T(8,128)(2,1)S(1)} collective-permute-done((bf16[256,512]{1,0:T(8,128)(2,1)S(1)}, bf16[256,512]{1,0:T(8,128)(2,1)S(1)}, u32[]{:S(2)}, u32[]{:S(2)}) %collective-permute-start.2) | collective-permute-done | bytes 262176 | tf_op jit(solution)/shard_map/ppermute | solution.py:344
  17.0 0.0 collective-permute-done.4.refs_6_
  17.0 0.1 shard_map.122
  17.2 0.7 collective-permute-start.8
  17.9 3.9 %collective-permute-start.6 = (bf16[512,512]{1,0:T(8,128)(2,1)S(1)}, bf16[512,512]{1,0:T(8,128)(2,1)S(1)}, u32[]{:S(2)}, u32[]{:S(2)}) collective-permute-start(bf16[512,512]{1,0:T(8,128)(2,1)S(1)} %get-tuple-element.43.refs_0_), channel_id=1, source_target_pairs={{0,8},{2,10},{4,12},{6,14},{8,0},{10,2},{12,4},{14,6},{16,24},{18,... | collective-permute-start | bytes 1572872 | tf_op jit(solution)/shard_map/ppermute | solution.py:351
  21.7 1.2 %collective-permute-start.10 = (bf16[256,128]{1,0:T(8,128)(2,1)S(1)}, bf16[256,128]{1,0:T(8,128)(2,1)S(1)}, u32[]{:S(2)}, u32[]{:S(2)}) collective-permute-start(bf16[256,128]{1,0:T(8,128)(2,1)S(1)} %get-tuple-element.47), channel_id=1, source_target_pairs={{0,1},{1,5},{2,3},{3,7},{4,0},{5,4},{6,2},{7,6},{8,9},{9,13},{10,1... | collective-permute-start | bytes 196616 | tf_op jit(solution)/shard_map/ppermute | solution.py:389
  23.0 1.2 %collective-permute-start.11 = (bf16[256,128]{1,0:T(8,128)(2,1)S(1)}, bf16[256,128]{1,0:T(8,128)(2,1)S(1)}, u32[]{:S(2)}, u32[]{:S(2)}) collective-permute-start(bf16[256,128]{1,0:T(8,128)(2,1)S(1)} %get-tuple-element.48), channel_id=1, source_target_pairs={{0,2},{1,6},{2,0},{3,4},{4,3},{5,7},{6,1},{7,5},{8,10},{9,14},{10,... | collective-permute-start | bytes 196616 | tf_op jit(solution)/shard_map/ppermute | solution.py:389
  24.1 0.1 collective-permute-start.12
  24.2 0.9 %collective-permute-done.10.refs_1_ = bf16[256,128]{1,0:T(8,128)(2,1)S(1)} collective-permute-done((bf16[256,128]{1,0:T(8,128)(2,1)S(1)}, bf16[256,128]{1,0:T(8,128)(2,1)S(1)}, u32[]{:S(2)}, u32[]{:S(2)}) %collective-permute-start.10) | collective-permute-done | bytes 65568 | tf_op jit(solution)/shard_map/ppermute | solution.py:389
  25.1 3.1 %collective-permute-start.9 = (bf16[256,128]{1,0:T(8,128)(2,1)S(1)}, bf16[256,128]{1,0:T(8,128)(2,1)S(1)}, u32[]{:S(2)}, u32[]{:S(2)}) collective-permute-start(bf16[256,128]{1,0:T(8,128)(2,1)S(1)} %get-tuple-element.47), channel_id=1, source_target_pairs={{0,0},{1,4},{2,2},{3,6},{4,1},{5,5},{6,3},{7,7},{8,8},{9,12},{10,1... | collective-permute-start | bytes 196616 | tf_op jit(solution)/shard_map/ppermute | solution.py:389
  28.3 1.8 %shard_map.123 = (f32[2,1024,512]{2,1,0:T(8,128)S(1)}, f32[1024,128]{1,0:T(8,128)S(1)}) custom-call(bf16[512,512]{1,0:T(8,128)(2,1)S(1)} %get-tuple-element.43.refs_0_, bf16[512,512]{1,0:T(8,128)(2,1)S(1)} %get-tuple-element.44.refs_1_, bf16[1024,512]{1,0:T(8,128)(2,1)S(1)} %copy-done), custom_call_target="tpu_custom_call" | custom-call | tf_op jit(solution)/shard_map/pallas_call | solution.py:43
  30.1 0.9 %collective-permute-done.9.refs_0_ = bf16[256,128]{1,0:T(8,128)(2,1)S(1)} collective-permute-done((bf16[256,128]{1,0:T(8,128)(2,1)S(1)}, bf16[256,128]{1,0:T(8,128)(2,1)S(1)}, u32[]{:S(2)}, u32[]{:S(2)}) %collective-permute-start.9) | collective-permute-done | bytes 65568 | tf_op jit(solution)/shard_map/ppermute | solution.py:389
  31.0 1.3 %shard_map.124.refs_7_.refs_1_.refs_3_ = f32[3,1024,128]{2,1,0:T(8,128)S(1)} custom-call(bf16[256,128]{1,0:T(8,128)(2,1)S(1)} %collective-permute-done.9.refs_0_, bf16[256,128]{1,0:T(8,128)(2,1)S(1)} %collective-permute-done.10.refs_1_, bf16[256,128]{1,0:T(8,128)(2,1)S(1)} %collective-permute-done.11.refs_2_, ...), custom_call_target="tpu_custom_call" | custom-call | tf_op jit(solution)/shard_map/pallas_call | solution.py:43
  32.4 1.4 %collective-permute-start.14 = (bf16[512,512]{1,0:T(8,128)(2,1)S(1)}, bf16[512,512]{1,0:T(8,128)(2,1)S(1)}, u32[]{:S(2)}, u32[]{:S(2)}) collective-permute-start(bf16[512,512]{1,0:T(8,128)(2,1)S(1)} %shard_map.126), channel_id=1, source_target_pairs={{0,8},{2,10},{4,12},{6,14},{8,0},{10,2},{12,4},{14,6},{16,24},{18,... | collective-permute-start | bytes 1572872 | tf_op jit(solution)/shard_map/ppermute | solution.py:351
  33.8 0.7 collective-permute-start.7
  34.5 5.0 %shard_map.125 = (f32[2,1024,512]{2,1,0:T(8,128)S(1)}, f32[512,128]{1,0:T(8,128)S(1)}, bf16[512,128]{1,0:T(8,128)(2,1)S(1)}) custom-call(bf16[512,512]{1,0:T(8,128)(2,1)S(1)} %collective-permute-done.6.refs_0_, bf16[512,512]{1,0:T(8,128)(2,1)S(1)} %collective-permute-done.8.refs_1_.refs_0_, f32[2,1024,512]{2,1,0:T(8,128)S(1)} %get-tuple-element.45.refs_2_, ...), custom_call_target="tpu_custom_call" | custom-call | tf_op jit(solution)/shard_map/pallas_call | solution.py:43
  39.5 0.3 collective-permute-start.13
  39.8 3.9 %collective-permute-done.14.refs_0_ = bf16[512,512]{1,0:T(8,128)(2,1)S(1)} collective-permute-done((bf16[512,512]{1,0:T(8,128)(2,1)S(1)}, bf16[512,512]{1,0:T(8,128)(2,1)S(1)}, u32[]{:S(2)}, u32[]{:S(2)}) %collective-permute-start.14) | collective-permute-done | bytes 524320 | tf_op jit(solution)/shard_map/ppermute | solution.py:351
  43.7 2.6 %shard_map.127 = (bf16[128,512]{1,0:T(8,128)(2,1)S(1)}, bf16[128,512]{1,0:T(8,128)(2,1)S(1)}, bf16[128,512]{1,0:T(8,128)(2,1)S(1)}, bf16[128,512]{1,0:T(8,128)(2,1)S(1)}) custom-call(bf16[512,512]{1,0:T(8,128)(2,1)S(1)} %collective-permute-done.14.refs_0_, f32[2,1024,512]{2,1,0:T(8,128)S(1)} %get-tuple-element.49.refs_1_, ...), custom_call_target="tpu_custom_call" | custom-call | tf_op jit(solution)/shard_map/pallas_call | solution.py:43
  46.2 3.2 %collective-permute-start.15 = (bf16[128,512]{1,0:T(8,128)(2,1)S(1)}, bf16[128,512]{1,0:T(8,128)(2,1)S(1)}, u32[]{:S(2)}, u32[]{:S(2)}) collective-permute-start(bf16[128,512]{1,0:T(8,128)(2,1)S(1)} %get-tuple-element.54), channel_id=1, source_target_pairs={{0,2},{2,0},{4,6},{6,4},{8,10},{10,8},{12,14},{14,12},{16,18},{18,... | collective-permute-start | bytes 393224 | tf_op jit(solution)/shard_map/ppermute | solution.py:344
  49.5 2.4 %collective-permute-start.21 = (bf16[256,128]{1,0:T(8,128)(2,1)S(1)}, bf16[256,128]{1,0:T(8,128)(2,1)S(1)}, u32[]{:S(2)}, u32[]{:S(2)}) collective-permute-start(bf16[256,128]{1,0:T(8,128)(2,1)S(1)} %get-tuple-element.61), channel_id=1, source_target_pairs={{0,16},{2,18},{4,20},{6,22},{8,24},{10,26},{12,28},{14,30},{16,0},... | collective-permute-start | bytes 196616 | tf_op jit(solution)/shard_map/ppermute | solution.py:347
  51.8 1.2 %collective-permute-start.19 = (bf16[128,512]{1,0:T(8,128)(2,1)S(1)}, bf16[128,512]{1,0:T(8,128)(2,1)S(1)}, u32[]{:S(2)}, u32[]{:S(2)}) collective-permute-start(bf16[128,512]{1,0:T(8,128)(2,1)S(1)} %get-tuple-element.59), channel_id=1, source_target_pairs={{0,4},{2,6},{4,0},{6,2},{8,12},{10,14},{12,8},{14,10},{16,20},{18,... | collective-permute-start | bytes 393224 | tf_op jit(solution)/shard_map/ppermute | solution.py:344
  53.1 0.7 %collective-permute-start.20 = (bf16[128,512]{1,0:T(8,128)(2,1)S(1)}, bf16[128,512]{1,0:T(8,128)(2,1)S(1)}, u32[]{:S(2)}, u32[]{:S(2)}) collective-permute-start(bf16[128,512]{1,0:T(8,128)(2,1)S(1)} %get-tuple-element.60), channel_id=1, source_target_pairs={{0,6},{2,4},{4,2},{6,0},{8,14},{10,12},{12,10},{14,8},{16,22},{18,... | collective-permute-start | bytes 393224 | tf_op jit(solution)/shard_map/ppermute | solution.py:344
  53.8 0.0 copy-start.3
  53.8 0.0 copy-start.4
  53.8 2.6 %shard_map.129 = (bf16[128,512]{1,0:T(8,128)(2,1)S(1)}, bf16[128,512]{1,0:T(8,128)(2,1)S(1)}, bf16[128,512]{1,0:T(8,128)(2,1)S(1)}, bf16[128,512]{1,0:T(8,128)(2,1)S(1)}) custom-call(bf16[512,512]{1,0:T(8,128)(2,1)S(1)} %collective-permute-done.7.refs_0_, f32[2,1024,512]{2,1,0:T(8,128)S(1)} %get-tuple-element.49.refs_1_, ...), custom_call_target="tpu_custom_call" | custom-call | tf_op jit(solution)/shard_map/pallas_call | solution.py:43
  56.4 0.1 collective-permute-start.16
  56.5 1.3 %collective-permute-start.17 = (bf16[128,512]{1,0:T(8,128)(2,1)S(1)}, bf16[128,512]{1,0:T(8,128)(2,1)S(1)}, u32[]{:S(2)}, u32[]{:S(2)}) collective-permute-start(bf16[128,512]{1,0:T(8,128)(2,1)S(1)} %get-tuple-element.57), channel_id=1, source_target_pairs={{0,4},{2,6},{4,0},{6,2},{8,12},{10,14},{12,8},{14,10},{16,20},{18,... | collective-permute-start | bytes 393224 | tf_op jit(solution)/shard_map/ppermute | solution.py:344
  57.8 0.8 %collective-permute-start.18 = (bf16[128,512]{1,0:T(8,128)(2,1)S(1)}, bf16[128,512]{1,0:T(8,128)(2,1)S(1)}, u32[]{:S(2)}, u32[]{:S(2)}) collective-permute-start(bf16[128,512]{1,0:T(8,128)(2,1)S(1)} %get-tuple-element.58), channel_id=1, source_target_pairs={{0,6},{2,4},{4,2},{6,0},{8,14},{10,12},{12,10},{14,8},{16,22},{18,... | collective-permute-start | bytes 393224 | tf_op jit(solution)/shard_map/ppermute | solution.py:344
  58.6 0.1 collective-permute-start.22
  58.7 1.9 %collective-permute-done.20.refs_3_ = bf16[128,512]{1,0:T(8,128)(2,1)S(1)} collective-permute-done((bf16[128,512]{1,0:T(8,128)(2,1)S(1)}, bf16[128,512]{1,0:T(8,128)(2,1)S(1)}, u32[]{:S(2)}, u32[]{:S(2)}) %collective-permute-start.20) | collective-permute-done | bytes 131104 | tf_op jit(solution)/shard_map/ppermute | solution.py:344
  60.6 1.3 %shard_map.131 = (bf16[128,2048]{1,0:T(8,128)(2,1)}, bf16[128,2048]{1,0:T(8,128)(2,1)}, bf16[128,2048]{1,0:T(8,128)(2,1)}, f32[8,128]{1,0:T(8,128)S(1)}) custom-call(bf16[128,512]{1,0:T(8,128)(2,1)S(1)} %get-tuple-element.52.refs_2_.refs_0_, bf16[128,512]{1,0:T(8,128)(2,1)S(1)} %collective-permute-done.15.refs_7_.refs_1_, ...), custom_call_target="tpu_custom_call" | custom-call | tf_op jit(solution)/shard_map/pallas_call | solution.py:43
  62.0 3.1 %collective-permute-start.23 = (f32[64,128]{1,0:T(8,128)S(1)}, f32[64,128]{1,0:T(8,128)S(1)}, u32[]{:S(2)}, u32[]{:S(2)}) collective-permute-start(f32[64,128]{1,0:T(8,128)S(1)} %get-tuple-element.68.refs_10_), channel_id=1, source_target_pairs={{0,0},{1,4},{2,2},{3,6},{4,1},{5,5},{6,3},{7,7},{8,8},{9,12},{10,1... | collective-permute-start | bytes 98312 | tf_op jit(solution)/shard_map/ppermute | solution.py:502
  65.1 1.9 %collective-permute-start.24 = (f32[64,128]{1,0:T(8,128)S(1)}, f32[64,128]{1,0:T(8,128)S(1)}, u32[]{:S(2)}, u32[]{:S(2)}) collective-permute-start(f32[64,128]{1,0:T(8,128)S(1)} %get-tuple-element.72), channel_id=1, source_target_pairs={{0,2},{1,6},{2,0},{3,4},{4,3},{5,7},{6,1},{7,5},{8,10},{9,14},{10,... | collective-permute-start | bytes 98312 | tf_op jit(solution)/shard_map/ppermute | solution.py:502
  67.1 1.1 %shard_map.133 = (bf16[128,2048]{1,0:T(8,128)(2,1)}, bf16[128,2048]{1,0:T(8,128)(2,1)}, bf16[128,2048]{1,0:T(8,128)(2,1)}, f32[8,128]{1,0:T(8,128)S(1)}) custom-call(bf16[128,512]{1,0:T(8,128)(2,1)S(1)} %get-tuple-element.55.refs_2_.refs_0_, ...), custom_call_target="tpu_custom_call", output_to_operand_aliasing={{0}: (7, {}), {1}: (8, {}), {2}: (9, {})} | custom-call | tf_op jit(solution)/shard_map/pallas_call | solution.py:43
  68.1 1.8 %collective-permute-done.24.refs_1_ = f32[64,128]{1,0:T(8,128)S(1)} collective-permute-done((f32[64,128]{1,0:T(8,128)S(1)}, f32[64,128]{1,0:T(8,128)S(1)}, u32[]{:S(2)}, u32[]{:S(2)}) %collective-permute-start.24) | collective-permute-done | bytes 32800 | tf_op jit(solution)/shard_map/ppermute | solution.py:502
  70.0 0.6 shard_map.134
  (33 shorter events, 0.2 us)
Async XLA Ops:
  0.6 27.6 %copy-start = (bf16[1024,512]{1,0:T(8,128)(2,1)S(1)}, bf16[1024,512]{1,0:T(8,128)(2,1)}, u32[]{:S(2)}) copy-start(bf16[1024,512]{1,0:T(8,128)(2,1)} %constant.8.clone.refs_2_.refs_4_) | copy-start | bytes 3145732
  0.6 30.4 %copy-start.6 = (bf16[1024,512]{1,0:T(8,128)(2,1)S(1)}, bf16[1024,512]{1,0:T(8,128)(2,1)}, u32[]{:S(2)}) copy-start(bf16[1024,512]{1,0:T(8,128)(2,1)} %constant.9.clone.refs_5_) | copy-start | bytes 3145732
  2.6 2.5 %collective-permute-start = (bf16[256,512]{1,0:T(8,128)(2,1)S(1)}, bf16[256,512]{1,0:T(8,128)(2,1)S(1)}, u32[]{:S(2)}, u32[]{:S(2)}) collective-permute-start(bf16[256,512]{1,0:T(8,128)(2,1)S(1)} %get-tuple-element.40), channel_id=1, source_target_pairs={{0,2},{2,0},{4,6},{6,4},{8,10},{10,8},{12,14},{14,12},{16,18},{18,... | collective-permute-start | bytes 786440 | tf_op jit(solution)/shard_map/ppermute | solution.py:344
  3.4 7.9 %collective-permute-start.1 = (bf16[256,512]{1,0:T(8,128)(2,1)S(1)}, bf16[256,512]{1,0:T(8,128)(2,1)S(1)}, u32[]{:S(2)}, u32[]{:S(2)}) collective-permute-start(bf16[256,512]{1,0:T(8,128)(2,1)S(1)} %get-tuple-element.41), channel_id=1, source_target_pairs={{0,4},{2,6},{4,0},{6,2},{8,12},{10,14},{12,8},{14,10},{16,20},{18,... | collective-permute-start | bytes 786440 | tf_op jit(solution)/shard_map/ppermute | solution.py:344
  4.6 12.4 %collective-permute-start.2 = (bf16[256,512]{1,0:T(8,128)(2,1)S(1)}, bf16[256,512]{1,0:T(8,128)(2,1)S(1)}, u32[]{:S(2)}, u32[]{:S(2)}) collective-permute-start(bf16[256,512]{1,0:T(8,128)(2,1)S(1)} %get-tuple-element.42), channel_id=1, source_target_pairs={{0,6},{2,4},{4,2},{6,0},{8,14},{10,12},{12,10},{14,8},{16,22},{18,... | collective-permute-start | bytes 786440 | tf_op jit(solution)/shard_map/ppermute | solution.py:344
  5.1 0.8 %copy-start.7 = (bf16[64,256]{1,0:T(8,128)(2,1)S(1)}, bf16[64,256]{1,0:T(8,128)(2,1)}, u32[]{:S(2)}) copy-start(bf16[64,256]{1,0:T(8,128)(2,1)} %refs_0_.3) | copy-start | bytes 98308
  5.8 11.2 %collective-permute-start.3 = (bf16[64,256]{1,0:T(8,128)(2,1)S(1)}, bf16[64,256]{1,0:T(8,128)(2,1)S(1)}, u32[]{:S(2)}, u32[]{:S(2)}) collective-permute-start(bf16[64,256]{1,0:T(8,128)(2,1)S(1)} %shard_map.121.refs_4_), channel_id=1, source_target_pairs={{0,8},{2,10},{4,12},{6,14},{8,0},{10,2},{12,4},{14,6},{16,24},{18,... | collective-permute-start | bytes 98312 | tf_op jit(solution)/shard_map/ppermute | solution.py:347
  7.1 9.9 %collective-permute-start.4 = (bf16[64,256]{1,0:T(8,128)(2,1)S(1)}, bf16[64,256]{1,0:T(8,128)(2,1)S(1)}, u32[]{:S(2)}, u32[]{:S(2)}) collective-permute-start(bf16[64,256]{1,0:T(8,128)(2,1)S(1)} %shard_map.121.refs_4_), channel_id=1, source_target_pairs={{0,16},{2,18},{4,20},{6,22},{8,24},{10,26},{12,28},{14,30},{16,0},... | collective-permute-start | bytes 98312 | tf_op jit(solution)/shard_map/ppermute | solution.py:347
  9.4 7.6 %collective-permute-start.5 = (bf16[64,256]{1,0:T(8,128)(2,1)S(1)}, bf16[64,256]{1,0:T(8,128)(2,1)S(1)}, u32[]{:S(2)}, u32[]{:S(2)}) collective-permute-start(bf16[64,256]{1,0:T(8,128)(2,1)S(1)} %shard_map.121.refs_4_), channel_id=1, source_target_pairs={{0,24},{2,26},{4,28},{6,30},{8,16},{10,18},{12,20},{14,22},{16,8},... | collective-permute-start | bytes 98312 | tf_op jit(solution)/shard_map/ppermute | solution.py:347
  17.2 15.2 %collective-permute-start.8 = (bf16[512,512]{1,0:T(8,128)(2,1)S(1)}, bf16[512,512]{1,0:T(8,128)(2,1)S(1)}, u32[]{:S(2)}, u32[]{:S(2)}) collective-permute-start(bf16[512,512]{1,0:T(8,128)(2,1)S(1)} %get-tuple-element.44.refs_1_), channel_id=1, source_target_pairs={{8,16},{10,18},{12,20},{14,22},{16,8},{18,10},{20,12},{22,14},{9,1... | collective-permute-start | bytes 1572872 | tf_op jit(solution)/shard_map/ppermute | solution.py:351
  17.9 15.9 %collective-permute-start.6 = (bf16[512,512]{1,0:T(8,128)(2,1)S(1)}, bf16[512,512]{1,0:T(8,128)(2,1)S(1)}, u32[]{:S(2)}, u32[]{:S(2)}) collective-permute-start(bf16[512,512]{1,0:T(8,128)(2,1)S(1)} %get-tuple-element.43.refs_0_), channel_id=1, source_target_pairs={{0,8},{2,10},{4,12},{6,14},{8,0},{10,2},{12,4},{14,6},{16,24},{18,... | collective-permute-start | bytes 1572872 | tf_op jit(solution)/shard_map/ppermute | solution.py:351
  21.7 3.4 %collective-permute-start.10 = (bf16[256,128]{1,0:T(8,128)(2,1)S(1)}, bf16[256,128]{1,0:T(8,128)(2,1)S(1)}, u32[]{:S(2)}, u32[]{:S(2)}) collective-permute-start(bf16[256,128]{1,0:T(8,128)(2,1)S(1)} %get-tuple-element.47), channel_id=1, source_target_pairs={{0,1},{1,5},{2,3},{3,7},{4,0},{5,4},{6,2},{7,6},{8,9},{9,13},{10,1... | collective-permute-start | bytes 196616 | tf_op jit(solution)/shard_map/ppermute | solution.py:389
  23.0 11.5 %copy-start.1 = (bf16[512,1024]{1,0:T(8,128)(2,1)S(1)}, bf16[512,1024]{1,0:T(8,128)(2,1)}, u32[]{:S(2)}) copy-start(bf16[512,1024]{1,0:T(8,128)(2,1)} %constant.10.clone.refs_5_) | copy-start | bytes 3145732
  23.0 11.5 %copy-start.5 = (bf16[512,1024]{1,0:T(8,128)(2,1)S(1)}, bf16[512,1024]{1,0:T(8,128)(2,1)}, u32[]{:S(2)}) copy-start(bf16[512,1024]{1,0:T(8,128)(2,1)} %constant.11.clone.refs_6_) | copy-start | bytes 3145732
  23.0 7.1 %collective-permute-start.11 = (bf16[256,128]{1,0:T(8,128)(2,1)S(1)}, bf16[256,128]{1,0:T(8,128)(2,1)S(1)}, u32[]{:S(2)}, u32[]{:S(2)}) collective-permute-start(bf16[256,128]{1,0:T(8,128)(2,1)S(1)} %get-tuple-element.48), channel_id=1, source_target_pairs={{0,2},{1,6},{2,0},{3,4},{4,3},{5,7},{6,1},{7,5},{8,10},{9,14},{10,... | collective-permute-start | bytes 196616 | tf_op jit(solution)/shard_map/ppermute | solution.py:389
  24.1 6.0 %collective-permute-start.12 = (bf16[256,128]{1,0:T(8,128)(2,1)S(1)}, bf16[256,128]{1,0:T(8,128)(2,1)S(1)}, u32[]{:S(2)}, u32[]{:S(2)}) collective-permute-start(bf16[256,128]{1,0:T(8,128)(2,1)S(1)} %get-tuple-element.48), channel_id=1, source_target_pairs={{0,3},{1,7},{2,1},{3,5},{4,2},{5,6},{6,0},{7,4},{8,11},{9,15},{10,... | collective-permute-start | bytes 196616 | tf_op jit(solution)/shard_map/ppermute | solution.py:389
  25.1 5.9 %collective-permute-start.9 = (bf16[256,128]{1,0:T(8,128)(2,1)S(1)}, bf16[256,128]{1,0:T(8,128)(2,1)S(1)}, u32[]{:S(2)}, u32[]{:S(2)}) collective-permute-start(bf16[256,128]{1,0:T(8,128)(2,1)S(1)} %get-tuple-element.47), channel_id=1, source_target_pairs={{0,0},{1,4},{2,2},{3,6},{4,1},{5,5},{6,3},{7,7},{8,8},{9,12},{10,1... | collective-permute-start | bytes 196616 | tf_op jit(solution)/shard_map/ppermute | solution.py:389
  32.4 11.3 %collective-permute-start.14 = (bf16[512,512]{1,0:T(8,128)(2,1)S(1)}, bf16[512,512]{1,0:T(8,128)(2,1)S(1)}, u32[]{:S(2)}, u32[]{:S(2)}) collective-permute-start(bf16[512,512]{1,0:T(8,128)(2,1)S(1)} %shard_map.126), channel_id=1, source_target_pairs={{0,8},{2,10},{4,12},{6,14},{8,0},{10,2},{12,4},{14,6},{16,24},{18,... | collective-permute-start | bytes 1572872 | tf_op jit(solution)/shard_map/ppermute | solution.py:351
  33.8 20.0 %collective-permute-start.7 = (bf16[512,512]{1,0:T(8,128)(2,1)S(1)}, bf16[512,512]{1,0:T(8,128)(2,1)S(1)}, u32[]{:S(2)}, u32[]{:S(2)}) collective-permute-start(bf16[512,512]{1,0:T(8,128)(2,1)S(1)} %collective-permute-done.6.refs_0_), channel_id=1, source_target_pairs={{8,16},{10,18},{12,20},{14,22},{16,8},{18,10},{20,12},{22,14},{9,1... | collective-permute-start | bytes 1572872 | tf_op jit(solution)/shard_map/ppermute | solution.py:351
  39.5 10.0 %collective-permute-start.13 = (bf16[512,128]{1,0:T(8,128)(2,1)S(1)}, bf16[512,128]{1,0:T(8,128)(2,1)S(1)}, u32[]{:S(2)}, u32[]{:S(2)}) collective-permute-start(bf16[512,128]{1,0:T(8,128)(2,1)S(1)} %get-tuple-element.51), channel_id=1, source_target_pairs={{0,1},{1,0},{2,3},{3,2},{4,5},{5,4},{6,7},{7,6},{8,9},{9,8},{10,11... | collective-permute-start | bytes 393224 | tf_op jit(solution)/shard_map/ppermute | solution.py:354
  46.2 7.6 %collective-permute-start.15 = (bf16[128,512]{1,0:T(8,128)(2,1)S(1)}, bf16[128,512]{1,0:T(8,128)(2,1)S(1)}, u32[]{:S(2)}, u32[]{:S(2)}) collective-permute-start(bf16[128,512]{1,0:T(8,128)(2,1)S(1)} %get-tuple-element.54), channel_id=1, source_target_pairs={{0,2},{2,0},{4,6},{6,4},{8,10},{10,8},{12,14},{14,12},{16,18},{18,... | collective-permute-start | bytes 393224 | tf_op jit(solution)/shard_map/ppermute | solution.py:344
  49.5 8.3 %collective-permute-start.21 = (bf16[256,128]{1,0:T(8,128)(2,1)S(1)}, bf16[256,128]{1,0:T(8,128)(2,1)S(1)}, u32[]{:S(2)}, u32[]{:S(2)}) collective-permute-start(bf16[256,128]{1,0:T(8,128)(2,1)S(1)} %get-tuple-element.61), channel_id=1, source_target_pairs={{0,16},{2,18},{4,20},{6,22},{8,24},{10,26},{12,28},{14,30},{16,0},... | collective-permute-start | bytes 196616 | tf_op jit(solution)/shard_map/ppermute | solution.py:347
  51.8 6.8 %collective-permute-start.19 = (bf16[128,512]{1,0:T(8,128)(2,1)S(1)}, bf16[128,512]{1,0:T(8,128)(2,1)S(1)}, u32[]{:S(2)}, u32[]{:S(2)}) collective-permute-start(bf16[128,512]{1,0:T(8,128)(2,1)S(1)} %get-tuple-element.59), channel_id=1, source_target_pairs={{0,4},{2,6},{4,0},{6,2},{8,12},{10,14},{12,8},{14,10},{16,20},{18,... | collective-permute-start | bytes 393224 | tf_op jit(solution)/shard_map/ppermute | solution.py:344
  53.1 7.5 %collective-permute-start.20 = (bf16[128,512]{1,0:T(8,128)(2,1)S(1)}, bf16[128,512]{1,0:T(8,128)(2,1)S(1)}, u32[]{:S(2)}, u32[]{:S(2)}) collective-permute-start(bf16[128,512]{1,0:T(8,128)(2,1)S(1)} %get-tuple-element.60), channel_id=1, source_target_pairs={{0,6},{2,4},{4,2},{6,0},{8,14},{10,12},{12,10},{14,8},{16,22},{18,... | collective-permute-start | bytes 393224 | tf_op jit(solution)/shard_map/ppermute | solution.py:344
  53.8 6.8 %copy-start.2 = (bf16[128,2048]{1,0:T(8,128)(2,1)S(1)}, bf16[128,2048]{1,0:T(8,128)(2,1)}, u32[]{:S(2)}) copy-start(bf16[128,2048]{1,0:T(8,128)(2,1)} %refs_6_.4) | copy-start | bytes 1572868
  53.8 6.8 %copy-start.3 = (bf16[128,2048]{1,0:T(8,128)(2,1)S(1)}, bf16[128,2048]{1,0:T(8,128)(2,1)}, u32[]{:S(2)}) copy-start(bf16[128,2048]{1,0:T(8,128)(2,1)} %refs_5_.7) | copy-start | bytes 1572868
  53.8 6.8 %copy-start.4 = (bf16[128,2048]{1,0:T(8,128)(2,1)S(1)}, bf16[128,2048]{1,0:T(8,128)(2,1)}, u32[]{:S(2)}) copy-start(bf16[128,2048]{1,0:T(8,128)(2,1)} %refs_4_.7) | copy-start | bytes 1572868
  56.4 10.7 %collective-permute-start.16 = (bf16[128,512]{1,0:T(8,128)(2,1)S(1)}, bf16[128,512]{1,0:T(8,128)(2,1)S(1)}, u32[]{:S(2)}, u32[]{:S(2)}) collective-permute-start(bf16[128,512]{1,0:T(8,128)(2,1)S(1)} %get-tuple-element.56), channel_id=1, source_target_pairs={{0,2},{2,0},{4,6},{6,4},{8,10},{10,8},{12,14},{14,12},{16,18},{18,... | collective-permute-start | bytes 393224 | tf_op jit(solution)/shard_map/ppermute | solution.py:344
  56.5 10.6 %collective-permute-start.17 = (bf16[128,512]{1,0:T(8,128)(2,1)S(1)}, bf16[128,512]{1,0:T(8,128)(2,1)S(1)}, u32[]{:S(2)}, u32[]{:S(2)}) collective-permute-start(bf16[128,512]{1,0:T(8,128)(2,1)S(1)} %get-tuple-element.57), channel_id=1, source_target_pairs={{0,4},{2,6},{4,0},{6,2},{8,12},{10,14},{12,8},{14,10},{16,20},{18,... | collective-permute-start | bytes 393224 | tf_op jit(solution)/shard_map/ppermute | solution.py:344
  57.8 9.3 %collective-permute-start.18 = (bf16[128,512]{1,0:T(8,128)(2,1)S(1)}, bf16[128,512]{1,0:T(8,128)(2,1)S(1)}, u32[]{:S(2)}, u32[]{:S(2)}) collective-permute-start(bf16[128,512]{1,0:T(8,128)(2,1)S(1)} %get-tuple-element.58), channel_id=1, source_target_pairs={{0,6},{2,4},{4,2},{6,0},{8,14},{10,12},{12,10},{14,8},{16,22},{18,... | collective-permute-start | bytes 393224 | tf_op jit(solution)/shard_map/ppermute | solution.py:344
  58.6 3.3 %collective-permute-start.22 = (bf16[128,128]{1,0:T(8,128)(2,1)S(1)}, bf16[128,128]{1,0:T(8,128)(2,1)S(1)}, u32[]{:S(2)}, u32[]{:S(2)}) collective-permute-start(bf16[128,128]{1,0:T(8,128)(2,1)S(1)} %get-tuple-element.66), channel_id=1, source_target_pairs={{0,8},{2,10},{4,12},{6,14},{8,0},{10,2},{12,4},{14,6},{16,24},{18,... | collective-permute-start | bytes 98312 | tf_op jit(solution)/shard_map/ppermute | solution.py:347
  62.0 6.1 %collective-permute-start.23 = (f32[64,128]{1,0:T(8,128)S(1)}, f32[64,128]{1,0:T(8,128)S(1)}, u32[]{:S(2)}, u32[]{:S(2)}) collective-permute-start(f32[64,128]{1,0:T(8,128)S(1)} %get-tuple-element.68.refs_10_), channel_id=1, source_target_pairs={{0,0},{1,4},{2,2},{3,6},{4,1},{5,5},{6,3},{7,7},{8,8},{9,12},{10,1... | collective-permute-start | bytes 98312 | tf_op jit(solution)/shard_map/ppermute | solution.py:502
  65.1 4.8 %collective-permute-start.24 = (f32[64,128]{1,0:T(8,128)S(1)}, f32[64,128]{1,0:T(8,128)S(1)}, u32[]{:S(2)}, u32[]{:S(2)}) collective-permute-start(f32[64,128]{1,0:T(8,128)S(1)} %get-tuple-element.72), channel_id=1, source_target_pairs={{0,2},{1,6},{2,0},{3,4},{4,3},{5,7},{6,1},{7,5},{8,10},{9,14},{10,... | collective-permute-start | bytes 98312 | tf_op jit(solution)/shard_map/ppermute | solution.py:502

commit v2 on v1

--- a/solution.py
+++ b/solution.py
@@ -14,7 +14,7 @@
 f32 = jnp.float32
 bf16 = jnp.bfloat16
 VMEM_LIMIT = 24 * 1024 * 1024
-BINS = 16
+BINS = 64
 
 
 def dft_tables(block):
@@ -28,7 +28,7 @@
     table = np.concatenate(rows, axis=0)
     high = table.astype(ml_dtypes.bfloat16)
     rest = (table - high.astype(np.float64)).astype(ml_dtypes.bfloat16)
-    return high, rest, np.ascontiguousarray(high.T), np.ascontiguousarray(rest.T)
+    return high, rest, np.ascontiguousarray(high.T)
 
 
 def call(kernel, outs, *args, scratch=(), flops=0, specs=None, out_specs=None, after=(), aliases=None):
@@ -113,8 +113,10 @@
             outs[p][at, :] = ref[:, pl.ds(pl.multiple_of((low ^ p) * part, part), part)]
 
 
-def pass_kernel(value, out):
-    out[...] = value[...]
+def pass_kernel(*refs):
+    n = len(refs) // 2
+    for value, out in zip(refs[:n], refs[n:]):
+        out[...] = value[...]
 
 
 def filter_spectra_kernel(scale, fast, *refs):
@@ -194,9 +196,9 @@
     bin_rows(block, visit)
 
 
-def lag_kernel(fast, scale, one, two, own, own_lag, table, inverse, inverse_rest, spec, *refs):
+def lag_kernel(fast, scale, one, two, own, own_lag, table, inverse, spec, *refs):
     n_out = 2 if fast else 1
-    lag_outs, (lag_prod, lag_low, lag_result) = refs[:n_out], refs[n_out:]
+    lag_outs, (lag_prod, lag_result) = refs[:n_out], refs[n_out:]
     block, wide = one.shape
     part = own_lag.shape[1]
     spec[0] = jnp.dot(table[...], one[...], preferred_element_type=f32)
@@ -217,16 +219,11 @@
             cols = slice(k * part, (k + 1) * part)
             w_re = lags[k][0] + sign * lags[k + 1][1]
             w_im = lags[k][1] - sign * lags[k + 1][0]
-            for rows, w in ((re, w_re), (im, w_im)):
-                high = w.astype(bf16)
-                lag_prod[rows, cols] = high
-                lag_low[rows, cols] = (w - high.astype(f32)).astype(bf16)
+            lag_prod[re, cols] = w_re.astype(bf16)
+            lag_prod[im, cols] = w_im.astype(bf16)
 
     bin_rows(block, visit)
-    total = jnp.dot(inverse[...], lag_prod[...], preferred_element_type=f32)
-    total = total + jnp.dot(inverse[...], lag_low[...], preferred_element_type=f32)
-    total = total + jnp.dot(inverse_rest[...], lag_prod[...], preferred_element_type=f32)
-    lag_result[...] = total * (scale / block)
+    lag_result[...] = jnp.dot(inverse[...], lag_prod[...], preferred_element_type=f32) * (scale / block)
     if fast:
         x = lax.axis_index("ch")
         keep, send = lag_outs
@@ -234,8 +231,10 @@
         for s in range(keep.shape[0] // piece):
             i, low = divmod(2 * piece * s, block)
             cols = slice(i * part, (i + 1) * part)
-            to = slice(s * piece, (s + 1) * piece)
-            keep[to, :] = lag_result[pl.ds(pl.multiple_of(low + x * piece, piece), piece), cols]
+            order = s // 2 + s % 2 * 2
+            to = slice(order * piece, (order + 1) * piece)
+            here = pl.ds(pl.multiple_of(low + x * piece, piece), piece)
+            keep[to, :] = lag_result[here, cols]
             there = pl.ds(pl.multiple_of(low + (1 - x) * piece, piece), piece)
             send[to, :] = lag_result[there, cols].astype(bf16)
     else:
@@ -270,12 +269,20 @@
         outs[d][...] = result[pl.ds(pl.multiple_of((mine ^ d) * rows, rows), rows), :]
 
 
-def lag_half_kernel(by, a, b, mine, theirs):
+def lag_add_kernel(a, b, out):
+    out[...] = (a[...] + b[...].astype(f32)).astype(out.dtype)
+
+
+def lag_half_kernel(by, *refs):
+    terms, (mine, theirs) = refs[:-2], refs[-2:]
     rows = mine.shape[0]
     side = lax.rem(lax.axis_index("ctx") // (GROUP * by), 2)
     for out, at in ((mine, side), (theirs, 1 - side)):
         at = pl.ds(pl.multiple_of(at * rows, rows), rows)
-        out[...] = (a[at, :] + b[at, :].astype(f32)).astype(out.dtype)
+        total = terms[0][at, :].astype(f32)
+        for term in terms[1:]:
+            total = total + term[at, :].astype(f32)
+        out[...] = total.astype(out.dtype)
 
 
 def lag_sum_kernel(a, b, *outs):
@@ -337,7 +344,7 @@
     assert span == 2 and taps % block == 0
     supers = n // GROUP
     scale = 1.0 / math.sqrt(taps)
-    table, rest, inverse, inverse_rest = (jnp.asarray(t) for t in dft_tables(block))
+    table, rest, inverse = (jnp.asarray(t) for t in dft_tables(block))
     fast = n_ch == 2 and supers == 4 and taps // supers <= block
 
     def inside(value, d):
@@ -409,8 +416,8 @@
         after=[own_lag],
     )[0]
     one, two = beside(lower, 0), beside(upper, 1)
-    passed = call(pass_kernel, [block_shape], two, after=[weights])[0]
-    far_one, far_two = beside(passed, 0), beside(one, 1)
+    pass_two, pass_one = call(pass_kernel, [block_shape] * 2, two, one, after=[weights])
+    far_one, far_two = beside(pass_two, 0), beside(pass_one, 1)
     near, *lags = call(
         functools.partial(lag_kernel, fast, scale),
         [((2, 2 * block, wide), f32)] + ([((taps // 2, part), t) for t in (f32, bf16)] if fast else [((taps, part), f32)]),
@@ -420,8 +427,7 @@
         own_lag,
         table,
         inverse,
-        inverse_rest,
-        scratch=[pltpu.VMEM((2 * block, 2 * part), bf16)] * 2 + [pltpu.VMEM((block, 2 * part), f32)],
+        scratch=[pltpu.VMEM((2 * block, 2 * part), bf16), pltpu.VMEM((block, 2 * part), f32)],
         after=[weights],
     )
 
@@ -459,49 +465,49 @@
             after=[prior],
         )
 
-    conv = convolve(0, lags[0], far_one)
+    prior = lags[0]
+    if fast:
+        total = call(lag_add_kernel, [((taps // 2, part), bf16)], lags[0], swap(lags[1]))[0]
+        prior = total
+        turned = []
+        for i in range(n):
+            for x in range(2):
+                to = i // GROUP * GROUP + 2 * x + i % 2
+                turned.append((i * 2 + x, to * 2 + (i // 2) % 2))
+        total = lax.ppermute(total, ("ctx", "ch"), turned)
+    conv = convolve(0, prior, far_one)
     prior = conv[0]
-    if fast:
-        mine, theirs = lags
-        mine, theirs = call(
-            functools.partial(lag_half_kernel, 2),
-            [((taps // 4, part), t) for t in (f32, bf16)],
-            mine,
-            swap(theirs),
-            after=[prior],
-        )
-        prior = mine
     conv = trade(conv)
-    back = convolve(1, prior, far_two, conv[1])
+    back = convolve(1, prior, far_two)
     prior = back[0]
+    back = trade(back)
     if fast:
         mine, theirs = call(
             functools.partial(lag_half_kernel, 1),
-            [((taps // 8, part), t) for t in (f32, bf16)],
-            mine,
-            across(theirs, 2),
+            [((taps // 4, part), t) for t in (f32, bf16)],
+            total,
             after=[prior],
         )
         prior = mine
     *grads, prior = finish(conv, prior, 0)
     if fast:
+        mine, theirs = call(
+            functools.partial(lag_half_kernel, 2),
+            [((taps // 8, part), t) for t in (f32, bf16)],
+            mine,
+            across(theirs, 1),
+            after=[prior],
+        )
+        prior = mine
+    if fast:
         sums = call(
-            lag_sum_kernel, [((tap_rows, part), f32)] * 2, mine, across(theirs, 1), after=[prior]
+            lag_sum_kernel, [((tap_rows, part), f32)] * 2, mine, across(theirs, 2), after=[prior]
         )
         prior = sums[0]
-    *grads, prior = finish(trade(back), prior, 1, *grads)
-    if fast:
-
-        def owner(value, p):
-            pairs = []
-            for i in range(n):
-                j1, j0 = (i // 2) % 2, i % 2
-                for x in range(2):
-                    to = i // GROUP * GROUP + 2 * x + (p ^ j0)
-                    pairs.append((i * 2 + x, to * 2 + j1))
-            return lax.ppermute(value, ("ctx", "ch"), pairs)
-
-        landed = [owner(s, p) for p, s in enumerate(sums)]
+    *grads, prior = finish(back, prior, 1, *grads)
+    if fast:
+
+        landed = [sums[0], inside(sums[1], 1)]
         grad_filter = call(lag_place_kernel, [((tap_rows, own_filters), f32)], *landed, after=[prior])[0]
     else:
         start = lax.rem(lax.axis_index("ctx"), GROUP) * part

time: 70.9 us -> 68.6 us (0.968)
  Pallas kernels: 18.4 us -> 15.9 us
  starting transfers between devices: 33.4 us -> 32.6 us
    ppermute x1, waiting for transfers between devices: 0.01 us -> 3.87 us  [swap(): return lax.ppermute(value, 'ch', [(0, 1), (1, 0)])]
    pallas_call x15 -> x16, Pallas kernels: 18.4 us -> 15.9 us  [call(): pl.pallas_call(run, out_shape=[jax.ShapeDtypeStruct(s, t) for s, t in out...]
    ppermute x5, starting transfers between devices: 6.05 us -> 8.24 us  [across(): return lax.ppermute(value, 'ctx', [(i, i ^ d * GROUP) for i in range(n)])]
    ppermute x4, waiting for transfers between devices: 3.89 us -> 1.83 us  [beside(): lax.ppermute(value, 'ctx', [(i, s * GROUP + i % GROUP) for i, s in sides...]
    ppermute x2 -> x1, starting transfers between devices: 5.04 us -> 3.11 us  [local(): total = lax.ppermute(total, ('ctx', 'ch'), turned)]
    ppermute x5, waiting for transfers between devices: 0.01 us -> 1.89 us  [across(): return lax.ppermute(value, 'ctx', [(i, i ^ d * GROUP) for i in range(n)])]
    ppermute x2 -> x1, waiting for transfers between devices: 1.83 us -> 0.01 us  [local(): total = lax.ppermute(total, ('ctx', 'ch'), turned)]
    ppermute x9 -> x10, waiting for transfers between devices: 9.49 us -> 7.89 us  [inside(): return lax.ppermute(value, 'ctx', [(i, i ^ d) for i in range(n)])]
  transfers between devices with their start and end apart: 25 -> 25, of which waited for: 7 -> 10; matrix products, arithmetic and copies ran while one was open for 0% -> 0% of each run, Pallas kernels for 22% -> 19%
where the time goes in v2:
time: 68.6 us; the launch traced here: 67.9 us
  starting transfers between devices  32.6 us (48%)
  waiting for transfers between devices  17.7 us (26%)
  Pallas kernels  15.9 us (23%)
  between operations  0.86 us (1%)
  local copies, waits for them, and re-layouts  0.79 us (1%)
    pallas_call x16, Pallas kernels, call(): pl.pallas_call(run, out_shape=[jax.ShapeDtypeStruct(s, t) for s, t in out...  15.9 us
    ppermute x10, starting transfers between devices, inside(): return lax.ppermute(value, 'ctx', [(i, i ^ d) for i in range(n)])  9.44 us
    ppermute x5, starting transfers between devices, across(): return lax.ppermute(value, 'ctx', [(i, i ^ d * GROUP) for i in range(n)])  8.24 us
    ppermute x10, waiting for transfers between devices, inside(): return lax.ppermute(value, 'ctx', [(i, i ^ d) for i in range(n)])  7.89 us
    ppermute x4, starting transfers between devices, beside(): lax.ppermute(value, 'ctx', [(i, s * GROUP + i % GROUP) for i, s in sides...  6.46 us
    ppermute x4, starting transfers between devices, to_users(): return lax.ppermute(value, ('ctx', 'ch'), pairs)  5.08 us
    ppermute x1, waiting for transfers between devices, swap(): return lax.ppermute(value, 'ch', [(0, 1), (1, 0)])  3.87 us
    ppermute x1, starting transfers between devices, local(): total = lax.ppermute(total, ('ctx', 'ch'), turned)  3.11 us
  transfers between devices with their start and end apart: 25, of which 10 were waited for; matrix products, arithmetic and copies ran while one was open for 0% of the time, Pallas kernels for 19%

profile of v2, /device:TPU:3, one launch (start us, length us, event | category | flops | bytes accessed | tf_op | source)
XLA Modules:
  0.0 67.9 jit_solution(3708216957065463626)
XLA Ops:
  0.6 0.0 copy-start
  0.6 0.0 copy-start.5
  0.7 1.9 %shard_map.111 = (bf16[256,512]{1,0:T(8,128)(2,1)S(1)}, bf16[256,512]{1,0:T(8,128)(2,1)S(1)}, bf16[256,512]{1,0:T(8,128)(2,1)S(1)}, bf16[256,512]{1,0:T(8,128)(2,1)S(1)}) custom-call(bf16[128,2048]{1,0:T(8,128)(2,1)} %refs_6_.3, bf16[128,2048]{1,0:T(8,128)(2,1)} %refs_5_.7, bf16[128,2048]{1,0:T(8,128)(2,1)} %refs_4_.7, bf16[128,2048]{1,0:T(8,128)(2,1)} %refs_3_.1), custom_call_target="tpu_custom_call" | custom-call | tf_op jit(solution)/shard_map/pallas_call | solution.py:43
  2.6 0.7 %collective-permute-start = (bf16[256,512]{1,0:T(8,128)(2,1)S(1)}, bf16[256,512]{1,0:T(8,128)(2,1)S(1)}, u32[]{:S(2)}, u32[]{:S(2)}) collective-permute-start(bf16[256,512]{1,0:T(8,128)(2,1)S(1)} %get-tuple-element.42), channel_id=1, source_target_pairs={{0,2},{2,0},{4,6},{6,4},{8,10},{10,8},{12,14},{14,12},{16,18},{18,... | collective-permute-start | bytes 786440 | tf_op jit(solution)/shard_map/ppermute | solution.py:351
  3.4 1.3 %collective-permute-start.1 = (bf16[256,512]{1,0:T(8,128)(2,1)S(1)}, bf16[256,512]{1,0:T(8,128)(2,1)S(1)}, u32[]{:S(2)}, u32[]{:S(2)}) collective-permute-start(bf16[256,512]{1,0:T(8,128)(2,1)S(1)} %get-tuple-element.43), channel_id=1, source_target_pairs={{0,4},{2,6},{4,0},{6,2},{8,12},{10,14},{12,8},{14,10},{16,20},{18,... | collective-permute-start | bytes 786440 | tf_op jit(solution)/shard_map/ppermute | solution.py:351
  4.6 0.5 collective-permute-start.2
  5.1 0.0 collective-permute-done.refs_1_
  5.1 0.8 %copy-done.6 = bf16[64,256]{1,0:T(8,128)(2,1)S(1)} copy-done((bf16[64,256]{1,0:T(8,128)(2,1)S(1)}, bf16[64,256]{1,0:T(8,128)(2,1)}, u32[]{:S(2)}) %copy-start.6) | copy-done | bytes 32792
  5.8 1.3 %collective-permute-start.3 = (bf16[64,256]{1,0:T(8,128)(2,1)S(1)}, bf16[64,256]{1,0:T(8,128)(2,1)S(1)}, u32[]{:S(2)}, u32[]{:S(2)}) collective-permute-start(bf16[64,256]{1,0:T(8,128)(2,1)S(1)} %shard_map.112.refs_4_), channel_id=1, source_target_pairs={{0,8},{2,10},{4,12},{6,14},{8,0},{10,2},{12,4},{14,6},{16,24},{18,... | collective-permute-start | bytes 98312 | tf_op jit(solution)/shard_map/ppermute | solution.py:354
  7.1 2.3 %collective-permute-start.4 = (bf16[64,256]{1,0:T(8,128)(2,1)S(1)}, bf16[64,256]{1,0:T(8,128)(2,1)S(1)}, u32[]{:S(2)}, u32[]{:S(2)}) collective-permute-start(bf16[64,256]{1,0:T(8,128)(2,1)S(1)} %shard_map.112.refs_4_), channel_id=1, source_target_pairs={{0,16},{2,18},{4,20},{6,22},{8,24},{10,26},{12,28},{14,30},{16,0},... | collective-permute-start | bytes 98312 | tf_op jit(solution)/shard_map/ppermute | solution.py:354
  9.4 1.8 %collective-permute-done.1.refs_2_ = bf16[256,512]{1,0:T(8,128)(2,1)S(1)} collective-permute-done((bf16[256,512]{1,0:T(8,128)(2,1)S(1)}, bf16[256,512]{1,0:T(8,128)(2,1)S(1)}, u32[]{:S(2)}, u32[]{:S(2)}) %collective-permute-start.1) | collective-permute-done | bytes 262176 | tf_op jit(solution)/shard_map/ppermute | solution.py:351
  11.2 5.8 %collective-permute-done.2.refs_3_ = bf16[256,512]{1,0:T(8,128)(2,1)S(1)} collective-permute-done((bf16[256,512]{1,0:T(8,128)(2,1)S(1)}, bf16[256,512]{1,0:T(8,128)(2,1)S(1)}, u32[]{:S(2)}, u32[]{:S(2)}) %collective-permute-start.2) | collective-permute-done | bytes 262176 | tf_op jit(solution)/shard_map/ppermute | solution.py:351
  17.0 0.1 shard_map.113
  17.2 0.7 %collective-permute-start.6 = (bf16[512,512]{1,0:T(8,128)(2,1)S(1)}, bf16[512,512]{1,0:T(8,128)(2,1)S(1)}, u32[]{:S(2)}, u32[]{:S(2)}) collective-permute-start(bf16[512,512]{1,0:T(8,128)(2,1)S(1)} %get-tuple-element.45.refs_1_), channel_id=1, source_target_pairs={{8,16},{10,18},{12,20},{14,22},{16,8},{18,10},{20,12},{22,14},{9,1... | collective-permute-start | bytes 1572872 | tf_op jit(solution)/shard_map/ppermute | solution.py:358
  17.9 3.9 %collective-permute-start.7 = (bf16[512,512]{1,0:T(8,128)(2,1)S(1)}, bf16[512,512]{1,0:T(8,128)(2,1)S(1)}, u32[]{:S(2)}, u32[]{:S(2)}) collective-permute-start(bf16[512,512]{1,0:T(8,128)(2,1)S(1)} %get-tuple-element.46.refs_0_), channel_id=1, source_target_pairs={{0,8},{2,10},{4,12},{6,14},{8,0},{10,2},{12,4},{14,6},{16,24},{18,... | collective-permute-start | bytes 1572872 | tf_op jit(solution)/shard_map/ppermute | solution.py:358
  21.7 1.9 %collective-permute-start.10 = (bf16[256,128]{1,0:T(8,128)(2,1)S(1)}, bf16[256,128]{1,0:T(8,128)(2,1)S(1)}, u32[]{:S(2)}, u32[]{:S(2)}) collective-permute-start(bf16[256,128]{1,0:T(8,128)(2,1)S(1)} %get-tuple-element.48), channel_id=1, source_target_pairs={{0,2},{1,6},{2,0},{3,4},{4,3},{5,7},{6,1},{7,5},{8,10},{9,14},{10,... | collective-permute-start | bytes 196616 | tf_op jit(solution)/shard_map/ppermute | solution.py:396
  23.6 0.0 collective-permute-start.11
  23.7 3.2 %collective-permute-start.8 = (bf16[256,128]{1,0:T(8,128)(2,1)S(1)}, bf16[256,128]{1,0:T(8,128)(2,1)S(1)}, u32[]{:S(2)}, u32[]{:S(2)}) collective-permute-start(bf16[256,128]{1,0:T(8,128)(2,1)S(1)} %get-tuple-element.47), channel_id=1, source_target_pairs={{0,0},{1,4},{2,2},{3,6},{4,1},{5,5},{6,3},{7,7},{8,8},{9,12},{10,1... | collective-permute-start | bytes 196616 | tf_op jit(solution)/shard_map/ppermute | solution.py:396
  26.8 0.4 collective-permute-done.10.refs_2_
  27.2 1.6 %shard_map.114 = (f32[2,1024,512]{2,1,0:T(8,128)S(1)}, f32[1024,128]{1,0:T(8,128)S(1)}) custom-call(bf16[512,512]{1,0:T(8,128)(2,1)S(1)} %get-tuple-element.46.refs_0_, bf16[512,512]{1,0:T(8,128)(2,1)S(1)} %get-tuple-element.45.refs_1_, bf16[1024,512]{1,0:T(8,128)(2,1)S(1)} %copy-done), custom_call_target="tpu_custom_call" | custom-call | tf_op jit(solution)/shard_map/pallas_call | solution.py:43
  28.8 0.9 %collective-permute-done.8.refs_0_ = bf16[256,128]{1,0:T(8,128)(2,1)S(1)} collective-permute-done((bf16[256,128]{1,0:T(8,128)(2,1)S(1)}, bf16[256,128]{1,0:T(8,128)(2,1)S(1)}, u32[]{:S(2)}, u32[]{:S(2)}) %collective-permute-start.8) | collective-permute-done | bytes 65568 | tf_op jit(solution)/shard_map/ppermute | solution.py:396
  29.7 0.9 %collective-permute-done.9.refs_1_ = bf16[256,128]{1,0:T(8,128)(2,1)S(1)} collective-permute-done((bf16[256,128]{1,0:T(8,128)(2,1)S(1)}, bf16[256,128]{1,0:T(8,128)(2,1)S(1)}, u32[]{:S(2)}, u32[]{:S(2)}) %collective-permute-start.9) | collective-permute-done | bytes 65568 | tf_op jit(solution)/shard_map/ppermute | solution.py:396
  30.6 1.3 %shard_map.115.refs_2_.refs_6_.refs_3_ = f32[3,1024,128]{2,1,0:T(8,128)S(1)} custom-call(bf16[256,128]{1,0:T(8,128)(2,1)S(1)} %collective-permute-done.8.refs_0_, bf16[256,128]{1,0:T(8,128)(2,1)S(1)} %collective-permute-done.9.refs_1_, bf16[256,128]{1,0:T(8,128)(2,1)S(1)} %collective-permute-done.10.refs_2_, ...), custom_call_target="tpu_custom_call" | custom-call | tf_op jit(solution)/shard_map/pallas_call | solution.py:43
  31.9 1.6 %collective-permute-done.7.refs_1_.refs_0_ = bf16[512,512]{1,0:T(8,128)(2,1)S(1)} collective-permute-done((bf16[512,512]{1,0:T(8,128)(2,1)S(1)}, bf16[512,512]{1,0:T(8,128)(2,1)S(1)}, u32[]{:S(2)}, u32[]{:S(2)}) %collective-permute-start.7) | collective-permute-done | bytes 524320 | tf_op jit(solution)/shard_map/ppermute | solution.py:358
  33.6 0.1 shard_map.116
  33.6 1.2 %collective-permute-start.13 = (bf16[512,512]{1,0:T(8,128)(2,1)S(1)}, bf16[512,512]{1,0:T(8,128)(2,1)S(1)}, u32[]{:S(2)}, u32[]{:S(2)}) collective-permute-start(bf16[512,512]{1,0:T(8,128)(2,1)S(1)} %get-tuple-element.53), channel_id=1, source_target_pairs={{0,8},{2,10},{4,12},{6,14},{8,0},{10,2},{12,4},{14,6},{16,24},{18,... | collective-permute-start | bytes 1572872 | tf_op jit(solution)/shard_map/ppermute | solution.py:358
  34.8 0.7 %collective-permute-start.12 = (bf16[512,512]{1,0:T(8,128)(2,1)S(1)}, bf16[512,512]{1,0:T(8,128)(2,1)S(1)}, u32[]{:S(2)}, u32[]{:S(2)}) collective-permute-start(bf16[512,512]{1,0:T(8,128)(2,1)S(1)} %get-tuple-element.50), channel_id=1, source_target_pairs={{8,16},{10,18},{12,20},{14,22},{16,8},{18,10},{20,12},{22,14},{9,1... | collective-permute-start | bytes 1572872 | tf_op jit(solution)/shard_map/ppermute | solution.py:358
  35.5 3.0 %shard_map.117 = (f32[2,1024,512]{2,1,0:T(8,128)S(1)}, f32[512,128]{1,0:T(8,128)S(1)}, bf16[512,128]{1,0:T(8,128)(2,1)S(1)}) custom-call(bf16[512,512]{1,0:T(8,128)(2,1)S(1)} %collective-permute-done.7.refs_1_.refs_0_, bf16[512,512]{1,0:T(8,128)(2,1)S(1)} %collective-permute-done.6.refs_0_.refs_1_, f32[2,1024,512]{2,1,0:T(8,128)S(1)} %get-tuple-element.51.refs_2_, ...), custom_call_target="tpu_custom_call" | custom-call | tf_op jit(solution)/shard_map/pallas_call | solution.py:43
  38.6 0.3 collective-permute-start.14
  38.9 3.9 %collective-permute-done.14.refs_1_ = bf16[512,128]{1,0:T(8,128)(2,1)S(1)} collective-permute-done((bf16[512,128]{1,0:T(8,128)(2,1)S(1)}, bf16[512,128]{1,0:T(8,128)(2,1)S(1)}, u32[]{:S(2)}, u32[]{:S(2)}) %collective-permute-start.14) | collective-permute-done | bytes 131104 | tf_op jit(solution)/shard_map/ppermute | solution.py:361
  42.8 3.1 %collective-permute-start.21 = (bf16[512,128]{1,0:T(8,128)(2,1)S(1)}, bf16[512,128]{1,0:T(8,128)(2,1)S(1)}, u32[]{:S(2)}, u32[]{:S(2)}) collective-permute-start(bf16[512,128]{1,0:T(8,128)(2,1)S(1)} %shard_map.118.refs_6_), channel_id=1, source_target_pairs={{0,0},{1,4},{2,2},{3,6},{4,1},{5,5},{6,3},{7,7},{8,8},{9,12},{10,1... | collective-permute-start | bytes 393224 | tf_op jit(solution)/shard_map/ppermute | solution.py:477
  45.9 0.2 collective-permute-done.13.refs_0_
  46.1 2.4 %shard_map.119 = (bf16[128,512]{1,0:T(8,128)(2,1)S(1)}, bf16[128,512]{1,0:T(8,128)(2,1)S(1)}, bf16[128,512]{1,0:T(8,128)(2,1)S(1)}, bf16[128,512]{1,0:T(8,128)(2,1)S(1)}) custom-call(bf16[512,512]{1,0:T(8,128)(2,1)S(1)} %collective-permute-done.13.refs_0_, f32[2,1024,512]{2,1,0:T(8,128)S(1)} %get-tuple-element.52.refs_1_, ...), custom_call_target="tpu_custom_call" | custom-call | tf_op jit(solution)/shard_map/pallas_call | solution.py:43
  48.5 2.7 %collective-permute-start.18 = (bf16[128,512]{1,0:T(8,128)(2,1)S(1)}, bf16[128,512]{1,0:T(8,128)(2,1)S(1)}, u32[]{:S(2)}, u32[]{:S(2)}) collective-permute-start(bf16[128,512]{1,0:T(8,128)(2,1)S(1)} %get-tuple-element.61), channel_id=1, source_target_pairs={{0,2},{2,0},{4,6},{6,4},{8,10},{10,8},{12,14},{14,12},{16,18},{18,... | collective-permute-start | bytes 393224 | tf_op jit(solution)/shard_map/ppermute | solution.py:351
  51.1 0.6 collective-permute-start.19
  51.7 1.1 %collective-permute-start.20 = (bf16[128,512]{1,0:T(8,128)(2,1)S(1)}, bf16[128,512]{1,0:T(8,128)(2,1)S(1)}, u32[]{:S(2)}, u32[]{:S(2)}) collective-permute-start(bf16[128,512]{1,0:T(8,128)(2,1)S(1)} %get-tuple-element.63), channel_id=1, source_target_pairs={{0,6},{2,4},{4,2},{6,0},{8,14},{10,12},{12,10},{14,8},{16,22},{18,... | collective-permute-start | bytes 393224 | tf_op jit(solution)/shard_map/ppermute | solution.py:351
  52.9 2.4 %shard_map.120 = (bf16[128,512]{1,0:T(8,128)(2,1)S(1)}, bf16[128,512]{1,0:T(8,128)(2,1)S(1)}, bf16[128,512]{1,0:T(8,128)(2,1)S(1)}, bf16[128,512]{1,0:T(8,128)(2,1)S(1)}) custom-call(bf16[512,512]{1,0:T(8,128)(2,1)S(1)} %collective-permute-done.12.refs_0_, f32[2,1024,512]{2,1,0:T(8,128)S(1)} %get-tuple-element.52.refs_1_, ...), custom_call_target="tpu_custom_call" | custom-call | tf_op jit(solution)/shard_map/pallas_call | solution.py:43
  55.3 1.7 %collective-permute-start.22 = (bf16[256,128]{1,0:T(8,128)(2,1)S(1)}, bf16[256,128]{1,0:T(8,128)(2,1)S(1)}, u32[]{:S(2)}, u32[]{:S(2)}) collective-permute-start(bf16[256,128]{1,0:T(8,128)(2,1)S(1)} %get-tuple-element.68), channel_id=1, source_target_pairs={{0,8},{2,10},{4,12},{6,14},{8,0},{10,2},{12,4},{14,6},{16,24},{18,... | collective-permute-start | bytes 196616 | tf_op jit(solution)/shard_map/ppermute | solution.py:354
  57.0 0.4 collective-permute-start.15
  57.5 0.1 collective-permute-start.16
  57.6 1.6 %collective-permute-start.17 = (bf16[128,512]{1,0:T(8,128)(2,1)S(1)}, bf16[128,512]{1,0:T(8,128)(2,1)S(1)}, u32[]{:S(2)}, u32[]{:S(2)}) collective-permute-start(bf16[128,512]{1,0:T(8,128)(2,1)S(1)} %get-tuple-element.60), channel_id=1, source_target_pairs={{0,6},{2,4},{4,2},{6,0},{8,14},{10,12},{12,10},{14,8},{16,22},{18,... | collective-permute-start | bytes 393224 | tf_op jit(solution)/shard_map/ppermute | solution.py:351
  59.2 0.3 collective-permute-done.20.refs_3_
  59.5 1.3 %shard_map.122 = (bf16[128,2048]{1,0:T(8,128)(2,1)}, bf16[128,2048]{1,0:T(8,128)(2,1)}, bf16[128,2048]{1,0:T(8,128)(2,1)}, f32[8,128]{1,0:T(8,128)S(1)}) custom-call(bf16[128,512]{1,0:T(8,128)(2,1)S(1)} %get-tuple-element.56.refs_6_.refs_0_, bf16[128,512]{1,0:T(8,128)(2,1)S(1)} %collective-permute-done.18.refs_1_, ...), custom_call_target="tpu_custom_call" | custom-call | tf_op jit(solution)/shard_map/pallas_call | solution.py:43
  60.9 2.9 %collective-permute-start.23 = (bf16[128,128]{1,0:T(8,128)(2,1)S(1)}, bf16[128,128]{1,0:T(8,128)(2,1)S(1)}, u32[]{:S(2)}, u32[]{:S(2)}) collective-permute-start(bf16[128,128]{1,0:T(8,128)(2,1)S(1)} %get-tuple-element.71), channel_id=1, source_target_pairs={{0,16},{2,18},{4,20},{6,22},{8,24},{10,26},{12,28},{14,30},{16,0},... | collective-permute-start | bytes 98312 | tf_op jit(solution)/shard_map/ppermute | solution.py:354
  63.8 1.9 %collective-permute-done.23.refs_1_ = bf16[128,128]{1,0:T(8,128)(2,1)S(1)} collective-permute-done((bf16[128,128]{1,0:T(8,128)(2,1)S(1)}, bf16[128,128]{1,0:T(8,128)(2,1)S(1)}, u32[]{:S(2)}, u32[]{:S(2)}) %collective-permute-start.23) | collective-permute-done | bytes 32800 | tf_op jit(solution)/shard_map/ppermute | solution.py:354
  65.7 0.5 collective-permute-start.24
  66.1 1.1 %shard_map.125 = (bf16[128,2048]{1,0:T(8,128)(2,1)}, bf16[128,2048]{1,0:T(8,128)(2,1)}, bf16[128,2048]{1,0:T(8,128)(2,1)}, f32[8,128]{1,0:T(8,128)S(1)}) custom-call(bf16[128,512]{1,0:T(8,128)(2,1)S(1)} %get-tuple-element.57.refs_1_.refs_0_, ...), custom_call_target="tpu_custom_call", output_to_operand_aliasing={{0}: (7, {}), {1}: (8, {}), {2}: (9, {})} | custom-call | tf_op jit(solution)/shard_map/pallas_call | solution.py:43
  67.2 0.6 shard_map.126
  (32 shorter events, 0.2 us)
Async XLA Ops:
  0.6 26.6 %copy-start = (bf16[1024,512]{1,0:T(8,128)(2,1)S(1)}, bf16[1024,512]{1,0:T(8,128)(2,1)}, u32[]{:S(2)}) copy-start(bf16[1024,512]{1,0:T(8,128)(2,1)} %constant.6.clone.refs_2_.refs_4_) | copy-start | bytes 3145732
  0.6 30.0 %copy-start.5 = (bf16[1024,512]{1,0:T(8,128)(2,1)S(1)}, bf16[1024,512]{1,0:T(8,128)(2,1)}, u32[]{:S(2)}) copy-start(bf16[1024,512]{1,0:T(8,128)(2,1)} %constant.7.clone.refs_5_) | copy-start | bytes 3145732
  2.6 2.5 %collective-permute-start = (bf16[256,512]{1,0:T(8,128)(2,1)S(1)}, bf16[256,512]{1,0:T(8,128)(2,1)S(1)}, u32[]{:S(2)}, u32[]{:S(2)}) collective-permute-start(bf16[256,512]{1,0:T(8,128)(2,1)S(1)} %get-tuple-element.42), channel_id=1, source_target_pairs={{0,2},{2,0},{4,6},{6,4},{8,10},{10,8},{12,14},{14,12},{16,18},{18,... | collective-permute-start | bytes 786440 | tf_op jit(solution)/shard_map/ppermute | solution.py:351
  3.4 7.9 %collective-permute-start.1 = (bf16[256,512]{1,0:T(8,128)(2,1)S(1)}, bf16[256,512]{1,0:T(8,128)(2,1)S(1)}, u32[]{:S(2)}, u32[]{:S(2)}) collective-permute-start(bf16[256,512]{1,0:T(8,128)(2,1)S(1)} %get-tuple-element.43), channel_id=1, source_target_pairs={{0,4},{2,6},{4,0},{6,2},{8,12},{10,14},{12,8},{14,10},{16,20},{18,... | collective-permute-start | bytes 786440 | tf_op jit(solution)/shard_map/ppermute | solution.py:351
  4.6 12.4 %collective-permute-start.2 = (bf16[256,512]{1,0:T(8,128)(2,1)S(1)}, bf16[256,512]{1,0:T(8,128)(2,1)S(1)}, u32[]{:S(2)}, u32[]{:S(2)}) collective-permute-start(bf16[256,512]{1,0:T(8,128)(2,1)S(1)} %get-tuple-element.44), channel_id=1, source_target_pairs={{0,6},{2,4},{4,2},{6,0},{8,14},{10,12},{12,10},{14,8},{16,22},{18,... | collective-permute-start | bytes 786440 | tf_op jit(solution)/shard_map/ppermute | solution.py:351
  5.1 0.8 %copy-start.6 = (bf16[64,256]{1,0:T(8,128)(2,1)S(1)}, bf16[64,256]{1,0:T(8,128)(2,1)}, u32[]{:S(2)}) copy-start(bf16[64,256]{1,0:T(8,128)(2,1)} %refs_0_.3) | copy-start | bytes 98308
  5.8 11.2 %collective-permute-start.3 = (bf16[64,256]{1,0:T(8,128)(2,1)S(1)}, bf16[64,256]{1,0:T(8,128)(2,1)S(1)}, u32[]{:S(2)}, u32[]{:S(2)}) collective-permute-start(bf16[64,256]{1,0:T(8,128)(2,1)S(1)} %shard_map.112.refs_4_), channel_id=1, source_target_pairs={{0,8},{2,10},{4,12},{6,14},{8,0},{10,2},{12,4},{14,6},{16,24},{18,... | collective-permute-start | bytes 98312 | tf_op jit(solution)/shard_map/ppermute | solution.py:354
  7.1 9.9 %collective-permute-start.4 = (bf16[64,256]{1,0:T(8,128)(2,1)S(1)}, bf16[64,256]{1,0:T(8,128)(2,1)S(1)}, u32[]{:S(2)}, u32[]{:S(2)}) collective-permute-start(bf16[64,256]{1,0:T(8,128)(2,1)S(1)} %shard_map.112.refs_4_), channel_id=1, source_target_pairs={{0,16},{2,18},{4,20},{6,22},{8,24},{10,26},{12,28},{14,30},{16,0},... | collective-permute-start | bytes 98312 | tf_op jit(solution)/shard_map/ppermute | solution.py:354
  9.4 7.6 %collective-permute-start.5 = (bf16[64,256]{1,0:T(8,128)(2,1)S(1)}, bf16[64,256]{1,0:T(8,128)(2,1)S(1)}, u32[]{:S(2)}, u32[]{:S(2)}) collective-permute-start(bf16[64,256]{1,0:T(8,128)(2,1)S(1)} %shard_map.112.refs_4_), channel_id=1, source_target_pairs={{0,24},{2,26},{4,28},{6,30},{8,16},{10,18},{12,20},{14,22},{16,8},... | collective-permute-start | bytes 98312 | tf_op jit(solution)/shard_map/ppermute | solution.py:354
  17.2 14.8 %collective-permute-start.6 = (bf16[512,512]{1,0:T(8,128)(2,1)S(1)}, bf16[512,512]{1,0:T(8,128)(2,1)S(1)}, u32[]{:S(2)}, u32[]{:S(2)}) collective-permute-start(bf16[512,512]{1,0:T(8,128)(2,1)S(1)} %get-tuple-element.45.refs_1_), channel_id=1, source_target_pairs={{8,16},{10,18},{12,20},{14,22},{16,8},{18,10},{20,12},{22,14},{9,1... | collective-permute-start | bytes 1572872 | tf_op jit(solution)/shard_map/ppermute | solution.py:358
  17.9 15.7 %collective-permute-start.7 = (bf16[512,512]{1,0:T(8,128)(2,1)S(1)}, bf16[512,512]{1,0:T(8,128)(2,1)S(1)}, u32[]{:S(2)}, u32[]{:S(2)}) collective-permute-start(bf16[512,512]{1,0:T(8,128)(2,1)S(1)} %get-tuple-element.46.refs_0_), channel_id=1, source_target_pairs={{0,8},{2,10},{4,12},{6,14},{8,0},{10,2},{12,4},{14,6},{16,24},{18,... | collective-permute-start | bytes 1572872 | tf_op jit(solution)/shard_map/ppermute | solution.py:358
  21.7 5.5 %collective-permute-start.10 = (bf16[256,128]{1,0:T(8,128)(2,1)S(1)}, bf16[256,128]{1,0:T(8,128)(2,1)S(1)}, u32[]{:S(2)}, u32[]{:S(2)}) collective-permute-start(bf16[256,128]{1,0:T(8,128)(2,1)S(1)} %get-tuple-element.48), channel_id=1, source_target_pairs={{0,2},{1,6},{2,0},{3,4},{4,3},{5,7},{6,1},{7,5},{8,10},{9,14},{10,... | collective-permute-start | bytes 196616 | tf_op jit(solution)/shard_map/ppermute | solution.py:396
  23.6 5.2 %collective-permute-start.11 = (bf16[256,128]{1,0:T(8,128)(2,1)S(1)}, bf16[256,128]{1,0:T(8,128)(2,1)S(1)}, u32[]{:S(2)}, u32[]{:S(2)}) collective-permute-start(bf16[256,128]{1,0:T(8,128)(2,1)S(1)} %get-tuple-element.48), channel_id=1, source_target_pairs={{0,3},{1,7},{2,1},{3,5},{4,2},{5,6},{6,0},{7,4},{8,11},{9,15},{10,... | collective-permute-start | bytes 196616 | tf_op jit(solution)/shard_map/ppermute | solution.py:396
  23.7 11.9 %copy-start.1 = (bf16[512,1024]{1,0:T(8,128)(2,1)S(1)}, bf16[512,1024]{1,0:T(8,128)(2,1)}, u32[]{:S(2)}) copy-start(bf16[512,1024]{1,0:T(8,128)(2,1)} %constant.8.clone.refs_5_) | copy-start | bytes 3145732
  23.7 6.0 %collective-permute-start.8 = (bf16[256,128]{1,0:T(8,128)(2,1)S(1)}, bf16[256,128]{1,0:T(8,128)(2,1)S(1)}, u32[]{:S(2)}, u32[]{:S(2)}) collective-permute-start(bf16[256,128]{1,0:T(8,128)(2,1)S(1)} %get-tuple-element.47), channel_id=1, source_target_pairs={{0,0},{1,4},{2,2},{3,6},{4,1},{5,5},{6,3},{7,7},{8,8},{9,12},{10,1... | collective-permute-start | bytes 196616 | tf_op jit(solution)/shard_map/ppermute | solution.py:396
  27.2 3.4 %collective-permute-start.9 = (bf16[256,128]{1,0:T(8,128)(2,1)S(1)}, bf16[256,128]{1,0:T(8,128)(2,1)S(1)}, u32[]{:S(2)}, u32[]{:S(2)}) collective-permute-start(bf16[256,128]{1,0:T(8,128)(2,1)S(1)} %get-tuple-element.47), channel_id=1, source_target_pairs={{0,1},{1,5},{2,3},{3,7},{4,0},{5,4},{6,2},{7,6},{8,9},{9,13},{10,1... | collective-permute-start | bytes 196616 | tf_op jit(solution)/shard_map/ppermute | solution.py:396
  33.6 12.4 %collective-permute-start.13 = (bf16[512,512]{1,0:T(8,128)(2,1)S(1)}, bf16[512,512]{1,0:T(8,128)(2,1)S(1)}, u32[]{:S(2)}, u32[]{:S(2)}) collective-permute-start(bf16[512,512]{1,0:T(8,128)(2,1)S(1)} %get-tuple-element.53), channel_id=1, source_target_pairs={{0,8},{2,10},{4,12},{6,14},{8,0},{10,2},{12,4},{14,6},{16,24},{18,... | collective-permute-start | bytes 1572872 | tf_op jit(solution)/shard_map/ppermute | solution.py:358
  34.8 18.0 %collective-permute-start.12 = (bf16[512,512]{1,0:T(8,128)(2,1)S(1)}, bf16[512,512]{1,0:T(8,128)(2,1)S(1)}, u32[]{:S(2)}, u32[]{:S(2)}) collective-permute-start(bf16[512,512]{1,0:T(8,128)(2,1)S(1)} %get-tuple-element.50), channel_id=1, source_target_pairs={{8,16},{10,18},{12,20},{14,22},{16,8},{18,10},{20,12},{22,14},{9,1... | collective-permute-start | bytes 1572872 | tf_op jit(solution)/shard_map/ppermute | solution.py:358
  38.6 4.2 %collective-permute-start.14 = (bf16[512,128]{1,0:T(8,128)(2,1)S(1)}, bf16[512,128]{1,0:T(8,128)(2,1)S(1)}, u32[]{:S(2)}, u32[]{:S(2)}) collective-permute-start(bf16[512,128]{1,0:T(8,128)(2,1)S(1)} %get-tuple-element.55), channel_id=1, source_target_pairs={{0,1},{1,0},{2,3},{3,2},{4,5},{5,4},{6,7},{7,6},{8,9},{9,8},{10,11... | collective-permute-start | bytes 393224 | tf_op jit(solution)/shard_map/ppermute | solution.py:361
  42.8 12.5 %collective-permute-start.21 = (bf16[512,128]{1,0:T(8,128)(2,1)S(1)}, bf16[512,128]{1,0:T(8,128)(2,1)S(1)}, u32[]{:S(2)}, u32[]{:S(2)}) collective-permute-start(bf16[512,128]{1,0:T(8,128)(2,1)S(1)} %shard_map.118.refs_6_), channel_id=1, source_target_pairs={{0,0},{1,4},{2,2},{3,6},{4,1},{5,5},{6,3},{7,7},{8,8},{9,12},{10,1... | collective-permute-start | bytes 393224 | tf_op jit(solution)/shard_map/ppermute | solution.py:477
  48.5 9.0 %collective-permute-start.18 = (bf16[128,512]{1,0:T(8,128)(2,1)S(1)}, bf16[128,512]{1,0:T(8,128)(2,1)S(1)}, u32[]{:S(2)}, u32[]{:S(2)}) collective-permute-start(bf16[128,512]{1,0:T(8,128)(2,1)S(1)} %get-tuple-element.61), channel_id=1, source_target_pairs={{0,2},{2,0},{4,6},{6,4},{8,10},{10,8},{12,14},{14,12},{16,18},{18,... | collective-permute-start | bytes 393224 | tf_op jit(solution)/shard_map/ppermute | solution.py:351
  51.1 6.4 %collective-permute-start.19 = (bf16[128,512]{1,0:T(8,128)(2,1)S(1)}, bf16[128,512]{1,0:T(8,128)(2,1)S(1)}, u32[]{:S(2)}, u32[]{:S(2)}) collective-permute-start(bf16[128,512]{1,0:T(8,128)(2,1)S(1)} %get-tuple-element.62), channel_id=1, source_target_pairs={{0,4},{2,6},{4,0},{6,2},{8,12},{10,14},{12,8},{14,10},{16,20},{18,... | collective-permute-start | bytes 393224 | tf_op jit(solution)/shard_map/ppermute | solution.py:351
  51.7 7.7 %collective-permute-start.20 = (bf16[128,512]{1,0:T(8,128)(2,1)S(1)}, bf16[128,512]{1,0:T(8,128)(2,1)S(1)}, u32[]{:S(2)}, u32[]{:S(2)}) collective-permute-start(bf16[128,512]{1,0:T(8,128)(2,1)S(1)} %get-tuple-element.63), channel_id=1, source_target_pairs={{0,6},{2,4},{4,2},{6,0},{8,14},{10,12},{12,10},{14,8},{16,22},{18,... | collective-permute-start | bytes 393224 | tf_op jit(solution)/shard_map/ppermute | solution.py:351
  52.8 6.6 %copy-start.2 = (bf16[128,2048]{1,0:T(8,128)(2,1)S(1)}, bf16[128,2048]{1,0:T(8,128)(2,1)}, u32[]{:S(2)}) copy-start(bf16[128,2048]{1,0:T(8,128)(2,1)} %refs_6_.3) | copy-start | bytes 1572868
  52.8 6.6 %copy-start.3 = (bf16[128,2048]{1,0:T(8,128)(2,1)S(1)}, bf16[128,2048]{1,0:T(8,128)(2,1)}, u32[]{:S(2)}) copy-start(bf16[128,2048]{1,0:T(8,128)(2,1)} %refs_5_.7) | copy-start | bytes 1572868
  52.8 6.6 %copy-start.4 = (bf16[128,2048]{1,0:T(8,128)(2,1)S(1)}, bf16[128,2048]{1,0:T(8,128)(2,1)}, u32[]{:S(2)}) copy-start(bf16[128,2048]{1,0:T(8,128)(2,1)} %refs_4_.7) | copy-start | bytes 1572868
  55.3 5.5 %collective-permute-start.22 = (bf16[256,128]{1,0:T(8,128)(2,1)S(1)}, bf16[256,128]{1,0:T(8,128)(2,1)S(1)}, u32[]{:S(2)}, u32[]{:S(2)}) collective-permute-start(bf16[256,128]{1,0:T(8,128)(2,1)S(1)} %get-tuple-element.68), channel_id=1, source_target_pairs={{0,8},{2,10},{4,12},{6,14},{8,0},{10,2},{12,4},{14,6},{16,24},{18,... | collective-permute-start | bytes 196616 | tf_op jit(solution)/shard_map/ppermute | solution.py:354
  57.0 9.1 %collective-permute-start.15 = (bf16[128,512]{1,0:T(8,128)(2,1)S(1)}, bf16[128,512]{1,0:T(8,128)(2,1)S(1)}, u32[]{:S(2)}, u32[]{:S(2)}) collective-permute-start(bf16[128,512]{1,0:T(8,128)(2,1)S(1)} %get-tuple-element.58), channel_id=1, source_target_pairs={{0,2},{2,0},{4,6},{6,4},{8,10},{10,8},{12,14},{14,12},{16,18},{18,... | collective-permute-start | bytes 393224 | tf_op jit(solution)/shard_map/ppermute | solution.py:351
  57.5 8.6 %collective-permute-start.16 = (bf16[128,512]{1,0:T(8,128)(2,1)S(1)}, bf16[128,512]{1,0:T(8,128)(2,1)S(1)}, u32[]{:S(2)}, u32[]{:S(2)}) collective-permute-start(bf16[128,512]{1,0:T(8,128)(2,1)S(1)} %get-tuple-element.59), channel_id=1, source_target_pairs={{0,4},{2,6},{4,0},{6,2},{8,12},{10,14},{12,8},{14,10},{16,20},{18,... | collective-permute-start | bytes 393224 | tf_op jit(solution)/shard_map/ppermute | solution.py:351
  57.6 8.6 %collective-permute-start.17 = (bf16[128,512]{1,0:T(8,128)(2,1)S(1)}, bf16[128,512]{1,0:T(8,128)(2,1)S(1)}, u32[]{:S(2)}, u32[]{:S(2)}) collective-permute-start(bf16[128,512]{1,0:T(8,128)(2,1)S(1)} %get-tuple-element.60), channel_id=1, source_target_pairs={{0,6},{2,4},{4,2},{6,0},{8,14},{10,12},{12,10},{14,8},{16,22},{18,... | collective-permute-start | bytes 393224 | tf_op jit(solution)/shard_map/ppermute | solution.py:351
  60.9 4.8 %collective-permute-start.23 = (bf16[128,128]{1,0:T(8,128)(2,1)S(1)}, bf16[128,128]{1,0:T(8,128)(2,1)S(1)}, u32[]{:S(2)}, u32[]{:S(2)}) collective-permute-start(bf16[128,128]{1,0:T(8,128)(2,1)S(1)} %get-tuple-element.71), channel_id=1, source_target_pairs={{0,16},{2,18},{4,20},{6,22},{8,24},{10,26},{12,28},{14,30},{16,0},... | collective-permute-start | bytes 98312 | tf_op jit(solution)/shard_map/ppermute | solution.py:354
  65.7 1.5 %collective-permute-start.24 = (f32[64,128]{1,0:T(8,128)S(1)}, f32[64,128]{1,0:T(8,128)S(1)}, u32[]{:S(2)}, u32[]{:S(2)}) collective-permute-start(f32[64,128]{1,0:T(8,128)S(1)} %get-tuple-element.76), channel_id=1, source_target_pairs={{0,2},{2,0},{4,6},{6,4},{8,10},{10,8},{12,14},{14,12},{16,18},{18,... | collective-permute-start | bytes 98312 | tf_op jit(solution)/shard_map/ppermute | solution.py:351

commit v3 on v2

--- a/solution.py
+++ b/solution.py
@@ -14,7 +14,7 @@
 f32 = jnp.float32
 bf16 = jnp.bfloat16
 VMEM_LIMIT = 24 * 1024 * 1024
-BINS = 64
+BINS = 128
 
 
 def dft_tables(block):
@@ -361,7 +361,8 @@
         return lax.ppermute(value, "ch", [(0, 1), (1, 0)])
 
     def trade(pieces):
-        return [pieces[0]] + [inside(pieces[d], d) for d in range(1, GROUP)]
+        moved = {d: inside(pieces[d], d) for d in (2, 3, 1)}
+        return [pieces[0]] + [moved[d] for d in range(1, GROUP)]
 
     chunks = 4
     in_hbm, in_vmem = pl.BlockSpec(memory_space=pltpu.HBM), pl.BlockSpec(memory_space=pltpu.VMEM)
@@ -428,7 +429,6 @@
         table,
         inverse,
         scratch=[pltpu.VMEM((2 * block, 2 * part), bf16), pltpu.VMEM((block, 2 * part), f32)],
-        after=[weights],
     )
 
     def convolve(which, prior, far, *more):

time: 68.6 us -> 68.5 us (level)
  no operation moved by 1% of the time
where the time goes in v3:
time: 68.5 us; the launch traced here: 67.8 us
  starting transfers between devices  32.6 us (48%)
  waiting for transfers between devices  17.7 us (26%)
  Pallas kernels  15.8 us (23%)
  between operations  0.86 us (1%)
  local copies, waits for them, and re-layouts  0.79 us (1%)
    pallas_call x16, Pallas kernels, call(): pl.pallas_call(run, out_shape=[jax.ShapeDtypeStruct(s, t) for s, t in out...  15.8 us
    ppermute x10, starting transfers between devices, inside(): return lax.ppermute(value, 'ctx', [(i, i ^ d) for i in range(n)])  9.39 us
    ppermute x5, starting transfers between devices, across(): return lax.ppermute(value, 'ctx', [(i, i ^ d * GROUP) for i in range(n)])  8.24 us
    ppermute x10, waiting for transfers between devices, inside(): return lax.ppermute(value, 'ctx', [(i, i ^ d) for i in range(n)])  7.91 us
    ppermute x4, starting transfers between devices, beside(): lax.ppermute(value, 'ctx', [(i, s * GROUP + i % GROUP) for i, s in sides...  6.46 us
    ppermute x4, starting transfers between devices, to_users(): return lax.ppermute(value, ('ctx', 'ch'), pairs)  5.08 us
    ppermute x1, waiting for transfers between devices, swap(): return lax.ppermute(value, 'ch', [(0, 1), (1, 0)])  3.87 us
    ppermute x1, starting transfers between devices, local(): total = lax.ppermute(total, ('ctx', 'ch'), turned)  3.11 us
  transfers between devices with their start and end apart: 25, of which 10 were waited for; matrix products, arithmetic and copies ran while one was open for 0% of the time, Pallas kernels for 19%

profile of v3, /device:TPU:3, one launch (start us, length us, event | category | flops | bytes accessed | tf_op | source)
XLA Modules:
  0.0 67.8 jit_solution(2438956986485033379)
XLA Ops:
  0.6 0.0 copy-start
  0.6 0.0 copy-start.5
  0.7 1.9 %shard_map.111 = (bf16[256,512]{1,0:T(8,128)(2,1)S(1)}, bf16[256,512]{1,0:T(8,128)(2,1)S(1)}, bf16[256,512]{1,0:T(8,128)(2,1)S(1)}, bf16[256,512]{1,0:T(8,128)(2,1)S(1)}) custom-call(bf16[128,2048]{1,0:T(8,128)(2,1)} %refs_6_.3, bf16[128,2048]{1,0:T(8,128)(2,1)} %refs_5_.7, bf16[128,2048]{1,0:T(8,128)(2,1)} %refs_4_.7, bf16[128,2048]{1,0:T(8,128)(2,1)} %refs_3_.1), custom_call_target="tpu_custom_call" | custom-call | tf_op jit(solution)/shard_map/pallas_call | solution.py:43
  2.6 0.7 %collective-permute-start = (bf16[256,512]{1,0:T(8,128)(2,1)S(1)}, bf16[256,512]{1,0:T(8,128)(2,1)S(1)}, u32[]{:S(2)}, u32[]{:S(2)}) collective-permute-start(bf16[256,512]{1,0:T(8,128)(2,1)S(1)} %get-tuple-element.42), channel_id=1, source_target_pairs={{0,2},{2,0},{4,6},{6,4},{8,10},{10,8},{12,14},{14,12},{16,18},{18,... | collective-permute-start | bytes 786440 | tf_op jit(solution)/shard_map/ppermute | solution.py:351
  3.4 1.3 %collective-permute-start.1 = (bf16[256,512]{1,0:T(8,128)(2,1)S(1)}, bf16[256,512]{1,0:T(8,128)(2,1)S(1)}, u32[]{:S(2)}, u32[]{:S(2)}) collective-permute-start(bf16[256,512]{1,0:T(8,128)(2,1)S(1)} %get-tuple-element.43), channel_id=1, source_target_pairs={{0,4},{2,6},{4,0},{6,2},{8,12},{10,14},{12,8},{14,10},{16,20},{18,... | collective-permute-start | bytes 786440 | tf_op jit(solution)/shard_map/ppermute | solution.py:351
  4.6 0.5 collective-permute-start.2
  5.1 0.0 collective-permute-done.refs_1_
  5.1 0.8 %copy-done.6 = bf16[64,256]{1,0:T(8,128)(2,1)S(1)} copy-done((bf16[64,256]{1,0:T(8,128)(2,1)S(1)}, bf16[64,256]{1,0:T(8,128)(2,1)}, u32[]{:S(2)}) %copy-start.6) | copy-done | bytes 32792
  5.8 1.3 %collective-permute-start.3 = (bf16[64,256]{1,0:T(8,128)(2,1)S(1)}, bf16[64,256]{1,0:T(8,128)(2,1)S(1)}, u32[]{:S(2)}, u32[]{:S(2)}) collective-permute-start(bf16[64,256]{1,0:T(8,128)(2,1)S(1)} %shard_map.112.refs_4_), channel_id=1, source_target_pairs={{0,8},{2,10},{4,12},{6,14},{8,0},{10,2},{12,4},{14,6},{16,24},{18,... | collective-permute-start | bytes 98312 | tf_op jit(solution)/shard_map/ppermute | solution.py:354
  7.1 2.3 %collective-permute-start.4 = (bf16[64,256]{1,0:T(8,128)(2,1)S(1)}, bf16[64,256]{1,0:T(8,128)(2,1)S(1)}, u32[]{:S(2)}, u32[]{:S(2)}) collective-permute-start(bf16[64,256]{1,0:T(8,128)(2,1)S(1)} %shard_map.112.refs_4_), channel_id=1, source_target_pairs={{0,16},{2,18},{4,20},{6,22},{8,24},{10,26},{12,28},{14,30},{16,0},... | collective-permute-start | bytes 98312 | tf_op jit(solution)/shard_map/ppermute | solution.py:354
  9.4 1.8 %collective-permute-done.1.refs_2_ = bf16[256,512]{1,0:T(8,128)(2,1)S(1)} collective-permute-done((bf16[256,512]{1,0:T(8,128)(2,1)S(1)}, bf16[256,512]{1,0:T(8,128)(2,1)S(1)}, u32[]{:S(2)}, u32[]{:S(2)}) %collective-permute-start.1) | collective-permute-done | bytes 262176 | tf_op jit(solution)/shard_map/ppermute | solution.py:351
  11.2 5.8 %collective-permute-done.2.refs_3_ = bf16[256,512]{1,0:T(8,128)(2,1)S(1)} collective-permute-done((bf16[256,512]{1,0:T(8,128)(2,1)S(1)}, bf16[256,512]{1,0:T(8,128)(2,1)S(1)}, u32[]{:S(2)}, u32[]{:S(2)}) %collective-permute-start.2) | collective-permute-done | bytes 262176 | tf_op jit(solution)/shard_map/ppermute | solution.py:351
  17.0 0.1 shard_map.113
  17.2 0.7 %collective-permute-start.6 = (bf16[512,512]{1,0:T(8,128)(2,1)S(1)}, bf16[512,512]{1,0:T(8,128)(2,1)S(1)}, u32[]{:S(2)}, u32[]{:S(2)}) collective-permute-start(bf16[512,512]{1,0:T(8,128)(2,1)S(1)} %get-tuple-element.45.refs_1_), channel_id=1, source_target_pairs={{8,16},{10,18},{12,20},{14,22},{16,8},{18,10},{20,12},{22,14},{9,1... | collective-permute-start | bytes 1572872 | tf_op jit(solution)/shard_map/ppermute | solution.py:358
  17.9 3.9 %collective-permute-start.7 = (bf16[512,512]{1,0:T(8,128)(2,1)S(1)}, bf16[512,512]{1,0:T(8,128)(2,1)S(1)}, u32[]{:S(2)}, u32[]{:S(2)}) collective-permute-start(bf16[512,512]{1,0:T(8,128)(2,1)S(1)} %get-tuple-element.46.refs_0_), channel_id=1, source_target_pairs={{0,8},{2,10},{4,12},{6,14},{8,0},{10,2},{12,4},{14,6},{16,24},{18,... | collective-permute-start | bytes 1572872 | tf_op jit(solution)/shard_map/ppermute | solution.py:358
  21.7 1.9 %collective-permute-start.10 = (bf16[256,128]{1,0:T(8,128)(2,1)S(1)}, bf16[256,128]{1,0:T(8,128)(2,1)S(1)}, u32[]{:S(2)}, u32[]{:S(2)}) collective-permute-start(bf16[256,128]{1,0:T(8,128)(2,1)S(1)} %get-tuple-element.48), channel_id=1, source_target_pairs={{0,2},{1,6},{2,0},{3,4},{4,3},{5,7},{6,1},{7,5},{8,10},{9,14},{10,... | collective-permute-start | bytes 196616 | tf_op jit(solution)/shard_map/ppermute | solution.py:397
  23.6 0.0 collective-permute-start.11
  23.7 3.2 %collective-permute-start.8 = (bf16[256,128]{1,0:T(8,128)(2,1)S(1)}, bf16[256,128]{1,0:T(8,128)(2,1)S(1)}, u32[]{:S(2)}, u32[]{:S(2)}) collective-permute-start(bf16[256,128]{1,0:T(8,128)(2,1)S(1)} %get-tuple-element.47), channel_id=1, source_target_pairs={{0,0},{1,4},{2,2},{3,6},{4,1},{5,5},{6,3},{7,7},{8,8},{9,12},{10,1... | collective-permute-start | bytes 196616 | tf_op jit(solution)/shard_map/ppermute | solution.py:397
  26.8 0.4 collective-permute-done.10.refs_2_
  27.2 1.6 %shard_map.114 = (f32[2,1024,512]{2,1,0:T(8,128)S(1)}, f32[1024,128]{1,0:T(8,128)S(1)}) custom-call(bf16[512,512]{1,0:T(8,128)(2,1)S(1)} %get-tuple-element.46.refs_0_, bf16[512,512]{1,0:T(8,128)(2,1)S(1)} %get-tuple-element.45.refs_1_, bf16[1024,512]{1,0:T(8,128)(2,1)S(1)} %copy-done), custom_call_target="tpu_custom_call" | custom-call | tf_op jit(solution)/shard_map/pallas_call | solution.py:43
  28.8 0.8 %collective-permute-done.8.refs_0_ = bf16[256,128]{1,0:T(8,128)(2,1)S(1)} collective-permute-done((bf16[256,128]{1,0:T(8,128)(2,1)S(1)}, bf16[256,128]{1,0:T(8,128)(2,1)S(1)}, u32[]{:S(2)}, u32[]{:S(2)}) %collective-permute-start.8) | collective-permute-done | bytes 65568 | tf_op jit(solution)/shard_map/ppermute | solution.py:397
  29.7 0.9 %collective-permute-done.9.refs_1_ = bf16[256,128]{1,0:T(8,128)(2,1)S(1)} collective-permute-done((bf16[256,128]{1,0:T(8,128)(2,1)S(1)}, bf16[256,128]{1,0:T(8,128)(2,1)S(1)}, u32[]{:S(2)}, u32[]{:S(2)}) %collective-permute-start.9) | collective-permute-done | bytes 65568 | tf_op jit(solution)/shard_map/ppermute | solution.py:397
  30.6 1.3 %shard_map.115.refs_2_.refs_3_ = f32[3,1024,128]{2,1,0:T(8,128)S(1)} custom-call(bf16[256,128]{1,0:T(8,128)(2,1)S(1)} %collective-permute-done.8.refs_0_, bf16[256,128]{1,0:T(8,128)(2,1)S(1)} %collective-permute-done.9.refs_1_, bf16[256,128]{1,0:T(8,128)(2,1)S(1)} %collective-permute-done.10.refs_2_, bf16[256,128]{1,0:T(8,128)(2,1)S(1)} %collective-permute-done.11.refs_3_, ...), custom_call_target="tpu_custom_call" | custom-call | tf_op jit(solution)/shard_map/pallas_call | solution.py:43
  31.9 1.6 %collective-permute-done.7.refs_1_.refs_0_ = bf16[512,512]{1,0:T(8,128)(2,1)S(1)} collective-permute-done((bf16[512,512]{1,0:T(8,128)(2,1)S(1)}, bf16[512,512]{1,0:T(8,128)(2,1)S(1)}, u32[]{:S(2)}, u32[]{:S(2)}) %collective-permute-start.7) | collective-permute-done | bytes 524320 | tf_op jit(solution)/shard_map/ppermute | solution.py:358
  33.6 0.1 shard_map.116
  33.6 1.2 %collective-permute-start.13 = (bf16[512,512]{1,0:T(8,128)(2,1)S(1)}, bf16[512,512]{1,0:T(8,128)(2,1)S(1)}, u32[]{:S(2)}, u32[]{:S(2)}) collective-permute-start(bf16[512,512]{1,0:T(8,128)(2,1)S(1)} %get-tuple-element.53), channel_id=1, source_target_pairs={{0,8},{2,10},{4,12},{6,14},{8,0},{10,2},{12,4},{14,6},{16,24},{18,... | collective-permute-start | bytes 1572872 | tf_op jit(solution)/shard_map/ppermute | solution.py:358
  34.8 0.7 %collective-permute-start.12 = (bf16[512,512]{1,0:T(8,128)(2,1)S(1)}, bf16[512,512]{1,0:T(8,128)(2,1)S(1)}, u32[]{:S(2)}, u32[]{:S(2)}) collective-permute-start(bf16[512,512]{1,0:T(8,128)(2,1)S(1)} %get-tuple-element.50), channel_id=1, source_target_pairs={{8,16},{10,18},{12,20},{14,22},{16,8},{18,10},{20,12},{22,14},{9,1... | collective-permute-start | bytes 1572872 | tf_op jit(solution)/shard_map/ppermute | solution.py:358
  35.5 3.0 %shard_map.117 = (f32[2,1024,512]{2,1,0:T(8,128)S(1)}, f32[512,128]{1,0:T(8,128)S(1)}, bf16[512,128]{1,0:T(8,128)(2,1)S(1)}) custom-call(bf16[512,512]{1,0:T(8,128)(2,1)S(1)} %collective-permute-done.7.refs_1_.refs_0_, bf16[512,512]{1,0:T(8,128)(2,1)S(1)} %collective-permute-done.6.refs_0_.refs_1_, f32[2,1024,512]{2,1,0:T(8,128)S(1)} %get-tuple-element.51.refs_2_, ...), custom_call_target="tpu_custom_call" | custom-call | tf_op jit(solution)/shard_map/pallas_call | solution.py:43
  38.5 0.3 collective-permute-start.14
  38.8 3.9 %collective-permute-done.14.refs_1_ = bf16[512,128]{1,0:T(8,128)(2,1)S(1)} collective-permute-done((bf16[512,128]{1,0:T(8,128)(2,1)S(1)}, bf16[512,128]{1,0:T(8,128)(2,1)S(1)}, u32[]{:S(2)}, u32[]{:S(2)}) %collective-permute-start.14) | collective-permute-done | bytes 131104 | tf_op jit(solution)/shard_map/ppermute | solution.py:361
  42.7 3.1 %collective-permute-start.21 = (bf16[512,128]{1,0:T(8,128)(2,1)S(1)}, bf16[512,128]{1,0:T(8,128)(2,1)S(1)}, u32[]{:S(2)}, u32[]{:S(2)}) collective-permute-start(bf16[512,128]{1,0:T(8,128)(2,1)S(1)} %shard_map.118.refs_6_), channel_id=1, source_target_pairs={{0,0},{1,4},{2,2},{3,6},{4,1},{5,5},{6,3},{7,7},{8,8},{9,12},{10,1... | collective-permute-start | bytes 393224 | tf_op jit(solution)/shard_map/ppermute | solution.py:477
  45.8 0.2 collective-permute-done.13.refs_0_
  46.1 2.4 %shard_map.119 = (bf16[128,512]{1,0:T(8,128)(2,1)S(1)}, bf16[128,512]{1,0:T(8,128)(2,1)S(1)}, bf16[128,512]{1,0:T(8,128)(2,1)S(1)}, bf16[128,512]{1,0:T(8,128)(2,1)S(1)}) custom-call(bf16[512,512]{1,0:T(8,128)(2,1)S(1)} %collective-permute-done.13.refs_0_, f32[2,1024,512]{2,1,0:T(8,128)S(1)} %get-tuple-element.52.refs_1_, ...), custom_call_target="tpu_custom_call" | custom-call | tf_op jit(solution)/shard_map/pallas_call | solution.py:43
  48.4 2.6 %collective-permute-start.18 = (bf16[128,512]{1,0:T(8,128)(2,1)S(1)}, bf16[128,512]{1,0:T(8,128)(2,1)S(1)}, u32[]{:S(2)}, u32[]{:S(2)}) collective-permute-start(bf16[128,512]{1,0:T(8,128)(2,1)S(1)} %get-tuple-element.61), channel_id=1, source_target_pairs={{0,2},{2,0},{4,6},{6,4},{8,10},{10,8},{12,14},{14,12},{16,18},{18,... | collective-permute-start | bytes 393224 | tf_op jit(solution)/shard_map/ppermute | solution.py:351
  51.1 0.7 collective-permute-start.19
  51.7 1.1 %collective-permute-start.20 = (bf16[128,512]{1,0:T(8,128)(2,1)S(1)}, bf16[128,512]{1,0:T(8,128)(2,1)S(1)}, u32[]{:S(2)}, u32[]{:S(2)}) collective-permute-start(bf16[128,512]{1,0:T(8,128)(2,1)S(1)} %get-tuple-element.63), channel_id=1, source_target_pairs={{0,6},{2,4},{4,2},{6,0},{8,14},{10,12},{12,10},{14,8},{16,22},{18,... | collective-permute-start | bytes 393224 | tf_op jit(solution)/shard_map/ppermute | solution.py:351
  52.8 2.4 %shard_map.120 = (bf16[128,512]{1,0:T(8,128)(2,1)S(1)}, bf16[128,512]{1,0:T(8,128)(2,1)S(1)}, bf16[128,512]{1,0:T(8,128)(2,1)S(1)}, bf16[128,512]{1,0:T(8,128)(2,1)S(1)}) custom-call(bf16[512,512]{1,0:T(8,128)(2,1)S(1)} %collective-permute-done.12.refs_0_, f32[2,1024,512]{2,1,0:T(8,128)S(1)} %get-tuple-element.52.refs_1_, ...), custom_call_target="tpu_custom_call" | custom-call | tf_op jit(solution)/shard_map/pallas_call | solution.py:43
  55.2 1.7 %collective-permute-start.22 = (bf16[256,128]{1,0:T(8,128)(2,1)S(1)}, bf16[256,128]{1,0:T(8,128)(2,1)S(1)}, u32[]{:S(2)}, u32[]{:S(2)}) collective-permute-start(bf16[256,128]{1,0:T(8,128)(2,1)S(1)} %get-tuple-element.68), channel_id=1, source_target_pairs={{0,8},{2,10},{4,12},{6,14},{8,0},{10,2},{12,4},{14,6},{16,24},{18,... | collective-permute-start | bytes 196616 | tf_op jit(solution)/shard_map/ppermute | solution.py:354
  56.9 0.4 collective-permute-start.15
  57.4 0.1 collective-permute-start.16
  57.5 1.6 %collective-permute-start.17 = (bf16[128,512]{1,0:T(8,128)(2,1)S(1)}, bf16[128,512]{1,0:T(8,128)(2,1)S(1)}, u32[]{:S(2)}, u32[]{:S(2)}) collective-permute-start(bf16[128,512]{1,0:T(8,128)(2,1)S(1)} %get-tuple-element.60), channel_id=1, source_target_pairs={{0,6},{2,4},{4,2},{6,0},{8,14},{10,12},{12,10},{14,8},{16,22},{18,... | collective-permute-start | bytes 393224 | tf_op jit(solution)/shard_map/ppermute | solution.py:351
  59.1 0.3 collective-permute-done.20.refs_3_
  59.4 1.3 %shard_map.122 = (bf16[128,2048]{1,0:T(8,128)(2,1)}, bf16[128,2048]{1,0:T(8,128)(2,1)}, bf16[128,2048]{1,0:T(8,128)(2,1)}, f32[8,128]{1,0:T(8,128)S(1)}) custom-call(bf16[128,512]{1,0:T(8,128)(2,1)S(1)} %get-tuple-element.56.refs_6_.refs_0_, bf16[128,512]{1,0:T(8,128)(2,1)S(1)} %collective-permute-done.18.refs_1_, ...), custom_call_target="tpu_custom_call" | custom-call | tf_op jit(solution)/shard_map/pallas_call | solution.py:43
  60.8 2.9 %collective-permute-start.23 = (bf16[128,128]{1,0:T(8,128)(2,1)S(1)}, bf16[128,128]{1,0:T(8,128)(2,1)S(1)}, u32[]{:S(2)}, u32[]{:S(2)}) collective-permute-start(bf16[128,128]{1,0:T(8,128)(2,1)S(1)} %get-tuple-element.71), channel_id=1, source_target_pairs={{0,16},{2,18},{4,20},{6,22},{8,24},{10,26},{12,28},{14,30},{16,0},... | collective-permute-start | bytes 98312 | tf_op jit(solution)/shard_map/ppermute | solution.py:354
  63.7 1.9 %collective-permute-done.23.refs_1_ = bf16[128,128]{1,0:T(8,128)(2,1)S(1)} collective-permute-done((bf16[128,128]{1,0:T(8,128)(2,1)S(1)}, bf16[128,128]{1,0:T(8,128)(2,1)S(1)}, u32[]{:S(2)}, u32[]{:S(2)}) %collective-permute-start.23) | collective-permute-done | bytes 32800 | tf_op jit(solution)/shard_map/ppermute | solution.py:354
  65.6 0.5 collective-permute-start.24
  66.1 1.1 %shard_map.125 = (bf16[128,2048]{1,0:T(8,128)(2,1)}, bf16[128,2048]{1,0:T(8,128)(2,1)}, bf16[128,2048]{1,0:T(8,128)(2,1)}, f32[8,128]{1,0:T(8,128)S(1)}) custom-call(bf16[128,512]{1,0:T(8,128)(2,1)S(1)} %get-tuple-element.57.refs_1_.refs_0_, ...), custom_call_target="tpu_custom_call", output_to_operand_aliasing={{0}: (7, {}), {1}: (8, {}), {2}: (9, {})} | custom-call | tf_op jit(solution)/shard_map/pallas_call | solution.py:43
  67.1 0.6 shard_map.126
  (32 shorter events, 0.2 us)
Async XLA Ops:
  0.6 26.6 %copy-start = (bf16[1024,512]{1,0:T(8,128)(2,1)S(1)}, bf16[1024,512]{1,0:T(8,128)(2,1)}, u32[]{:S(2)}) copy-start(bf16[1024,512]{1,0:T(8,128)(2,1)} %constant.6.clone.refs_2_.refs_4_) | copy-start | bytes 3145732
  0.6 30.0 %copy-start.5 = (bf16[1024,512]{1,0:T(8,128)(2,1)S(1)}, bf16[1024,512]{1,0:T(8,128)(2,1)}, u32[]{:S(2)}) copy-start(bf16[1024,512]{1,0:T(8,128)(2,1)} %constant.7.clone.refs_5_) | copy-start | bytes 3145732
  2.6 2.5 %collective-permute-start = (bf16[256,512]{1,0:T(8,128)(2,1)S(1)}, bf16[256,512]{1,0:T(8,128)(2,1)S(1)}, u32[]{:S(2)}, u32[]{:S(2)}) collective-permute-start(bf16[256,512]{1,0:T(8,128)(2,1)S(1)} %get-tuple-element.42), channel_id=1, source_target_pairs={{0,2},{2,0},{4,6},{6,4},{8,10},{10,8},{12,14},{14,12},{16,18},{18,... | collective-permute-start | bytes 786440 | tf_op jit(solution)/shard_map/ppermute | solution.py:351
  3.4 7.9 %collective-permute-start.1 = (bf16[256,512]{1,0:T(8,128)(2,1)S(1)}, bf16[256,512]{1,0:T(8,128)(2,1)S(1)}, u32[]{:S(2)}, u32[]{:S(2)}) collective-permute-start(bf16[256,512]{1,0:T(8,128)(2,1)S(1)} %get-tuple-element.43), channel_id=1, source_target_pairs={{0,4},{2,6},{4,0},{6,2},{8,12},{10,14},{12,8},{14,10},{16,20},{18,... | collective-permute-start | bytes 786440 | tf_op jit(solution)/shard_map/ppermute | solution.py:351
  4.6 12.4 %collective-permute-start.2 = (bf16[256,512]{1,0:T(8,128)(2,1)S(1)}, bf16[256,512]{1,0:T(8,128)(2,1)S(1)}, u32[]{:S(2)}, u32[]{:S(2)}) collective-permute-start(bf16[256,512]{1,0:T(8,128)(2,1)S(1)} %get-tuple-element.44), channel_id=1, source_target_pairs={{0,6},{2,4},{4,2},{6,0},{8,14},{10,12},{12,10},{14,8},{16,22},{18,... | collective-permute-start | bytes 786440 | tf_op jit(solution)/shard_map/ppermute | solution.py:351
  5.1 0.8 %copy-start.6 = (bf16[64,256]{1,0:T(8,128)(2,1)S(1)}, bf16[64,256]{1,0:T(8,128)(2,1)}, u32[]{:S(2)}) copy-start(bf16[64,256]{1,0:T(8,128)(2,1)} %refs_0_.3) | copy-start | bytes 98308
  5.8 11.2 %collective-permute-start.3 = (bf16[64,256]{1,0:T(8,128)(2,1)S(1)}, bf16[64,256]{1,0:T(8,128)(2,1)S(1)}, u32[]{:S(2)}, u32[]{:S(2)}) collective-permute-start(bf16[64,256]{1,0:T(8,128)(2,1)S(1)} %shard_map.112.refs_4_), channel_id=1, source_target_pairs={{0,8},{2,10},{4,12},{6,14},{8,0},{10,2},{12,4},{14,6},{16,24},{18,... | collective-permute-start | bytes 98312 | tf_op jit(solution)/shard_map/ppermute | solution.py:354
  7.1 9.9 %collective-permute-start.4 = (bf16[64,256]{1,0:T(8,128)(2,1)S(1)}, bf16[64,256]{1,0:T(8,128)(2,1)S(1)}, u32[]{:S(2)}, u32[]{:S(2)}) collective-permute-start(bf16[64,256]{1,0:T(8,128)(2,1)S(1)} %shard_map.112.refs_4_), channel_id=1, source_target_pairs={{0,16},{2,18},{4,20},{6,22},{8,24},{10,26},{12,28},{14,30},{16,0},... | collective-permute-start | bytes 98312 | tf_op jit(solution)/shard_map/ppermute | solution.py:354
  9.4 7.6 %collective-permute-start.5 = (bf16[64,256]{1,0:T(8,128)(2,1)S(1)}, bf16[64,256]{1,0:T(8,128)(2,1)S(1)}, u32[]{:S(2)}, u32[]{:S(2)}) collective-permute-start(bf16[64,256]{1,0:T(8,128)(2,1)S(1)} %shard_map.112.refs_4_), channel_id=1, source_target_pairs={{0,24},{2,26},{4,28},{6,30},{8,16},{10,18},{12,20},{14,22},{16,8},... | collective-permute-start | bytes 98312 | tf_op jit(solution)/shard_map/ppermute | solution.py:354
  17.2 14.8 %collective-permute-start.6 = (bf16[512,512]{1,0:T(8,128)(2,1)S(1)}, bf16[512,512]{1,0:T(8,128)(2,1)S(1)}, u32[]{:S(2)}, u32[]{:S(2)}) collective-permute-start(bf16[512,512]{1,0:T(8,128)(2,1)S(1)} %get-tuple-element.45.refs_1_), channel_id=1, source_target_pairs={{8,16},{10,18},{12,20},{14,22},{16,8},{18,10},{20,12},{22,14},{9,1... | collective-permute-start | bytes 1572872 | tf_op jit(solution)/shard_map/ppermute | solution.py:358
  17.9 15.7 %collective-permute-start.7 = (bf16[512,512]{1,0:T(8,128)(2,1)S(1)}, bf16[512,512]{1,0:T(8,128)(2,1)S(1)}, u32[]{:S(2)}, u32[]{:S(2)}) collective-permute-start(bf16[512,512]{1,0:T(8,128)(2,1)S(1)} %get-tuple-element.46.refs_0_), channel_id=1, source_target_pairs={{0,8},{2,10},{4,12},{6,14},{8,0},{10,2},{12,4},{14,6},{16,24},{18,... | collective-permute-start | bytes 1572872 | tf_op jit(solution)/shard_map/ppermute | solution.py:358
  21.7 5.5 %collective-permute-start.10 = (bf16[256,128]{1,0:T(8,128)(2,1)S(1)}, bf16[256,128]{1,0:T(8,128)(2,1)S(1)}, u32[]{:S(2)}, u32[]{:S(2)}) collective-permute-start(bf16[256,128]{1,0:T(8,128)(2,1)S(1)} %get-tuple-element.48), channel_id=1, source_target_pairs={{0,2},{1,6},{2,0},{3,4},{4,3},{5,7},{6,1},{7,5},{8,10},{9,14},{10,... | collective-permute-start | bytes 196616 | tf_op jit(solution)/shard_map/ppermute | solution.py:397
  23.6 5.2 %collective-permute-start.11 = (bf16[256,128]{1,0:T(8,128)(2,1)S(1)}, bf16[256,128]{1,0:T(8,128)(2,1)S(1)}, u32[]{:S(2)}, u32[]{:S(2)}) collective-permute-start(bf16[256,128]{1,0:T(8,128)(2,1)S(1)} %get-tuple-element.48), channel_id=1, source_target_pairs={{0,3},{1,7},{2,1},{3,5},{4,2},{5,6},{6,0},{7,4},{8,11},{9,15},{10,... | collective-permute-start | bytes 196616 | tf_op jit(solution)/shard_map/ppermute | solution.py:397
  23.7 11.9 %copy-start.1 = (bf16[512,1024]{1,0:T(8,128)(2,1)S(1)}, bf16[512,1024]{1,0:T(8,128)(2,1)}, u32[]{:S(2)}) copy-start(bf16[512,1024]{1,0:T(8,128)(2,1)} %constant.8.clone.refs_5_) | copy-start | bytes 3145732
  23.7 6.0 %collective-permute-start.8 = (bf16[256,128]{1,0:T(8,128)(2,1)S(1)}, bf16[256,128]{1,0:T(8,128)(2,1)S(1)}, u32[]{:S(2)}, u32[]{:S(2)}) collective-permute-start(bf16[256,128]{1,0:T(8,128)(2,1)S(1)} %get-tuple-element.47), channel_id=1, source_target_pairs={{0,0},{1,4},{2,2},{3,6},{4,1},{5,5},{6,3},{7,7},{8,8},{9,12},{10,1... | collective-permute-start | bytes 196616 | tf_op jit(solution)/shard_map/ppermute | solution.py:397
  27.2 3.4 %collective-permute-start.9 = (bf16[256,128]{1,0:T(8,128)(2,1)S(1)}, bf16[256,128]{1,0:T(8,128)(2,1)S(1)}, u32[]{:S(2)}, u32[]{:S(2)}) collective-permute-start(bf16[256,128]{1,0:T(8,128)(2,1)S(1)} %get-tuple-element.47), channel_id=1, source_target_pairs={{0,1},{1,5},{2,3},{3,7},{4,0},{5,4},{6,2},{7,6},{8,9},{9,13},{10,1... | collective-permute-start | bytes 196616 | tf_op jit(solution)/shard_map/ppermute | solution.py:397
  33.6 12.4 %collective-permute-start.13 = (bf16[512,512]{1,0:T(8,128)(2,1)S(1)}, bf16[512,512]{1,0:T(8,128)(2,1)S(1)}, u32[]{:S(2)}, u32[]{:S(2)}) collective-permute-start(bf16[512,512]{1,0:T(8,128)(2,1)S(1)} %get-tuple-element.53), channel_id=1, source_target_pairs={{0,8},{2,10},{4,12},{6,14},{8,0},{10,2},{12,4},{14,6},{16,24},{18,... | collective-permute-start | bytes 1572872 | tf_op jit(solution)/shard_map/ppermute | solution.py:358
  34.8 17.9 %collective-permute-start.12 = (bf16[512,512]{1,0:T(8,128)(2,1)S(1)}, bf16[512,512]{1,0:T(8,128)(2,1)S(1)}, u32[]{:S(2)}, u32[]{:S(2)}) collective-permute-start(bf16[512,512]{1,0:T(8,128)(2,1)S(1)} %get-tuple-element.50), channel_id=1, source_target_pairs={{8,16},{10,18},{12,20},{14,22},{16,8},{18,10},{20,12},{22,14},{9,1... | collective-permute-start | bytes 1572872 | tf_op jit(solution)/shard_map/ppermute | solution.py:358
  38.5 4.2 %collective-permute-start.14 = (bf16[512,128]{1,0:T(8,128)(2,1)S(1)}, bf16[512,128]{1,0:T(8,128)(2,1)S(1)}, u32[]{:S(2)}, u32[]{:S(2)}) collective-permute-start(bf16[512,128]{1,0:T(8,128)(2,1)S(1)} %get-tuple-element.55), channel_id=1, source_target_pairs={{0,1},{1,0},{2,3},{3,2},{4,5},{5,4},{6,7},{7,6},{8,9},{9,8},{10,11... | collective-permute-start | bytes 393224 | tf_op jit(solution)/shard_map/ppermute | solution.py:361
  42.7 12.4 %collective-permute-start.21 = (bf16[512,128]{1,0:T(8,128)(2,1)S(1)}, bf16[512,128]{1,0:T(8,128)(2,1)S(1)}, u32[]{:S(2)}, u32[]{:S(2)}) collective-permute-start(bf16[512,128]{1,0:T(8,128)(2,1)S(1)} %shard_map.118.refs_6_), channel_id=1, source_target_pairs={{0,0},{1,4},{2,2},{3,6},{4,1},{5,5},{6,3},{7,7},{8,8},{9,12},{10,1... | collective-permute-start | bytes 393224 | tf_op jit(solution)/shard_map/ppermute | solution.py:477
  48.4 9.0 %collective-permute-start.18 = (bf16[128,512]{1,0:T(8,128)(2,1)S(1)}, bf16[128,512]{1,0:T(8,128)(2,1)S(1)}, u32[]{:S(2)}, u32[]{:S(2)}) collective-permute-start(bf16[128,512]{1,0:T(8,128)(2,1)S(1)} %get-tuple-element.61), channel_id=1, source_target_pairs={{0,2},{2,0},{4,6},{6,4},{8,10},{10,8},{12,14},{14,12},{16,18},{18,... | collective-permute-start | bytes 393224 | tf_op jit(solution)/shard_map/ppermute | solution.py:351
  51.1 6.5 %collective-permute-start.19 = (bf16[128,512]{1,0:T(8,128)(2,1)S(1)}, bf16[128,512]{1,0:T(8,128)(2,1)S(1)}, u32[]{:S(2)}, u32[]{:S(2)}) collective-permute-start(bf16[128,512]{1,0:T(8,128)(2,1)S(1)} %get-tuple-element.62), channel_id=1, source_target_pairs={{0,4},{2,6},{4,0},{6,2},{8,12},{10,14},{12,8},{14,10},{16,20},{18,... | collective-permute-start | bytes 393224 | tf_op jit(solution)/shard_map/ppermute | solution.py:351
  51.7 7.7 %collective-permute-start.20 = (bf16[128,512]{1,0:T(8,128)(2,1)S(1)}, bf16[128,512]{1,0:T(8,128)(2,1)S(1)}, u32[]{:S(2)}, u32[]{:S(2)}) collective-permute-start(bf16[128,512]{1,0:T(8,128)(2,1)S(1)} %get-tuple-element.63), channel_id=1, source_target_pairs={{0,6},{2,4},{4,2},{6,0},{8,14},{10,12},{12,10},{14,8},{16,22},{18,... | collective-permute-start | bytes 393224 | tf_op jit(solution)/shard_map/ppermute | solution.py:351
  52.8 6.6 %copy-start.2 = (bf16[128,2048]{1,0:T(8,128)(2,1)S(1)}, bf16[128,2048]{1,0:T(8,128)(2,1)}, u32[]{:S(2)}) copy-start(bf16[128,2048]{1,0:T(8,128)(2,1)} %refs_6_.3) | copy-start | bytes 1572868
  52.8 6.6 %copy-start.3 = (bf16[128,2048]{1,0:T(8,128)(2,1)S(1)}, bf16[128,2048]{1,0:T(8,128)(2,1)}, u32[]{:S(2)}) copy-start(bf16[128,2048]{1,0:T(8,128)(2,1)} %refs_5_.7) | copy-start | bytes 1572868
  52.8 6.6 %copy-start.4 = (bf16[128,2048]{1,0:T(8,128)(2,1)S(1)}, bf16[128,2048]{1,0:T(8,128)(2,1)}, u32[]{:S(2)}) copy-start(bf16[128,2048]{1,0:T(8,128)(2,1)} %refs_4_.7) | copy-start | bytes 1572868
  55.2 5.5 %collective-permute-start.22 = (bf16[256,128]{1,0:T(8,128)(2,1)S(1)}, bf16[256,128]{1,0:T(8,128)(2,1)S(1)}, u32[]{:S(2)}, u32[]{:S(2)}) collective-permute-start(bf16[256,128]{1,0:T(8,128)(2,1)S(1)} %get-tuple-element.68), channel_id=1, source_target_pairs={{0,8},{2,10},{4,12},{6,14},{8,0},{10,2},{12,4},{14,6},{16,24},{18,... | collective-permute-start | bytes 196616 | tf_op jit(solution)/shard_map/ppermute | solution.py:354
  56.9 9.1 %collective-permute-start.15 = (bf16[128,512]{1,0:T(8,128)(2,1)S(1)}, bf16[128,512]{1,0:T(8,128)(2,1)S(1)}, u32[]{:S(2)}, u32[]{:S(2)}) collective-permute-start(bf16[128,512]{1,0:T(8,128)(2,1)S(1)} %get-tuple-element.58), channel_id=1, source_target_pairs={{0,2},{2,0},{4,6},{6,4},{8,10},{10,8},{12,14},{14,12},{16,18},{18,... | collective-permute-start | bytes 393224 | tf_op jit(solution)/shard_map/ppermute | solution.py:351
  57.4 8.7 %collective-permute-start.16 = (bf16[128,512]{1,0:T(8,128)(2,1)S(1)}, bf16[128,512]{1,0:T(8,128)(2,1)S(1)}, u32[]{:S(2)}, u32[]{:S(2)}) collective-permute-start(bf16[128,512]{1,0:T(8,128)(2,1)S(1)} %get-tuple-element.59), channel_id=1, source_target_pairs={{0,4},{2,6},{4,0},{6,2},{8,12},{10,14},{12,8},{14,10},{16,20},{18,... | collective-permute-start | bytes 393224 | tf_op jit(solution)/shard_map/ppermute | solution.py:351
  57.5 8.5 %collective-permute-start.17 = (bf16[128,512]{1,0:T(8,128)(2,1)S(1)}, bf16[128,512]{1,0:T(8,128)(2,1)S(1)}, u32[]{:S(2)}, u32[]{:S(2)}) collective-permute-start(bf16[128,512]{1,0:T(8,128)(2,1)S(1)} %get-tuple-element.60), channel_id=1, source_target_pairs={{0,6},{2,4},{4,2},{6,0},{8,14},{10,12},{12,10},{14,8},{16,22},{18,... | collective-permute-start | bytes 393224 | tf_op jit(solution)/shard_map/ppermute | solution.py:351
  60.8 4.8 %collective-permute-start.23 = (bf16[128,128]{1,0:T(8,128)(2,1)S(1)}, bf16[128,128]{1,0:T(8,128)(2,1)S(1)}, u32[]{:S(2)}, u32[]{:S(2)}) collective-permute-start(bf16[128,128]{1,0:T(8,128)(2,1)S(1)} %get-tuple-element.71), channel_id=1, source_target_pairs={{0,16},{2,18},{4,20},{6,22},{8,24},{10,26},{12,28},{14,30},{16,0},... | collective-permute-start | bytes 98312 | tf_op jit(solution)/shard_map/ppermute | solution.py:354
  65.6 1.5 %collective-permute-start.24 = (f32[64,128]{1,0:T(8,128)S(1)}, f32[64,128]{1,0:T(8,128)S(1)}, u32[]{:S(2)}, u32[]{:S(2)}) collective-permute-start(f32[64,128]{1,0:T(8,128)S(1)} %get-tuple-element.76), channel_id=1, source_target_pairs={{0,2},{2,0},{4,6},{6,4},{8,10},{10,8},{12,14},{14,12},{16,18},{18,... | collective-permute-start | bytes 98312 | tf_op jit(solution)/shard_map/ppermute | solution.py:351
